TPU v7x, 32 devices: a whole 2x2x4 slice. The times are simulated.
32 devices in a mesh: dp: 8 (over z, core), tensor: 4 (over y, x).
Axes of the slice: x: 2, y: 2, z: 4, core: 2. Of those that a mesh axis runs over, the one named last changes fastest.
Arguments:
- latents: bfloat16 [8192, 1536], P(('dp', 'tensor')), may hold values from -6 to 6
- conditioning: bfloat16 [8, 130, 768], P('dp'), may hold values from -6 to 6
- gain_attn: float32 [1536], replicated, may hold values from 0.1 to 1.9
- w_qkv: float32 [1536, 4608], P('dp', 'tensor'), may hold values from -0.15625 to 0.15625
- w_attn_out: float32 [1536, 1536], P('tensor', 'dp'), may hold values from -3 to 3
- gain_cross: float32 [1536], replicated, may hold values from 0.1 to 1.9
- w_cross_q: float32 [1536, 1536], P('dp', 'tensor'), may hold values from -0.15625 to 0.15625
- w_cross_kv: float32 [768, 3072], P('dp', 'tensor'), may hold values from -0.21875 to 0.21875
- w_cross_out: float32 [1536, 1536], P('tensor', 'dp'), may hold values from -1 to 1
- gain_mlp: float32 [1536], replicated, may hold values from 0.1 to 1.9
- w_gate: float32 [1536, 6144], P('dp', 'tensor'), may hold values from -0.15625 to 0.15625
- w_up: float32 [1536, 6144], P('dp', 'tensor'), may hold values from -0.15625 to 0.15625
- w_down: float32 [6144, 1536], P('tensor', 'dp'), may hold values from -0.078125 to 0.078125
- cotangent: bfloat16 [8192, 1536], P(('dp', 'tensor')), may hold values from -6 to 6
Outputs:
- block_out: float32 [8192, 1536], P(('dp', 'tensor'))
- grad_latents: float32 [8192, 1536], P(('dp', 'tensor'))
- grad_conditioning: float32 [8, 130, 768], P('dp')
- grad_gain_attn: float32 [1536], replicated
- grad_w_qkv: float32 [1536, 4608], P('dp', 'tensor')
- grad_w_attn_out: float32 [1536, 1536], P('tensor', 'dp')
- grad_gain_cross: float32 [1536], replicated
- grad_w_cross_q: float32 [1536, 1536], P('dp', 'tensor')
- grad_w_cross_kv: float32 [768, 3072], P('dp', 'tensor')
- grad_w_cross_out: float32 [1536, 1536], P('tensor', 'dp')
- grad_gain_mlp: float32 [1536], replicated
- grad_w_gate: float32 [1536, 6144], P('dp', 'tensor')
- grad_w_up: float32 [1536, 6144], P('dp', 'tensor')
- grad_w_down: float32 [6144, 1536], P('tensor', 'dp')
All inputs are finite; a program needn't handle non-finite values.
Results may differ from a plain program's by a relative error of at most 0.025.
Values may be sent and summed in bfloat16 or wider, within the bound.
A program may use at most 192 MiB of HBM per device.

v0:
```python
from functools import reduce

import jax
import jax.numpy as jnp
from jax import lax
from jax.sharding import PartitionSpec as P

DH = 64
CTX = 130
LENGTH = 1024


norm_eps = 1e-05
rope_base = 10000.0


def dot_plain(left_op, right_op):
    return jnp.dot(left_op, right_op, preferred_element_type=jnp.float32)


def dot_rows(left_op, right_op):
    return lax.dot_general(
        left_op, right_op, (((0,), (0,)), ((), ())), preferred_element_type=jnp.float32
    )


def dot_cols(left_op, right_op):
    return lax.dot_general(
        left_op, right_op, (((1,), (1,)), ((), ())), preferred_element_type=jnp.float32
    )


def layer_norm(values, gain_vec):
    center = values - jnp.mean(values, axis=-1, keepdims=True)
    spread = jnp.mean(center * center, axis=-1, keepdims=True)
    inverse = lax.rsqrt(spread + norm_eps)
    scaled = center * inverse
    return (scaled * gain_vec, scaled, inverse)


def norm_backward(upstream, scaled, inverse, gain_vec):
    weighted = upstream * gain_vec
    inner = jnp.mean(weighted, axis=-1, keepdims=True) + scaled * jnp.mean(
        weighted * scaled, axis=-1, keepdims=True
    )
    return (inverse * (weighted - inner), jnp.sum(upstream * scaled, axis=0))


def rotary_tables(positions):
    quarter = DH // 4
    frequency = jnp.exp(-jnp.log(rope_base) * jnp.arange(quarter).astype(jnp.float32) / quarter)
    angles = positions.astype(jnp.float32)[:, None] * frequency[None, :]
    return (jnp.cos(angles)[:, None, :], jnp.sin(angles)[:, None, :])


def rotate_heads(values, cosine_table, sine_table):
    quarter = DH // 4
    first_half = values[..., :quarter]
    second_half = values[..., quarter : 2 * quarter]
    return jnp.concatenate(
        [
            first_half * cosine_table - second_half * sine_table,
            second_half * cosine_table + first_half * sine_table,
            values[..., 2 * quarter :],
        ],
        axis=-1,
    )


def spread_rows(values):
    return lax.all_gather(values, "tensor", axis=0, tiled=True)


def spread_grads(values):
    return lax.all_gather(values, "tensor", axis=0, tiled=True)


def branch_sum(left_rows, weights):
    return lax.psum_scatter(
        dot_plain(left_rows, weights), "tensor", scatter_dimension=0, tiled=True
    )


def grad_sum(operand_pairs):
    partials = [dot_cols(grad_rows, weights) for grad_rows, weights in operand_pairs]
    return lax.psum_scatter(reduce(jnp.add, partials), "tensor", scatter_dimension=0, tiled=True)


def self_forward(queries, keys_rot, values_in):
    block_rows = min(512, LENGTH)
    scaling = DH ** (-0.5)

    def one_sequence(operands):
        seq_queries, seq_keys, seq_values = operands
        blocks = seq_queries.reshape(LENGTH // block_rows, block_rows, seq_queries.shape[1], DH)

        def one_block(query_block):
            scores = (
                jnp.einsum(
                    "qhd,khd->hqk", query_block, seq_keys, preferred_element_type=jnp.float32
                )
                * scaling
            )
            peak_score = jnp.max(scores, axis=-1, keepdims=True)
            shifted = jnp.exp(scores - peak_score)
            totals = jnp.sum(shifted, axis=-1, keepdims=True)
            probabilities = (shifted / totals).astype(jnp.bfloat16)
            output = jnp.einsum(
                "hqk,khd->qhd", probabilities, seq_values, preferred_element_type=jnp.float32
            )
            return (output, (peak_score + jnp.log(totals))[..., 0])

        outputs, log_totals = lax.map(one_block, blocks)
        return (outputs.reshape(seq_queries.shape), log_totals)

    return lax.map(one_sequence, (queries, keys_rot, values_in))


def self_backward(queries, keys_rot, values_in, d_output, log_totals):
    block_rows = min(512, LENGTH)
    scaling = DH ** (-0.5)

    def one_sequence(operands):
        seq_queries, seq_keys, seq_values, seq_grads, seq_logs = operands
        blocks = seq_queries.reshape(LENGTH // block_rows, block_rows, seq_queries.shape[1], DH)
        grad_blocks = seq_grads.reshape(blocks.shape)

        def one_block(running, inputs):
            query_block, grad_block, log_block = inputs
            scores = (
                jnp.einsum(
                    "qhd,khd->hqk", query_block, seq_keys, preferred_element_type=jnp.float32
                )
                * scaling
            )
            probabilities = jnp.exp(scores - log_block[..., None])
            d_prob = jnp.einsum(
                "qhd,khd->hqk", grad_block, seq_values, preferred_element_type=jnp.float32
            )
            center = jnp.sum(probabilities * d_prob, axis=-1, keepdims=True)
            d_score = (probabilities * (d_prob - center)).astype(jnp.bfloat16)
            d_query = (
                jnp.einsum("hqk,khd->qhd", d_score, seq_keys, preferred_element_type=jnp.float32)
                * scaling
            )
            d_key = (
                running[0]
                + jnp.einsum(
                    "hqk,qhd->khd", d_score, query_block, preferred_element_type=jnp.float32
                )
                * scaling
            )
            d_value = running[1] + jnp.einsum(
                "hqk,qhd->khd",
                probabilities.astype(jnp.bfloat16),
                grad_block,
                preferred_element_type=jnp.float32,
            )
            return ((d_key, d_value), d_query)

        zeroed = jnp.zeros(seq_keys.shape, jnp.float32)
        (d_key, d_value), d_query = lax.scan(
            one_block, (zeroed, zeroed), (blocks, grad_blocks, seq_logs)
        )
        return (d_query.reshape(seq_queries.shape), d_key, d_value)

    return lax.map(one_sequence, (queries, keys_rot, values_in, d_output, log_totals))


def cross_forward(queries, keys_in, values_in):
    scores = jnp.einsum(
        "sqhd,skhd->shqk", queries, keys_in, preferred_element_type=jnp.float32
    ) * DH ** (-0.5)
    peak_score = jnp.max(scores, axis=-1, keepdims=True)
    shifted = jnp.exp(scores - peak_score)
    totals = jnp.sum(shifted, axis=-1, keepdims=True)
    probabilities = (shifted / totals).astype(jnp.bfloat16)
    output = jnp.einsum(
        "shqk,skhd->sqhd", probabilities, values_in, preferred_element_type=jnp.float32
    )
    return (output, peak_score + jnp.log(totals))


def cross_backward(queries, keys_in, values_in, d_output, log_totals):
    scaling = DH ** (-0.5)
    scores = (
        jnp.einsum("sqhd,skhd->shqk", queries, keys_in, preferred_element_type=jnp.float32)
        * scaling
    )
    probabilities = jnp.exp(scores - log_totals)
    d_prob = jnp.einsum("sqhd,skhd->shqk", d_output, values_in, preferred_element_type=jnp.float32)
    center = jnp.sum(probabilities * d_prob, axis=-1, keepdims=True)
    d_score = (probabilities * (d_prob - center)).astype(jnp.bfloat16)
    d_query = (
        jnp.einsum("shqk,skhd->sqhd", d_score, keys_in, preferred_element_type=jnp.float32)
        * scaling
    )
    d_key = (
        jnp.einsum("shqk,sqhd->skhd", d_score, queries, preferred_element_type=jnp.float32)
        * scaling
    )
    d_value = jnp.einsum(
        "shqk,sqhd->skhd",
        probabilities.astype(jnp.bfloat16),
        d_output,
        preferred_element_type=jnp.float32,
    )
    return (d_query, d_key, d_value)


def per_device(
    latents,
    conditioning,
    gain_attn,
    w_qkv,
    w_attn_out,
    gain_cross,
    w_cross_q,
    w_cross_kv,
    w_cross_out,
    gain_mlp,
    w_gate,
    w_up,
    w_down,
    cotangent,
):
    gathered = (
        lax.all_gather(w_qkv.astype(jnp.bfloat16), "dp", axis=0, tiled=True),
        lax.all_gather(w_attn_out.astype(jnp.bfloat16), "dp", axis=1, tiled=True),
        lax.all_gather(w_cross_q.astype(jnp.bfloat16), "dp", axis=0, tiled=True),
        lax.all_gather(w_cross_kv.astype(jnp.bfloat16), "dp", axis=0, tiled=True),
        lax.all_gather(w_cross_out.astype(jnp.bfloat16), "dp", axis=1, tiled=True),
        lax.all_gather(w_gate.astype(jnp.bfloat16), "dp", axis=0, tiled=True),
        lax.all_gather(w_up.astype(jnp.bfloat16), "dp", axis=0, tiled=True),
        lax.all_gather(w_down.astype(jnp.bfloat16), "dp", axis=1, tiled=True),
    )
    qkv_fwd, attn_out_fwd, cross_q_fwd, cross_kv_fwd, cross_out_fwd, gate_fwd, up_fwd, down_fwd = (
        gathered
    )
    resid_in = latents.astype(jnp.float32)
    normed_one, scaled_one, inverse_one = layer_norm(resid_in, gain_attn)
    rows_one = spread_rows(normed_one.astype(jnp.bfloat16))
    group_rows = rows_one.shape[0]
    seq_count = conditioning.shape[0]
    cosine_table, sine_table = rotary_tables(jnp.arange(group_rows) % LENGTH)
    packed = dot_plain(rows_one, qkv_fwd)
    local_heads = packed.shape[1] // (3 * DH)
    packed = packed.reshape(group_rows, local_heads, 3, DH)
    seq_shape = (seq_count, LENGTH, local_heads, DH)
    query_rot = (
        rotate_heads(packed[:, :, 0], cosine_table, sine_table)
        .astype(jnp.bfloat16)
        .reshape(seq_shape)
    )
    key_rot = (
        rotate_heads(packed[:, :, 1], cosine_table, sine_table)
        .astype(jnp.bfloat16)
        .reshape(seq_shape)
    )
    value_low = packed[:, :, 2].astype(jnp.bfloat16).reshape(seq_shape)
    attended, self_logs = self_forward(query_rot, key_rot, value_low)
    attended = attended.reshape(group_rows, local_heads * DH).astype(jnp.bfloat16)
    resid_one = resid_in + branch_sum(attended, attn_out_fwd)
    normed_two, scaled_two, inverse_two = layer_norm(resid_one, gain_cross)
    rows_two = spread_rows(normed_two.astype(jnp.bfloat16))
    cross_query = dot_plain(rows_two, cross_q_fwd).astype(jnp.bfloat16).reshape(seq_shape)
    context_flat = conditioning.reshape(seq_count * CTX, conditioning.shape[2])
    cross_pack = (
        dot_plain(context_flat, cross_kv_fwd)
        .astype(jnp.bfloat16)
        .reshape(seq_count, CTX, local_heads, 2, DH)
    )
    cross_key = cross_pack[:, :, :, 0]
    cross_value = cross_pack[:, :, :, 1]
    crossed, cross_logs = cross_forward(cross_query, cross_key, cross_value)
    crossed = crossed.reshape(group_rows, local_heads * DH).astype(jnp.bfloat16)
    resid_two = resid_one + branch_sum(crossed, cross_out_fwd)
    normed_three, scaled_three, inverse_three = layer_norm(resid_two, gain_mlp)
    rows_three = spread_rows(normed_three.astype(jnp.bfloat16))
    gate_pre = dot_plain(rows_three, gate_fwd)
    up_pre = dot_plain(rows_three, up_fwd)
    sigma_gate = jax.nn.sigmoid(gate_pre)
    swish = gate_pre * sigma_gate
    hidden = (swish * up_pre).astype(jnp.bfloat16)
    block_out = resid_two + branch_sum(hidden, down_fwd)
    (
        qkv_back,
        attn_out_back,
        cross_q_back,
        cross_kv_back,
        cross_out_back,
        gate_back,
        up_back,
        down_back,
    ) = gathered
    mlp_seed = spread_grads(cotangent)
    grad_down = dot_rows(hidden, mlp_seed)
    d_hidden = dot_cols(mlp_seed, down_back)
    d_gate = (d_hidden * up_pre * sigma_gate * (1.0 + gate_pre * (1.0 - sigma_gate))).astype(
        jnp.bfloat16
    )
    d_up = (d_hidden * swish).astype(jnp.bfloat16)
    grad_gate = dot_rows(rows_three, d_gate)
    grad_up = dot_rows(rows_three, d_up)
    d_normed = grad_sum(((d_gate, gate_back), (d_up, up_back)))
    d_part, gain_grad_three = norm_backward(d_normed, scaled_three, inverse_three, gain_mlp)
    d_resid = cotangent.astype(jnp.float32) + d_part
    cross_seed = spread_grads(d_resid.astype(jnp.bfloat16))
    grad_cross_out = dot_rows(crossed, cross_seed)
    d_crossed = dot_cols(cross_seed, cross_out_back).astype(jnp.bfloat16).reshape(seq_shape)
    d_query, d_key, d_value = cross_backward(
        cross_query, cross_key, cross_value, d_crossed, cross_logs
    )
    d_query = d_query.reshape(group_rows, local_heads * DH).astype(jnp.bfloat16)
    d_keyval = (
        jnp.stack([d_key, d_value], axis=3)
        .reshape(seq_count * CTX, local_heads * 2 * DH)
        .astype(jnp.bfloat16)
    )
    grad_cross_q = dot_rows(rows_two, d_query)
    grad_cross_kv = dot_rows(context_flat, d_keyval)
    context_part = dot_cols(d_keyval, cross_kv_back)
    d_normed = grad_sum(((d_query, cross_q_back),))
    d_part, gain_grad_two = norm_backward(d_normed, scaled_two, inverse_two, gain_cross)
    d_resid = d_resid + d_part
    self_seed = spread_grads(d_resid.astype(jnp.bfloat16))
    grad_attn_out = dot_rows(attended, self_seed)
    d_attended = dot_cols(self_seed, attn_out_back).astype(jnp.bfloat16).reshape(seq_shape)
    d_query, d_key, d_value = self_backward(query_rot, key_rot, value_low, d_attended, self_logs)
    head_shape = (group_rows, local_heads, DH)
    d_query = rotate_heads(d_query.reshape(head_shape), cosine_table, -sine_table)
    d_key = rotate_heads(d_key.reshape(head_shape), cosine_table, -sine_table)
    d_packed = jnp.stack([d_query, d_key, d_value.reshape(head_shape)], axis=2)
    d_packed = d_packed.reshape(group_rows, local_heads * 3 * DH).astype(jnp.bfloat16)
    grad_qkv = dot_rows(rows_one, d_packed)
    d_normed = grad_sum(((d_packed, qkv_back),))
    d_part, gain_grad_one = norm_backward(d_normed, scaled_one, inverse_one, gain_attn)
    grad_latents = d_resid + d_part
    grad_context = (
        lax.psum(context_part.astype(jnp.bfloat16), "tensor")
        .astype(jnp.float32)
        .reshape(conditioning.shape)
    )
    gain_one, gain_two, gain_three = lax.psum(
        (gain_grad_one, gain_grad_two, gain_grad_three), ("dp", "tensor")
    )
    summed = (
        lax.psum_scatter(
            grad_qkv.astype(jnp.bfloat16), "dp", scatter_dimension=0, tiled=True
        ).astype(jnp.float32),
        lax.psum_scatter(
            grad_attn_out.astype(jnp.bfloat16), "dp", scatter_dimension=1, tiled=True
        ).astype(jnp.float32),
        lax.psum_scatter(
            grad_cross_q.astype(jnp.bfloat16), "dp", scatter_dimension=0, tiled=True
        ).astype(jnp.float32),
        lax.psum_scatter(
            grad_cross_kv.astype(jnp.bfloat16), "dp", scatter_dimension=0, tiled=True
        ).astype(jnp.float32),
        lax.psum_scatter(
            grad_cross_out.astype(jnp.bfloat16), "dp", scatter_dimension=1, tiled=True
        ).astype(jnp.float32),
        lax.psum_scatter(
            grad_gate.astype(jnp.bfloat16), "dp", scatter_dimension=0, tiled=True
        ).astype(jnp.float32),
        lax.psum_scatter(
            grad_up.astype(jnp.bfloat16), "dp", scatter_dimension=0, tiled=True
        ).astype(jnp.float32),
        lax.psum_scatter(
            grad_down.astype(jnp.bfloat16), "dp", scatter_dimension=1, tiled=True
        ).astype(jnp.float32),
    )
    return (
        block_out,
        grad_latents,
        grad_context,
        gain_one,
        summed[0],
        summed[1],
        gain_two,
        summed[2],
        summed[3],
        summed[4],
        gain_three,
        summed[5],
        summed[6],
        summed[7],
    )


def solution(mesh):
    in_specs = (
        P(("dp", "tensor"), None),
        P("dp", None, None),
        P(),
        P("dp", "tensor"),
        P("tensor", "dp"),
        P(),
        P("dp", "tensor"),
        P("dp", "tensor"),
        P("tensor", "dp"),
        P(),
        P("dp", "tensor"),
        P("dp", "tensor"),
        P("tensor", "dp"),
        P(("dp", "tensor"), None),
    )
    out_specs = (
        P(("dp", "tensor"), None),
        P(("dp", "tensor"), None),
        P("dp", None, None),
        P(),
        P("dp", "tensor"),
        P("tensor", "dp"),
        P(),
        P("dp", "tensor"),
        P("dp", "tensor"),
        P("tensor", "dp"),
        P(),
        P("dp", "tensor"),
        P("dp", "tensor"),
        P("tensor", "dp"),
    )
    return jax.shard_map(
        per_device, mesh=mesh, in_specs=in_specs, out_specs=out_specs, check_vma=False
    )
```

profile of v0, /device:TPU:0, one launch (start us, length us, event | category | flops | bytes accessed | tf_op | source)
XLA Modules:
  0.0 1527.8 jit_solution(17127173364605925483)
XLA Ops:
  15.8 44.1 %all-gather.15.cloned.1.call-done = bf16[1024,1536]{1,0:T(8,128)(2,1)} async-done(((bf16[256,1536]{1,0:T(8,128)(2,1)}), bf16[1024,1536]{1,0:T(8,128)(2,1)}) %all-gather.15.cloned.1.call-update) | async-done | bytes 3145744 | tf_op jit(solution)/shard_map/all_gather | solution.py:71
  60.0 43.8 %all-gather.17.cloned.1.call-done = bf16[1536,1152]{1,0:T(8,128)(2,1)} async-done(((bf16[192,1152]{1,0:T(8,128)(2,1)}), bf16[1536,1152]{1,0:T(8,128)(2,1)}) %all-gather.17.cloned.1.call-update) | async-done | bytes 3538960 | tf_op jit(solution)/shard_map/all_gather | solution.py:228
  114.6 20.0 %while.47 = (s32[]{:T(128)}, bf16[2,512,6,64]{1,3,2,0:T(8,128)(2,1)S(1)}, f32[2,6,512]{2,1,0:T(8,128)S(1)}, bf16[2,512,6,64]{1,3,2,0:T(8,128)(2,1)}, bf16[1024,6...) while((s32[]{:T(128)}, bf16[2,512,6,64]{1,3,2,0:T(8,128)(2,1)S(1)}, ...), condition=%wide.region_5.6_spmd, body=%wide.region_2.5_spmd.sunk | while | flops 833614848 | bytes 40620128 | solution.py:113
  144.4 66.6 %reduce-scatter.17.cloned.1.call-done = f32[256,1536]{1,0:T(8,128)} async-done(((f32[1024,1536]{1,0:T(8,128)}), f32[256,1536]{1,0:T(8,128)}) %reduce-scatter.17.cloned.1.call-update) | async-done | bytes 1572880 | tf_op jit(solution)/shard_map/reduce_scatter | solution.py:79
  215.9 19.9 %all-gather.21.cloned.1.call-done = bf16[768,768]{1,0:T(8,128)(2,1)} async-done(((bf16[96,768]{1,0:T(8,128)(2,1)}), bf16[768,768]{1,0:T(8,128)(2,1)}) %all-gather.21.cloned.1.call-update) | async-done | bytes 1179664 | tf_op jit(solution)/shard_map/all_gather | solution.py:231
  240.3 20.0 %all-gather.25.cloned.1.call-done = bf16[1536,384]{1,0:T(8,128)(2,1)} async-done(((bf16[192,384]{1,0:T(8,128)(2,1)}), bf16[1536,384]{1,0:T(8,128)(2,1)}) %all-gather.25.cloned.1.call-update) | async-done | bytes 1179664 | tf_op jit(solution)/shard_map/all_gather | solution.py:230
  260.3 46.2 %all-gather.23.cloned.1.call-done = bf16[1024,1536]{1,0:T(8,128)(2,1)} async-done(((bf16[256,1536]{1,0:T(8,128)(2,1)}), bf16[1024,1536]{1,0:T(8,128)(2,1)}) %all-gather.23.cloned.1.call-update) | async-done | bytes 3145744 | tf_op jit(solution)/shard_map/all_gather | solution.py:71
  314.0 17.4 %all-gather.27.cloned.1.call-done = bf16[384,1536]{0,1:T(8,128)(2,1)} async-done(((bf16[384,192]{0,1:T(8,128)(2,1)}), bf16[384,1536]{0,1:T(8,128)(2,1)}) %all-gather.27.cloned.1.call-update) | async-done | bytes 1179664 | tf_op jit(solution)/shard_map/all_gather | solution.py:232
  339.8 67.8 %reduce-scatter.19.cloned.1.call-done = f32[256,1536]{1,0:T(8,128)} async-done(((f32[1024,1536]{1,0:T(8,128)}), f32[256,1536]{1,0:T(8,128)}) %reduce-scatter.19.cloned.1.call-update) | async-done | bytes 1572880 | tf_op jit(solution)/shard_map/reduce_scatter | solution.py:79
  418.4 42.4 %all-gather.33.cloned.1.call-done = bf16[1536,1536]{1,0:T(8,128)(2,1)} async-done(((bf16[192,1536]{1,0:T(8,128)(2,1)}), bf16[1536,1536]{1,0:T(8,128)(2,1)}) %all-gather.33.cloned.1.call-update) | async-done | bytes 4718608 | tf_op jit(solution)/shard_map/all_gather | solution.py:234
  460.9 45.2 %all-gather.29.cloned.1.call-done = bf16[1024,1536]{1,0:T(8,128)(2,1)} async-done(((bf16[256,1536]{1,0:T(8,128)(2,1)}), bf16[1024,1536]{1,0:T(8,128)(2,1)}) %all-gather.29.cloned.1.call-update) | async-done | bytes 3145744 | tf_op jit(solution)/shard_map/all_gather | solution.py:71
  515.8 43.5 %all-gather.31.cloned.1.call-done = bf16[1536,1536]{1,0:T(8,128)(2,1)} async-done(((bf16[192,1536]{1,0:T(8,128)(2,1)}), bf16[1536,1536]{1,0:T(8,128)(2,1)}) %all-gather.31.cloned.1.call-update) | async-done | bytes 4718608 | tf_op jit(solution)/shard_map/all_gather | solution.py:233
  569.1 34.9 %all-gather.37.cloned.1.call-done = bf16[1024,1536]{1,0:T(8,128)(2,1)} async-done(((bf16[256,1536]{1,0:T(8,128)(2,1)}), bf16[1024,1536]{1,0:T(8,128)(2,1)}) %all-gather.37.cloned.1.call-update) | async-done | bytes 3145744 | tf_op jit(solution)/shard_map/all_gather | solution.py:75
  604.0 53.2 %all-gather.35.cloned.1.call-done = bf16[1536,1536]{0,1:T(8,128)(2,1)} async-done(((bf16[1536,192]{0,1:T(8,128)(2,1)}), bf16[1536,1536]{0,1:T(8,128)(2,1)}) %all-gather.35.cloned.1.call-update) | async-done | bytes 4718608 | tf_op jit(solution)/shard_map/all_gather | solution.py:235
  657.2 13.7 multiply_convert_fusion.1
  685.4 9.9 fusion.87
  695.5 59.0 %reduce-scatter.23.cloned.1.call-done = f32[256,1536]{1,0:T(8,128)} async-done(((f32[1024,1536]{1,0:T(8,128)}), f32[256,1536]{1,0:T(8,128)}) %reduce-scatter.23.cloned.1.call-update) | async-done | bytes 1572880 | tf_op jit(solution)/shard_map/reduce_scatter | solution.py:86
  758.2 69.4 %reduce-scatter.21.cloned.1.call-done = f32[256,1536]{1,0:T(8,128)} async-done(((f32[1024,1536]{1,0:T(8,128)}), f32[256,1536]{1,0:T(8,128)}) %reduce-scatter.21.cloned.1.call-update) | async-done | bytes 1572880 | tf_op jit(solution)/shard_map/reduce_scatter | solution.py:79
  834.4 42.7 %all-gather.39.cloned.1.call-done = bf16[1024,1536]{1,0:T(8,128)(2,1)} async-done(((bf16[256,1536]{1,0:T(8,128)(2,1)}), bf16[1024,1536]{1,0:T(8,128)(2,1)}) %all-gather.39.cloned.1.call-update) | async-done | bytes 3145744 | tf_op jit(solution)/shard_map/all_gather | solution.py:75
  890.1 70.3 %reduce-scatter.25.cloned.1.call-done = f32[256,1536]{1,0:T(8,128)} async-done(((f32[1024,1536]{1,0:T(8,128)}), f32[256,1536]{1,0:T(8,128)}) %reduce-scatter.25.cloned.1.call-update) | async-done | bytes 1572880 | tf_op jit(solution)/shard_map/reduce_scatter | solution.py:86
  1028.1 84.1 %while.48 = (s32[]{:T(128)}, f32[1024,6,64]{0,2,1:T(8,128)S(1)}, f32[1024,6,64]{0,2,1:T(8,128)}, f32[2,512,6,64]{1,0,3,2:T(2,128)}, bf16[2,512,6,64]{1,3,2,0:T(8...) while((s32[]{:T(128)}, f32[1024,6,64]{0,2,1:T(8,128)S(1)}, ...), condition=%wide.region_24.25_spmd.clone, body=%wide.region_22.24_spmd.clone.sunk | while | flops 2053174272 | bytes 108613792 | solution.py:162
  1054.9 15.0 dynamic_update_slice.31
  1097.2 15.0 dynamic_update_slice.31
  1137.9 41.8 %reduce-scatter.41.cloned.1.call-done = bf16[1536,192]{0,1:T(8,128)(2,1)} async-done(((bf16[1536,1536]{0,1:T(8,128)(2,1)}), bf16[1536,192]{0,1:T(8,128)(2,1)}) %reduce-scatter.41.cloned.1.call-update) | async-done | bytes 589840 | tf_op jit(solution)/shard_map/reduce_scatter | solution.py:369
  1181.9 42.3 %all-reduce.3.cloned.1.call-done = bf16[1,130,768]{2,1,0:T(8,128)(2,1)} async-done(((bf16[1,130,768]{2,1,0:T(8,128)(2,1)}), bf16[1,130,768]{2,1,0:T(8,128)(2,1)}) %all-reduce.3.cloned.1.call-update) | async-done | bytes 199696 | tf_op jit(solution)/shard_map/psum | solution.py:340
  1226.2 33.1 %reduce-scatter.43.cloned.1.call-done = bf16[96,768]{1,0:T(8,128)(2,1)} async-done(((bf16[768,768]{1,0:T(8,128)(2,1)}), bf16[96,768]{1,0:T(8,128)(2,1)}) %reduce-scatter.43.cloned.1.call-update) | async-done | bytes 147472
  1261.2 31.6 %reduce-scatter.35.cloned.1.call-done = bf16[384,192]{0,1:T(8,128)(2,1)} async-done(((bf16[384,1536]{0,1:T(8,128)(2,1)}), bf16[384,192]{0,1:T(8,128)(2,1)}) %reduce-scatter.35.cloned.1.call-update) | async-done | bytes 147472 | tf_op jit(solution)/shard_map/reduce_scatter | solution.py:360
  1294.5 31.7 %reduce-scatter.33.cloned.1.call-done = bf16[192,384]{1,0:T(8,128)(2,1)} async-done(((bf16[1536,384]{1,0:T(8,128)(2,1)}), bf16[192,384]{1,0:T(8,128)(2,1)}) %reduce-scatter.33.cloned.1.call-update) | async-done | bytes 147472 | tf_op jit(solution)/shard_map/reduce_scatter | solution.py:354
  1327.8 31.5 %reduce-scatter.31.cloned.1.call-done = bf16[384,192]{0,1:T(8,128)(2,1)} async-done(((bf16[384,1536]{0,1:T(8,128)(2,1)}), bf16[384,192]{0,1:T(8,128)(2,1)}) %reduce-scatter.31.cloned.1.call-update) | async-done | bytes 147472 | tf_op jit(solution)/shard_map/reduce_scatter | solution.py:351
  1360.9 42.8 %reduce-scatter.29.cloned.1.call-done = bf16[192,1152]{1,0:T(8,128)(2,1)} async-done(((bf16[1536,1152]{1,0:T(8,128)(2,1)}), bf16[192,1152]{1,0:T(8,128)(2,1)}) %reduce-scatter.29.cloned.1.call-update) | async-done | bytes 442384 | tf_op jit(solution)/shard_map/reduce_scatter | solution.py:348
  1405.7 69.7 %reduce-scatter.27.cloned.1.call-done = f32[256,1536]{1,0:T(8,128)} async-done(((f32[1024,1536]{1,0:T(8,128)}), f32[256,1536]{1,0:T(8,128)}) %reduce-scatter.27.cloned.1.call-update) | async-done | bytes 1572880 | tf_op jit(solution)/shard_map/reduce_scatter | solution.py:86
  1477.7 40.0 %all-reduce = (f32[1536]{0:T(1024)}, f32[1536]{0:T(1024)}, f32[1536]{0:T(1024)}) all-reduce(f32[1536]{0:T(1024)S(1)} %get-tuple-element.249, f32[1536]{0:T(1024)S(1)} %copy-done.46, f32[1536]{0:T(1024)S(1)} %copy-done.45), channel_id=1, replica_groups=mesh['dp'=8,'tensor'=4] {'dp','tensor'}, use_global_device_ids=true, to_apply=%region_30.31 | all-reduce | flops 4608 | bytes 36864 | tf_op jit(solution)/shard_map/psum | solution.py:344
  (318 shorter events, 307.8 us)
Async XLA Ops:
  7.2 52.8 %all-gather.15.cloned.1.call-start = ((), (), s32[]{:S(2)}) async-start(), calls=%async_computation.14 | async-start | bytes 3932160 | tf_op jit(solution)/shard_map/all_gather | solution.py:71
  13.1 90.6 %all-gather.17.cloned.1.call-start = ((), (), s32[]{:S(2)}) async-start(), calls=%async_computation.15 | async-start | bytes 3981312 | tf_op jit(solution)/shard_map/all_gather | solution.py:228
  14.0 121.6 %all-gather.19.cloned.1.call-start = ((), (), s32[]{:S(2)}) async-start(), calls=%async_computation.16 | async-start | bytes 1327104 | tf_op jit(solution)/shard_map/all_gather | solution.py:229
  14.8 196.2 %reduce-scatter.17.cloned.1.call-start = ((), (), s32[]{:S(2)}) async-start(), calls=%async_computation.17 | async-start | bytes 7864320 | tf_op jit(solution)/shard_map/reduce_scatter | solution.py:79
  141.8 94.0 %all-gather.21.cloned.1.call-start = ((), (), s32[]{:S(2)}) async-start(), calls=%async_computation.18 | async-start | bytes 1327104 | tf_op jit(solution)/shard_map/all_gather | solution.py:231
  143.4 116.9 %all-gather.25.cloned.1.call-start = ((), (), s32[]{:S(2)}) async-start(), calls=%async_computation.20 | async-start | bytes 1327104 | tf_op jit(solution)/shard_map/all_gather | solution.py:230
  144.2 162.3 %all-gather.23.cloned.1.call-start = ((), (), s32[]{:S(2)}) async-start(), calls=%async_computation.19 | async-start | bytes 3932160 | tf_op jit(solution)/shard_map/all_gather | solution.py:71
  215.1 116.3 %all-gather.27.cloned.1.call-start = ((), (), s32[]{:S(2)}) async-start(), calls=%async_computation.21 | async-start | bytes 1327104 | tf_op jit(solution)/shard_map/all_gather | solution.py:232
  215.8 191.8 %reduce-scatter.19.cloned.1.call-start = ((), (), s32[]{:S(2)}) async-start(), calls=%async_computation.22 | async-start | bytes 7864320 | tf_op jit(solution)/shard_map/reduce_scatter | solution.py:79
  337.5 123.4 %all-gather.33.cloned.1.call-start = ((), (), s32[]{:S(2)}) async-start(), calls=%async_computation.25 | async-start | bytes 5308416 | tf_op jit(solution)/shard_map/all_gather | solution.py:234
  339.8 166.3 %all-gather.29.cloned.1.call-start = ((), (), s32[]{:S(2)}) async-start(), calls=%async_computation.23 | async-start | bytes 3932160 | tf_op jit(solution)/shard_map/all_gather | solution.py:71
  412.7 146.7 %all-gather.31.cloned.1.call-start = ((), (), s32[]{:S(2)}) async-start(), calls=%async_computation.24 | async-start | bytes 5308416 | tf_op jit(solution)/shard_map/all_gather | solution.py:233
  414.9 189.1 %all-gather.37.cloned.1.call-start = ((), (), s32[]{:S(2)}) async-start(), calls=%async_computation.28 | async-start | bytes 3932160 | tf_op jit(solution)/shard_map/all_gather | solution.py:75
  415.6 241.6 %all-gather.35.cloned.1.call-start = ((), (), s32[]{:S(2)}) async-start(), calls=%async_computation.26 | async-start | bytes 5308416 | tf_op jit(solution)/shard_map/all_gather | solution.py:235
  418.0 336.5 %reduce-scatter.23.cloned.1.call-start = ((), (), s32[]{:S(2)}) async-start(), calls=%async_computation.29 | async-start | bytes 7864320 | tf_op jit(solution)/shard_map/reduce_scatter | solution.py:86
  685.3 142.3 %reduce-scatter.21.cloned.1.call-start = ((), (), s32[]{:S(2)}) async-start(), calls=%async_computation.27 | async-start | bytes 7864320 | tf_op jit(solution)/shard_map/reduce_scatter | solution.py:79
  695.3 181.8 %all-gather.39.cloned.1.call-start = ((), (), s32[]{:S(2)}) async-start(), calls=%async_computation.30 | async-start | bytes 3932160 | tf_op jit(solution)/shard_map/all_gather | solution.py:75
  832.9 127.5 %reduce-scatter.25.cloned.1.call-start = ((), (), s32[]{:S(2)}) async-start(), calls=%async_computation.31 | async-start | bytes 7864320 | tf_op jit(solution)/shard_map/reduce_scatter | solution.py:86
  890.1 123.4 %all-gather.41.cloned.1.call-start = ((), (), s32[]{:S(2)}) async-start(), calls=%async_computation.32 | async-start | bytes 3932160 | tf_op jit(solution)/shard_map/all_gather | solution.py:75
  967.2 166.3 %reduce-scatter.39.cloned.1.call-start = ((), (), s32[]{:S(2)}) async-start(), calls=%async_computation.40 | async-start | bytes 5308416 | tf_op jit(solution)/shard_map/reduce_scatter | solution.py:366
  976.4 159.2 %reduce-scatter.37.cloned.1.call-start = ((), (), s32[]{:S(2)}) async-start(), calls=%async_computation.39 | async-start | bytes 5308416 | tf_op jit(solution)/shard_map/reduce_scatter | solution.py:363
  986.2 193.5 %reduce-scatter.41.cloned.1.call-start = ((), (), s32[]{:S(2)}) async-start(), calls=%async_computation.41 | async-start | bytes 5308416 | tf_op jit(solution)/shard_map/reduce_scatter | solution.py:369
  995.5 228.7 %all-reduce.3.cloned.1.call-start = ((), (), s32[]{:S(2)}) async-start(), calls=%async_computation.34 | async-start | bytes 417792 | tf_op jit(solution)/shard_map/psum | solution.py:340
  1001.3 258.0 %reduce-scatter.43.cloned.1.call-start = ((), (), s32[]{:S(2)}) async-start(), calls=%async_computation.42 | async-start | bytes 1327104
  1003.3 289.5 %reduce-scatter.35.cloned.1.call-start = ((), (), s32[]{:S(2)}) async-start(), calls=%async_computation.38 | async-start | bytes 1327104 | tf_op jit(solution)/shard_map/reduce_scatter | solution.py:360
  1008.2 317.9 %reduce-scatter.33.cloned.1.call-start = ((), (), s32[]{:S(2)}) async-start(), calls=%async_computation.37 | async-start | bytes 1327104 | tf_op jit(solution)/shard_map/reduce_scatter | solution.py:354
  1013.2 346.1 %reduce-scatter.31.cloned.1.call-start = ((), (), s32[]{:S(2)}) async-start(), calls=%async_computation.36 | async-start | bytes 1327104 | tf_op jit(solution)/shard_map/reduce_scatter | solution.py:351
  1028.0 375.7 %reduce-scatter.29.cloned.1.call-start = ((), (), s32[]{:S(2)}) async-start(), calls=%async_computation.35 | async-start | bytes 3981312 | tf_op jit(solution)/shard_map/reduce_scatter | solution.py:348
  1125.1 350.3 %reduce-scatter.27.cloned.1.call-start = ((), (), s32[]{:S(2)}) async-start(), calls=%async_computation.33 | async-start | bytes 7864320 | tf_op jit(solution)/shard_map/reduce_scatter | solution.py:86
  1181.9 293.5 %copy-start.42 = (f32[1536]{0:T(1024)S(1)}, f32[1536]{0:T(1024)}, u32[]{:S(2)}) copy-start(f32[1536]{0:T(1024)} %param.20) | copy-start | bytes 18436
  1181.9 293.5 %copy-start.48 = (f32[256]{0:T(256)S(1)}, f32[256]{0:T(256)}, u32[]{:S(2)}) copy-start(f32[256]{0:T(256)} %copy-done.47) | copy-start | bytes 3076
  1181.9 293.5 %copy-start.52 = (f32[256]{0:T(256)S(1)}, f32[256]{0:T(256)}, u32[]{:S(2)}) copy-start(f32[256]{0:T(256)} %copy-done.51) | copy-start | bytes 3076
  (56 other events, 1406.6 us)
Sparse Core Ops, SparseCore 0:
  13.3 46.6 all-gather.14
  62.2 41.5 all-gather.16
  106.0 21.5 all-gather.18
  141.9 69.0 reduce-scatter.16
  213.1 22.6 all-gather.20
  237.8 22.4 all-gather.24
  262.7 43.7 all-gather.22
  308.7 22.6 all-gather.26
  337.6 69.9 reduce-scatter.18
  409.1 51.6 all-gather.32
  463.3 42.7 all-gather.28
  507.6 51.6 all-gather.30
  561.2 42.7 all-gather.36
  605.5 51.6 all-gather.34
  685.4 68.9 reduce-scatter.22
  757.3 70.2 reduce-scatter.20
  833.1 43.9 all-gather.38
  890.2 70.2 reduce-scatter.24
  967.3 43.9 all-gather.40
  1013.4 54.9 reduce-scatter.38
  1070.7 53.2 reduce-scatter.36
  1126.4 53.3 reduce-scatter.40
  1183.2 40.9 all-reduce.2
  1226.4 32.8 reduce-scatter.42
  1261.7 31.1 reduce-scatter.34
  1295.1 31.0 reduce-scatter.32
  1328.4 30.8 reduce-scatter.30
  1361.7 41.9 reduce-scatter.28
  1406.7 68.6 reduce-scatter.26
where the time goes:
time: 1540 us; the launch traced here: 1530 us
  waiting for transfers between devices  1110 us (72%)
  matrix products  214 us (14%)
  other arithmetic  81.9 us (5%)
  local copies, waits for them, and re-layouts  61.9 us (4%)
  blocking collectives  40 us (3%)
  between operations  15.5 us (1%)
    reduce_scatter x3, waiting for transfers between devices, branch_sum(): lax.psum_scatter(dot_plain(left_rows, weights), 'tensor', scatter_dimensi...  204 us
    reduce_scatter x3, waiting for transfers between devices, grad_sum(): lax.psum_scatter(reduce(jnp.add, partials), 'tensor', scatter_dimension=0...  199 us
    all_gather x3, waiting for transfers between devices, spread_rows(): return lax.all_gather(values, 'tensor', axis=0, tiled=True)  136 us
    all_gather x3, waiting for transfers between devices, spread_grads(): return lax.all_gather(values, 'tensor', axis=0, tiled=True)  77.6 us
    dot_general x8, matrix products, dot_plain(): return jnp.dot(left_op, right_op, preferred_element_type=jnp.float32)  53.8 us
    all_gather x1, waiting for transfers between devices, per_device(): lax.all_gather(w_down.astype(jnp.bfloat16), 'dp', axis=1, tiled=True)  53.2 us
    dot_general x8, matrix products, dot_cols(): lax.dot_general(left_op, right_op, (((1,), (1,)), ((), ())), preferred_el...  50.3 us
    dot_general x8, matrix products, dot_rows(): lax.dot_general(left_op, right_op, (((0,), (0,)), ((), ())), preferred_el...  48.6 us
  transfers between devices with their start and end apart: 29, of which 25 were waited for; matrix products, arithmetic and copies ran while one was open for 18% of the time, Pallas kernels for 0%

commit v1 on v0

v1 whole, which is shorter than its diff:
```python
from functools import reduce

import jax
import jax.numpy as jnp
from jax import lax
from jax.experimental import pallas as pl
from jax.experimental.pallas import tpu as pltpu
from jax.sharding import PartitionSpec as P

DH = 64
CTX = 130
LENGTH = 1024
PAIR = 2 * DH
ROWS = 256
VMEM_BYTES = 48 * 2**20

norm_eps = 1e-05
rope_base = 10000.0


def head_turn(values, cosine, minus_sine, plus_sine):
    quarter = DH // 4
    ahead = pltpu.roll(values, PAIR - quarter, 1)
    behind = pltpu.roll(values, quarter, 1)
    return values * cosine + ahead * minus_sine + behind * plus_sine


def half_mask(shape, axis, which):
    place = lax.broadcasted_iota(jnp.int32, shape, axis)
    return (place >= DH) if which else (place < DH)


def attend_kernel(q_ref, k_ref, v_ref, cos_ref, msin_ref, psin_ref, out_ref, rot_ref, log_ref, kt_ref, vm_ref):
    pairs = pl.num_programs(0)
    pair = pl.program_id(0)
    turn = (cos_ref[...], msin_ref[...], psin_ref[...])
    query = head_turn(q_ref[...], *turn).astype(jnp.bfloat16)
    key = head_turn(k_ref[...], *turn).astype(jnp.bfloat16)
    value = v_ref[...].astype(jnp.bfloat16)
    for part, array in enumerate((query, key, value)):
        start = pl.multiple_of((part * pairs + pair) * PAIR, PAIR)
        rot_ref[:, pl.ds(start, PAIR)] = array
    key_t = key.astype(jnp.float32).T
    for which in range(2):
        kt_ref[which] = jnp.where(half_mask(key_t.shape, 0, which), key_t, 0.0).astype(jnp.bfloat16)
        vm_ref[which] = jnp.where(half_mask(value.shape, 1, which), value.astype(jnp.float32), 0.0).astype(jnp.bfloat16)
    q_start = pl.multiple_of(pair * PAIR, PAIR)

    def one_block(step, carry):
        rows = pl.ds(pl.multiple_of(step * ROWS, ROWS), ROWS)
        block = rot_ref[rows, pl.ds(q_start, PAIR)] * jnp.bfloat16(DH**-0.5)
        outs, logs = [], []
        for which in range(2):
            scores = jnp.dot(block, kt_ref[which], preferred_element_type=jnp.float32)
            peak = jnp.max(scores, axis=1, keepdims=True)
            shifted = jnp.exp(scores - peak)
            total = jnp.sum(shifted, axis=1, keepdims=True)
            product = jnp.dot(shifted.astype(jnp.bfloat16), vm_ref[which], preferred_element_type=jnp.float32)
            outs.append(product * (1.0 / total))
            logs.append(peak + jnp.log(total))
        out_ref[rows, :] = (outs[0] + outs[1]).astype(jnp.bfloat16)
        low = half_mask((ROWS, PAIR), 1, 0)
        log_ref[rows, :] = jnp.where(low, logs[0], logs[1])
        return carry

    lax.fori_loop(0, LENGTH // ROWS, one_block, 0)


def attend_back_kernel(
    q_ref, k_ref, v_ref, grad_ref, log_ref, cos_ref, msin_ref, psin_ref, out_ref,
    kt_ref, vt_ref, km_ref, qt_ref, gt_ref, dq_ref, dk_ref, dv_ref,
):
    pairs = pl.num_programs(0)
    pair = pl.program_id(0)
    key_t = k_ref[...].astype(jnp.float32).T
    value_t = v_ref[...].astype(jnp.float32).T
    for which in range(2):
        keep = half_mask(key_t.shape, 0, which)
        kt_ref[which] = jnp.where(keep, key_t, 0.0).astype(jnp.bfloat16)
        vt_ref[which] = jnp.where(keep, value_t, 0.0).astype(jnp.bfloat16)
        key = k_ref[...].astype(jnp.float32)
        km_ref[which] = jnp.where(half_mask(key.shape, 1, which), key, 0.0).astype(jnp.bfloat16)
    qt_ref[...] = (q_ref[...].astype(jnp.float32) * DH**-0.5).T.astype(jnp.bfloat16)
    gt_ref[...] = grad_ref[...].astype(jnp.float32).T.astype(jnp.bfloat16)
    dk_ref[...] = jnp.zeros_like(dk_ref)
    dv_ref[...] = jnp.zeros_like(dv_ref)

    def one_block(step, carry):
        rows = pl.ds(pl.multiple_of(step * ROWS, ROWS), ROWS)
        block = q_ref[rows, :] * jnp.bfloat16(DH**-0.5)
        grads = grad_ref[rows, :]
        d_query = jnp.zeros((ROWS, PAIR), jnp.float32)
        for which in range(2):
            half = slice(which * DH, (which + 1) * DH)
            scores = jnp.dot(block, kt_ref[which], preferred_element_type=jnp.float32)
            probs = jnp.exp(scores - log_ref[rows, which * DH : which * DH + 1])
            d_prob = jnp.dot(grads, vt_ref[which], preferred_element_type=jnp.float32)
            center = jnp.sum(probs * d_prob, axis=1, keepdims=True)
            d_score = (probs * (d_prob - center)).astype(jnp.bfloat16)
            d_query += jnp.dot(d_score, km_ref[which], preferred_element_type=jnp.float32)
            dk_ref[half, :] += jnp.dot(qt_ref[half, rows], d_score, preferred_element_type=jnp.float32)
            dv_ref[half, :] += jnp.dot(
                gt_ref[half, rows], probs.astype(jnp.bfloat16), preferred_element_type=jnp.float32
            )
        dq_ref[rows, :] = d_query * DH**-0.5
        return carry

    lax.fori_loop(0, LENGTH // ROWS, one_block, 0)
    turn = (cos_ref[...], -msin_ref[...], -psin_ref[...])
    results = (head_turn(dq_ref[...], *turn), head_turn(dk_ref[...].T, *turn), dv_ref[...].T)
    for part, array in enumerate(results):
        start = pl.multiple_of((part * pairs + pair) * PAIR, PAIR)
        out_ref[:, pl.ds(start, PAIR)] = array.astype(jnp.bfloat16)


def column_block(offset):
    return pl.BlockSpec((LENGTH, PAIR), lambda pair: (0, pair + offset))


def whole_block(columns):
    return pl.BlockSpec((LENGTH, columns), lambda pair: (0, 0))


def attend(packed, tables):
    columns = packed.shape[1]
    pairs = columns // (3 * PAIR)
    return pl.pallas_call(
        attend_kernel,
        grid=(pairs,),
        in_specs=[column_block(part * pairs) for part in range(3)] + [whole_block(PAIR)] * 3,
        out_specs=[column_block(0), whole_block(columns), column_block(0)],
        out_shape=[
            jax.ShapeDtypeStruct((LENGTH, pairs * PAIR), jnp.bfloat16),
            jax.ShapeDtypeStruct((LENGTH, columns), jnp.bfloat16),
            jax.ShapeDtypeStruct((LENGTH, pairs * PAIR), jnp.float32),
        ],
        scratch_shapes=[pltpu.VMEM((2, PAIR, LENGTH), jnp.bfloat16), pltpu.VMEM((2, LENGTH, PAIR), jnp.bfloat16)],
        compiler_params=pltpu.CompilerParams(vmem_limit_bytes=VMEM_BYTES),
        cost_estimate=pl.CostEstimate(flops=pairs * 2**32, bytes_accessed=2**24, transcendentals=pairs * 2**21),
    )(packed, packed, packed, *tables)


def attend_back(rotated, d_attended, logs, tables):
    columns = rotated.shape[1]
    pairs = columns // (3 * PAIR)
    tall = pltpu.VMEM((PAIR, LENGTH), jnp.bfloat16)
    return pl.pallas_call(
        attend_back_kernel,
        grid=(pairs,),
        in_specs=[column_block(part * pairs) for part in range(3)]
        + [column_block(0), column_block(0)]
        + [whole_block(PAIR)] * 3,
        out_specs=whole_block(columns),
        out_shape=jax.ShapeDtypeStruct((LENGTH, columns), jnp.bfloat16),
        scratch_shapes=[
            pltpu.VMEM((2, PAIR, LENGTH), jnp.bfloat16),
            pltpu.VMEM((2, PAIR, LENGTH), jnp.bfloat16),
            pltpu.VMEM((2, LENGTH, PAIR), jnp.bfloat16),
            tall,
            tall,
            pltpu.VMEM((LENGTH, PAIR), jnp.float32),
            pltpu.VMEM((PAIR, LENGTH), jnp.float32),
            pltpu.VMEM((PAIR, LENGTH), jnp.float32),
        ],
        compiler_params=pltpu.CompilerParams(vmem_limit_bytes=VMEM_BYTES),
        cost_estimate=pl.CostEstimate(flops=pairs * 2**33, bytes_accessed=2**24, transcendentals=pairs * 2**21),
    )(rotated, rotated, rotated, d_attended, logs, *tables)


def turn_tables(positions):
    quarter = DH // 4
    frequency = jnp.exp(-jnp.log(rope_base) * jnp.arange(quarter).astype(jnp.float32) / quarter)
    angles = positions.astype(jnp.float32)[:, None] * frequency[None, :]
    cosine, sine = jnp.cos(angles), jnp.sin(angles)
    zeros, ones = jnp.zeros_like(sine), jnp.ones_like(sine)
    rows = (
        jnp.concatenate([cosine, cosine, ones, ones], axis=1),
        jnp.concatenate([-sine, zeros, zeros, zeros], axis=1),
        jnp.concatenate([zeros, sine, zeros, zeros], axis=1),
    )
    return tuple(jnp.concatenate([row, row], axis=1) for row in rows)


def dot_plain(left_op, right_op):
    return jnp.dot(left_op, right_op, preferred_element_type=jnp.float32)


def dot_rows(left_op, right_op):
    return lax.dot_general(
        left_op, right_op, (((0,), (0,)), ((), ())), preferred_element_type=jnp.float32
    )


def dot_cols(left_op, right_op):
    return lax.dot_general(
        left_op, right_op, (((1,), (1,)), ((), ())), preferred_element_type=jnp.float32
    )


def layer_norm(values, gain_vec):
    center = values - jnp.mean(values, axis=-1, keepdims=True)
    spread = jnp.mean(center * center, axis=-1, keepdims=True)
    inverse = lax.rsqrt(spread + norm_eps)
    scaled = center * inverse
    return (scaled * gain_vec, scaled, inverse)


def norm_backward(upstream, scaled, inverse, gain_vec):
    weighted = upstream * gain_vec
    inner = jnp.mean(weighted, axis=-1, keepdims=True) + scaled * jnp.mean(
        weighted * scaled, axis=-1, keepdims=True
    )
    return (inverse * (weighted - inner), jnp.sum(upstream * scaled, axis=0))


def swap(values, bit):
    return lax.ppermute(values, "tensor", [(member, member ^ bit) for member in range(4)])


def spread_rows(values):
    if lax.axis_size("tensor") != 4:
        return lax.all_gather(values, "tensor", axis=0, tiled=True)
    half = values.shape[0] // 2
    near, far = swap(values, 1), swap(values, 2)
    return jnp.concatenate([values, near, far, swap(near[:half], 2), swap(far[half:], 1)], axis=0)


def sum_rows(partial):
    if lax.axis_size("tensor") != 4:
        return lax.psum_scatter(
            partial.astype(jnp.bfloat16), "tensor", scatter_dimension=0, tiled=True
        ).astype(jnp.float32)
    size = partial.shape[0] // 4
    half = size // 2
    own, near, far, last = (partial[part * size : (part + 1) * size] for part in range(4))
    first = swap(last[:half].astype(jnp.bfloat16), 1)
    second = swap(last[half:].astype(jnp.bfloat16), 2)
    far = jnp.concatenate([far[:half] + first.astype(jnp.float32), far[half:]], axis=0)
    near = jnp.concatenate([near[:half], near[half:] + second.astype(jnp.float32)], axis=0)
    return (
        own
        + swap(near.astype(jnp.bfloat16), 1).astype(jnp.float32)
        + swap(far.astype(jnp.bfloat16), 2).astype(jnp.float32)
    )


def group_positions(rows):
    group = lax.axis_size("tensor")
    blocks = jnp.arange(group)
    if group == 4:
        blocks = blocks ^ lax.axis_index("tensor")
    return (blocks[:, None] * rows + jnp.arange(rows)[None, :]).reshape(-1)


def cross_forward(queries, keys_in, values_in):
    scores = jnp.einsum("qhd,khd->hqk", queries, keys_in, preferred_element_type=jnp.float32) * DH ** (-0.5)
    peak_score = jnp.max(scores, axis=-1, keepdims=True)
    shifted = jnp.exp(scores - peak_score)
    totals = jnp.sum(shifted, axis=-1, keepdims=True)
    probabilities = (shifted / totals).astype(jnp.bfloat16)
    output = jnp.einsum("hqk,khd->qhd", probabilities, values_in, preferred_element_type=jnp.float32)
    return (output, peak_score + jnp.log(totals))


def cross_backward(queries, keys_in, values_in, d_output, log_totals):
    scaling = DH ** (-0.5)
    scores = jnp.einsum("qhd,khd->hqk", queries, keys_in, preferred_element_type=jnp.float32) * scaling
    probabilities = jnp.exp(scores - log_totals)
    d_prob = jnp.einsum("qhd,khd->hqk", d_output, values_in, preferred_element_type=jnp.float32)
    center = jnp.sum(probabilities * d_prob, axis=-1, keepdims=True)
    d_score = (probabilities * (d_prob - center)).astype(jnp.bfloat16)
    d_query = jnp.einsum("hqk,khd->qhd", d_score, keys_in, preferred_element_type=jnp.float32) * scaling
    d_key = jnp.einsum("hqk,qhd->khd", d_score, queries, preferred_element_type=jnp.float32) * scaling
    d_value = jnp.einsum(
        "hqk,qhd->khd", probabilities.astype(jnp.bfloat16), d_output, preferred_element_type=jnp.float32
    )
    return (d_query, d_key, d_value)


def by_part(columns, parts):
    rows = columns.shape[0]
    return columns.reshape(rows, -1, parts, DH).swapaxes(1, 2).reshape(rows, -1)


def by_head(columns, parts):
    rows = columns.shape[0]
    return columns.reshape(rows, parts, -1, DH).swapaxes(1, 2).reshape(rows, -1)


def pad_heads(columns, parts):
    rows, width = columns.shape
    each = width // parts
    if each % PAIR == 0:
        return columns
    return jnp.pad(columns.reshape(rows, parts, each), ((0, 0), (0, 0), (0, -each % PAIR))).reshape(rows, -1)


def drop_heads(columns, parts, width):
    rows = columns.shape[0]
    return columns.reshape(rows, parts, -1)[:, :, : width // parts].reshape(rows, width)


def dp_sum(grads):
    return lax.psum_scatter(grads.astype(jnp.bfloat16), "dp", scatter_dimension=0, tiled=True)


def after(value, earlier):
    return lax.optimization_barrier((value, earlier))[0]


def per_device(
    latents,
    conditioning,
    gain_attn,
    w_qkv,
    w_attn_out,
    gain_cross,
    w_cross_q,
    w_cross_kv,
    w_cross_out,
    gain_mlp,
    w_gate,
    w_up,
    w_down,
    cotangent,
):
    low = jnp.bfloat16
    heads_wide = w_cross_q.shape[1]
    hidden_wide = w_gate.shape[1]
    resid_in = latents.astype(jnp.float32)
    normed_one, scaled_one, inverse_one = layer_norm(resid_in, gain_attn)
    rows_one = spread_rows(normed_one.astype(low))
    own_qkv = by_part(w_qkv.astype(low), 3)
    qkv_all = lax.all_gather(own_qkv, "dp", axis=0, tiled=True)
    own_kv = by_part(w_cross_kv.astype(low), 2)
    own_kv = jnp.concatenate([own_kv[:, :heads_wide], own_kv[:, heads_wide:]], axis=0)
    own_mid = jnp.concatenate(
        [w_attn_out.astype(low).T, w_cross_q.astype(low), w_cross_out.astype(low).T, own_kv], axis=1
    )
    mid_all = lax.all_gather(after(own_mid, qkv_all), "dp", axis=0, tiled=True)
    own_mlp = jnp.concatenate([w_gate.astype(low), w_up.astype(low)], axis=1)
    mlp_all = lax.all_gather(after(own_mlp, mid_all), "dp", axis=0, tiled=True)
    down_all = lax.all_gather(after(w_down.astype(low).T, mlp_all), "dp", axis=0, tiled=True)
    attn_out_t, cross_q, cross_out_t = (mid_all[:, part * heads_wide : (part + 1) * heads_wide] for part in range(3))
    model = mid_all.shape[0]
    cross_kv = (
        mid_all[:, 3 * heads_wide :]
        .reshape(lax.axis_size("dp"), 2, -1, heads_wide)
        .transpose(0, 2, 1, 3)
        .reshape(model // 2, 2 * heads_wide)
    )

    tables = turn_tables(group_positions(latents.shape[0]))
    packed = dot_plain(rows_one, qkv_all)
    attended, rotated, logs = attend(pad_heads(packed, 3), tables)
    attended = attended[:, :heads_wide]
    resid_one = resid_in + sum_rows(dot_cols(attended, attn_out_t))
    normed_two, scaled_two, inverse_two = layer_norm(resid_one, gain_cross)
    rows_two = spread_rows(normed_two.astype(low))
    head_shape = (-1, heads_wide // DH, DH)
    cross_query = dot_plain(rows_two, cross_q).astype(low).reshape(head_shape)
    context = conditioning.reshape(CTX, conditioning.shape[2])
    cross_pack = dot_plain(context, cross_kv).astype(low)
    cross_key = cross_pack[:, :heads_wide].reshape(head_shape)
    cross_value = cross_pack[:, heads_wide:].reshape(head_shape)
    crossed, cross_logs = cross_forward(cross_query, cross_key, cross_value)
    crossed = crossed.reshape(-1, heads_wide).astype(low)
    resid_two = resid_one + sum_rows(dot_cols(crossed, cross_out_t))
    normed_three, scaled_three, inverse_three = layer_norm(resid_two, gain_mlp)
    rows_three = spread_rows(normed_three.astype(low))
    mlp_seed = spread_rows(cotangent)
    both = dot_plain(rows_three, mlp_all)
    gate_pre, up_pre = both[:, :hidden_wide], both[:, hidden_wide:]
    sigma_gate = jax.nn.sigmoid(gate_pre)
    swish = gate_pre * sigma_gate
    hidden = (swish * up_pre).astype(low)
    sum_down = dp_sum(dot_rows(mlp_seed, hidden))
    d_hidden = dot_plain(mlp_seed, down_all)
    d_gate = (d_hidden * up_pre * sigma_gate * (1.0 + gate_pre * (1.0 - sigma_gate))).astype(low)
    d_up = (d_hidden * swish).astype(low)
    d_both = jnp.concatenate([d_gate, d_up], axis=1)
    sum_mlp = dp_sum(after(dot_rows(rows_three, d_both), sum_down))
    d_normed = sum_rows(dot_cols(d_both, mlp_all))
    d_part, gain_grad_three = norm_backward(d_normed, scaled_three, inverse_three, gain_mlp)
    d_resid = cotangent.astype(jnp.float32) + d_part
    block_out = resid_two + sum_rows(dot_cols(hidden, down_all))
    cross_seed = spread_rows(d_resid.astype(low))
    grad_cross_out = dot_rows(cross_seed, crossed)
    d_crossed = dot_plain(cross_seed, cross_out_t).astype(low).reshape(head_shape)
    d_query, d_key, d_value = cross_backward(cross_query, cross_key, cross_value, d_crossed, cross_logs)
    d_query = d_query.reshape(-1, heads_wide).astype(low)
    d_keyval = jnp.concatenate([d_key.reshape(CTX, -1), d_value.reshape(CTX, -1)], axis=1).astype(low)
    grad_cross_q = dot_rows(rows_two, d_query)
    grad_cross_kv = dot_rows(context, d_keyval)
    context_part = dot_cols(d_keyval, cross_kv)
    d_normed = sum_rows(dot_cols(d_query, cross_q))
    d_part, gain_grad_two = norm_backward(d_normed, scaled_two, inverse_two, gain_cross)
    d_resid = d_resid + d_part
    self_seed = spread_rows(d_resid.astype(low))
    grad_attn_out = dot_rows(self_seed, attended)
    grad_kv = (
        grad_cross_kv.astype(low)
        .reshape(lax.axis_size("dp"), -1, 2, heads_wide)
        .transpose(0, 2, 1, 3)
        .reshape(model, heads_wide)
    )
    grad_mid = jnp.concatenate([grad_attn_out.astype(low), grad_cross_q.astype(low), grad_cross_out.astype(low), grad_kv], axis=1)
    sum_mid = dp_sum(after(grad_mid, sum_mlp))
    d_attended = dot_plain(self_seed, attn_out_t).astype(low)
    d_packed = drop_heads(attend_back(rotated, pad_heads(d_attended, 1), logs, tables), 3, packed.shape[1])
    sum_qkv = dp_sum(after(dot_rows(rows_one, d_packed), sum_mid))
    d_normed = sum_rows(dot_cols(d_packed, qkv_all))
    d_part, gain_grad_one = norm_backward(d_normed, scaled_one, inverse_one, gain_attn)
    grad_latents = d_resid + d_part
    grad_context = (
        lax.psum(context_part.astype(low), "tensor").astype(jnp.float32).reshape(conditioning.shape)
    )
    gains = lax.psum(jnp.stack([gain_grad_one, gain_grad_two, gain_grad_three]), ("dp", "tensor"))
    sums = [sum_mid[:, part * heads_wide : (part + 1) * heads_wide].astype(jnp.float32) for part in range(4)]
    half = sums[3].shape[0] // 2
    sum_kv = jnp.concatenate([sums[3][:half], sums[3][half:]], axis=1)
    return (
        block_out,
        grad_latents,
        grad_context,
        gains[0],
        by_head(sum_qkv, 3).astype(jnp.float32),
        sums[0].T,
        gains[1],
        sums[1],
        by_head(sum_kv, 2),
        sums[2].T,
        gains[2],
        sum_mlp[:, :hidden_wide].astype(jnp.float32),
        sum_mlp[:, hidden_wide:].astype(jnp.float32),
        sum_down.astype(jnp.float32).T,
    )


def solution(mesh):
    in_specs = (
        P(("dp", "tensor"), None),
        P("dp", None, None),
        P(),
        P("dp", "tensor"),
        P("tensor", "dp"),
        P(),
        P("dp", "tensor"),
        P("dp", "tensor"),
        P("tensor", "dp"),
        P(),
        P("dp", "tensor"),
        P("dp", "tensor"),
        P("tensor", "dp"),
        P(("dp", "tensor"), None),
    )
    out_specs = (
        P(("dp", "tensor"), None),
        P(("dp", "tensor"), None),
        P("dp", None, None),
        P(),
        P("dp", "tensor"),
        P("tensor", "dp"),
        P(),
        P("dp", "tensor"),
        P("dp", "tensor"),
        P("tensor", "dp"),
        P(),
        P("dp", "tensor"),
        P("dp", "tensor"),
        P("tensor", "dp"),
    )
    return jax.shard_map(
        per_device, mesh=mesh, in_specs=in_specs, out_specs=out_specs, check_vma=False
    )
```

time: 1540 us -> 777 us (0.50)
  waiting for transfers between devices: 1110 us -> 370 us
  matrix products: 214 us -> 123 us
  starting transfers between devices: 2.57 us -> 59.1 us
  Pallas kernels: 0 us -> 47.7 us
  other arithmetic: 81.9 us -> 44.6 us
    reduce_scatter x13 -> x3, waiting for transfers between devices: 582 us -> 35.9 us  [dp_sum(): lax.psum_scatter(grads.astype(jnp.bfloat16), 'dp', scatter_dimension=0, t...]
    all_gather x14 -> x4, waiting for transfers between devices: 453 us -> 91.4 us  [the longest x1 50.1 us: per_device(): mid_all = lax.all_gather(after(own_mid, qkv_all), 'dp', axis=0, tiled=True)]
    ppermute x0 -> x48, waiting for transfers between devices: none -> 203 us  [swap(): lax.ppermute(values, 'tensor', [(member, member ^ bit) for member in rang...]
    ppermute x0 -> x48, starting transfers between devices: none -> 58.1 us  [swap(): lax.ppermute(values, 'tensor', [(member, member ^ bit) for member in rang...]
    dot_general x20 -> x6, matrix products: 61 us -> 4.51 us  [the longest x1 0.97 us: cross_backward(): jnp.einsum('qhd,khd->hqk', d_output, values_in, preferred_element_type=jn...]
    pallas_call x0 -> x2, Pallas kernels: none -> 47.7 us  [the longest x1 28.3 us: attend_back(): pl.pallas_call(attend_back_kernel, grid=(pairs,), in_specs=[column_block(...]
    convert_element_type x24 -> x4, other arithmetic: 50.1 us -> 4.14 us  [the longest x1 1.68 us: per_device(): sum_mlp[:, hidden_wide:].astype(jnp.float32)]
    dynamic_update_slice x4 -> x0, local copies, waits for them, and re-layouts: 31.6 us -> none  [one_sequence(): outputs, log_totals = lax.map(one_block, blocks)]
  transfers between devices with their start and end apart: 29 -> 57, of which waited for: 25 -> 33; matrix products, arithmetic and copies ran while one was open for 18% -> 24% of each run, Pallas kernels for 0% -> 6%
where the time goes in v1:
time: 777 us; the launch traced here: 768 us
  waiting for transfers between devices  370 us (48%)
  matrix products  123 us (16%)
  local copies, waits for them, and re-layouts  66.3 us (9%)
  starting transfers between devices  59.1 us (8%)
  Pallas kernels  47.7 us (6%)
  other arithmetic  44.6 us (6%)
  blocking collectives  41.9 us (5%)
  between operations  15.8 us (2%)
    ppermute x48, waiting for transfers between devices, swap(): lax.ppermute(values, 'tensor', [(member, member ^ bit) for member in rang...  203 us
    ppermute x48, starting transfers between devices, swap(): lax.ppermute(values, 'tensor', [(member, member ^ bit) for member in rang...  58.1 us
    all_gather x1, waiting for transfers between devices, per_device(): mid_all = lax.all_gather(after(own_mid, qkv_all), 'dp', axis=0, tiled=True)  50.1 us
    dot_general x7, matrix products, dot_plain(): return jnp.dot(left_op, right_op, preferred_element_type=jnp.float32)  41.9 us
    psum x1, blocking collectives, per_device(): lax.psum(jnp.stack([gain_grad_one, gain_grad_two, gain_grad_three]), ('dp...  41.9 us
    all_gather x1, waiting for transfers between devices, per_device(): qkv_all = lax.all_gather(own_qkv, 'dp', axis=0, tiled=True)  41.3 us
    dot_general x7, matrix products, dot_cols(): lax.dot_general(left_op, right_op, (((1,), (1,)), ((), ())), preferred_el...  40.2 us
    unnamed x167, local copies, waits for them, and re-layouts  38.4 us
  transfers between devices with their start and end apart: 57, of which 33 were waited for; matrix products, arithmetic and copies ran while one was open for 24% of the time, Pallas kernels for 6%

profile of v1, /device:TPU:0, one launch (start us, length us, event | category | flops | bytes accessed | tf_op | source)
XLA Modules:
  0.0 768.5 jit_solution(4938666672755143964)
XLA Ops:
  13.2 41.3 %all-gather.5.cloned.1.call-done = bf16[1536,1152]{1,0:T(8,128)(2,1)} async-done(((bf16[192,1152]{1,0:T(8,128)(2,1)}), bf16[1536,1152]{1,0:T(8,128)(2,1)}) %all-gather.5.cloned.1.call-update) | async-done | bytes 3538960 | tf_op jit(solution)/shard_map/all_gather | solution.py:334
  57.3 50.1 %all-gather.7.cloned.1.call-done = bf16[1536,1536]{1,0:T(8,128)(2,1)} async-done(((bf16[192,1536]{1,0:T(8,128)(2,1)}), bf16[1536,1536]{1,0:T(8,128)(2,1)}) %all-gather.7.cloned.1.call-update) | async-done | bytes 4718608 | tf_op jit(solution)/shard_map/all_gather | solution.py:340
  117.4 12.1 %collective-permute-done.1 = bf16[256,1536]{1,0:T(8,128)(2,1)} collective-permute-done((bf16[256,1536]{1,0:T(8,128)(2,1)}, bf16[256,1536]{1,0:T(8,128)(2,1)}, u32[]{:S(2)}, u32[]{:S(2)}) %collective-permute-start.1) | collective-permute-done | bytes 786464 | tf_op jit(solution)/shard_map/ppermute | solution.py:217
  151.1 19.3 %shard_map.245 = (bf16[1024,384]{1,0:T(8,128)(2,1)S(1)}, bf16[1024,1152]{1,0:T(8,128)(2,1)}, f32[1024,384]{1,0:T(8,128)S(1)}) custom-call(f32[1024,1152]{1,0:T(8,128)} %fusion.92.q_ref.k_ref.v_ref, f32[1024,1152]{1,0:T(8,128)} %fusion.92.q_ref.k_ref.v_ref, f32[1024,1152]{1,0:T(8,128)} %fusion.92.q_ref.k_ref.v_ref, f32[1024,128]{1,0:T(8,128)S(1)} %concatenate.114.cos_ref, ...), custom_call_target="tpu_custom_call" | custom-call | flops 12884901888 | bytes 16777216 | tf_op jit(solution)/shard_map/pallas_call | solution.py:127
  174.5 7.3 collective-permute-done.6
  185.5 13.7 %collective-permute-done.7 = bf16[256,1536]{1,0:T(8,128)(2,1)S(1)} collective-permute-done((bf16[256,1536]{1,0:T(8,128)(2,1)S(1)}, bf16[256,1536]{1,0:T(8,128)(2,1)S(1)}, u32[]{:S(2)}, u32[]{:S(2)}) %collective-permute-start.7) | collective-permute-done | bytes 786464 | tf_op jit(solution)/shard_map/ppermute | solution.py:217
  210.7 8.9 %collective-permute-done.9 = bf16[256,1536]{1,0:T(8,128)(2,1)} collective-permute-done((bf16[256,1536]{1,0:T(8,128)(2,1)}, bf16[256,1536]{1,0:T(8,128)(2,1)}, u32[]{:S(2)}, u32[]{:S(2)}) %collective-permute-start.9) | collective-permute-done | bytes 786464 | tf_op jit(solution)/shard_map/ppermute | solution.py:217
  252.0 8.0 %collective-permute-done.14 = bf16[128,1536]{1,0:T(8,128)(2,1)S(1)} collective-permute-done((bf16[128,1536]{1,0:T(8,128)(2,1)S(1)}, bf16[128,1536]{1,0:T(8,128)(2,1)S(1)}, u32[]{:S(2)}, u32[]{:S(2)}) %collective-permute-start.14) | collective-permute-done | bytes 393248 | tf_op jit(solution)/shard_map/ppermute | solution.py:217
  265.3 11.5 %collective-permute-done.24 = bf16[256,1536]{1,0:T(8,128)(2,1)S(1)} collective-permute-done((bf16[256,1536]{1,0:T(8,128)(2,1)S(1)}, bf16[256,1536]{1,0:T(8,128)(2,1)S(1)}, u32[]{:S(2)}, u32[]{:S(2)}) %collective-permute-start.24) | collective-permute-done | bytes 786464 | tf_op jit(solution)/shard_map/ppermute | solution.py:217
  279.8 14.6 %collective-permute-done.15 = bf16[256,1536]{1,0:T(8,128)(2,1)S(1)} collective-permute-done((bf16[256,1536]{1,0:T(8,128)(2,1)S(1)}, bf16[256,1536]{1,0:T(8,128)(2,1)S(1)}, u32[]{:S(2)}, u32[]{:S(2)}) %collective-permute-start.15) | collective-permute-done | bytes 786464 | tf_op jit(solution)/shard_map/ppermute | solution.py:217
  303.0 12.1 %collective-permute-done.17 = bf16[256,1536]{1,0:T(8,128)(2,1)S(1)} collective-permute-done((bf16[256,1536]{1,0:T(8,128)(2,1)S(1)}, bf16[256,1536]{1,0:T(8,128)(2,1)S(1)}, u32[]{:S(2)}, u32[]{:S(2)}) %collective-permute-start.17) | collective-permute-done | bytes 786464 | tf_op jit(solution)/shard_map/ppermute | solution.py:217
  318.8 7.1 collective-permute-done.18
  327.7 12.3 %fusion.93 = f32[1024,3072]{1,0:T(8,128)} fusion(bf16[1024,1536]{1,0:T(8,128)(2,1)S(1)} %constant_dynamic-update-slice_fusion.10, bf16[1536,3072]{1,0:T(8,128)(2,1)S(1)} %bitcast.145), kind=kOutput, calls=%fused_computation.224 | convolution fusion | flops 9663676416 | bytes 25165824 | tf_op jit(solution)/shard_map/dot_general | solution.py:185
  340.1 14.2 %multiply_convert_fusion.1 = (bf16[1024,1536]{1,0:T(8,128)(2,1)}, bf16[1024,1536]{1,0:T(8,128)(2,1)}, bf16[1024,1536]{1,0:T(8,128)(2,1)S(1)}) fusion(f32[1024,3072]{1,0:T(8,128)} %fusion.93, bf16[1024,1536]{1,0:T(8,128)(2,1)} %copy-done.37, bf16[1536,1536]{1,0:T(8,128)(2,1)} %all-gather.11.cloned.1.call-done), kind=kOutput, calls=%fused_computation.3 | convolution fusion | flops 4855431168 | bytes 29884416 | tf_op jit(solution)/shard_map/dot_general | solution.py:185
  356.1 7.1 convolution_convert_fusion
  363.7 16.1 %fusion.1 = bf16[1536,3072]{1,0:T(8,128)(2,1)} fusion(bf16[1024,1536]{1,0:T(8,128)(2,1)} %copy-done.42, bf16[1024,1536]{1,0:T(8,128)(2,1)} %get-tuple-element.134, bf16[1024,1536]{1,0:T(8,128)(2,1)} %get-tuple-element.133), kind=kOutput, calls=%fused_computation.8 | convolution fusion | flops 9676259328 | bytes 18874368 | tf_op jit(solution)/shard_map/dot_general | solution.py:189
  379.8 35.9 %reduce-scatter.7.cloned.1.call-done = bf16[192,1536]{1,0:T(8,128)(2,1)} async-done(((bf16[1536,1536]{1,0:T(8,128)(2,1)}), bf16[192,1536]{1,0:T(8,128)(2,1)}) %reduce-scatter.7.cloned.1.call-update) | async-done | bytes 589840 | tf_op jit(solution)/shard_map/reduce_scatter | solution.py:304
  415.7 15.2 %fusion.88 = (bf16[1024,1536]{1,0:T(8,128)(2,1)}, f32[1024,1536]{1,0:T(8,128)S(1)}) fusion(bf16[1536,3072]{1,0:T(8,128)(2,1)} %all-gather.9.cloned.1.call-done, bf16[1024,1536]{1,0:T(8,128)(2,1)} %get-tuple-element.134, bf16[1024,1536]{1,0:T(8,128)(2,1)} %get-tuple-element.133), kind=kOutput, calls=%fused_computation.219 | convolution fusion | flops 9677832192 | bytes 25165824 | tf_op jit(solution)/shard_map/dot_general | solution.py:195
  435.4 7.2 fusion.89
  447.3 7.5 collective-permute-done.22
  457.9 14.3 %collective-permute-done.31 = bf16[256,1536]{1,0:T(8,128)(2,1)S(1)} collective-permute-done((bf16[256,1536]{1,0:T(8,128)(2,1)S(1)}, bf16[256,1536]{1,0:T(8,128)(2,1)S(1)}, u32[]{:S(2)}, u32[]{:S(2)}) %collective-permute-start.31) | collective-permute-done | bytes 786464 | tf_op jit(solution)/shard_map/ppermute | solution.py:217
  472.2 12.6 %collective-permute-done.23 = bf16[256,1536]{1,0:T(8,128)(2,1)S(1)} collective-permute-done((bf16[256,1536]{1,0:T(8,128)(2,1)S(1)}, bf16[256,1536]{1,0:T(8,128)(2,1)S(1)}, u32[]{:S(2)}, u32[]{:S(2)}) %collective-permute-start.23) | collective-permute-done | bytes 786464 | tf_op jit(solution)/shard_map/ppermute | solution.py:217
  490.9 14.0 %collective-permute-done.33 = bf16[256,1536]{1,0:T(8,128)(2,1)S(1)} collective-permute-done((bf16[256,1536]{1,0:T(8,128)(2,1)S(1)}, bf16[256,1536]{1,0:T(8,128)(2,1)S(1)}, u32[]{:S(2)}, u32[]{:S(2)}) %collective-permute-start.33) | collective-permute-done | bytes 786464 | tf_op jit(solution)/shard_map/ppermute | solution.py:217
  509.4 7.6 collective-permute-done.34
  525.8 8.0 %collective-permute-done.38 = bf16[128,1536]{1,0:T(8,128)(2,1)S(1)} collective-permute-done((bf16[128,1536]{1,0:T(8,128)(2,1)S(1)}, bf16[128,1536]{1,0:T(8,128)(2,1)S(1)}, u32[]{:S(2)}, u32[]{:S(2)}) %collective-permute-start.38) | collective-permute-done | bytes 393248 | tf_op jit(solution)/shard_map/ppermute | solution.py:217
  564.2 11.3 %collective-permute-done.41 = bf16[256,1536]{1,0:T(8,128)(2,1)S(1)} collective-permute-done((bf16[256,1536]{1,0:T(8,128)(2,1)S(1)}, bf16[256,1536]{1,0:T(8,128)(2,1)S(1)}, u32[]{:S(2)}, u32[]{:S(2)}) %collective-permute-start.41) | collective-permute-done | bytes 786464 | tf_op jit(solution)/shard_map/ppermute | solution.py:217
  601.8 28.3 %shard_map.246 = bf16[1024,1152]{1,0:T(8,128)(2,1)} custom-call(bf16[1024,1152]{1,0:T(8,128)(2,1)} %get-tuple-element.27.q_ref.k_ref.v_ref, bf16[1024,1152]{1,0:T(8,128)(2,1)} %get-tuple-element.27.q_ref.k_ref.v_ref, bf16[1024,1152]{1,0:T(8,128)(2,1)} %get-tuple-element.27.q_ref.k_ref.v_ref, bf16[1024,384]{1,0:T(8,128)(2,1)S(1)} %convolution_convert_fusion.5.grad_ref, ...), custom_call_target="tpu_custom_call" | custom-call | flops 25769803776 | bytes 16777216 | tf_op jit(solution)/shard_map/pallas_call | solution.py:147
  630.2 7.4 fusion.94
  637.6 17.0 %reduce-scatter.13.cloned.1.call-done = bf16[192,1536]{1,0:T(8,128)(2,1)} async-done(((bf16[1536,1536]{1,0:T(8,128)(2,1)}), bf16[192,1536]{1,0:T(8,128)(2,1)}) %reduce-scatter.13.cloned.1.call-update) | async-done | bytes 589840
  666.3 7.1 collective-permute-done.46
  677.5 22.9 %all-reduce.2.cloned.1.call-done = bf16[1,130,768]{2,1,0:T(8,128)(2,1)} async-done(((bf16[1,130,768]{2,1,0:T(8,128)(2,1)}), bf16[1,130,768]{2,1,0:T(8,128)(2,1)}) %all-reduce.2.cloned.1.call-update) | async-done | bytes 199696 | tf_op jit(solution)/shard_map/psum | solution.py:416
  706.3 41.9 %psum.15 = f32[3,1536]{1,0:T(4,128)S(1)} all-reduce(f32[3,1536]{1,0:T(4,128)S(1)} %pad_maximum_fusion.22), channel_id=1, replica_groups=mesh['dp'=8,'tensor'=4] {'dp','tensor'}, use_global_device_ids=true, to_apply=%region_19.0 | all-reduce | flops 4608 | bytes 36864 | tf_op jit(solution)/shard_map/psum | solution.py:418
  (410 shorter events, 238.4 us)
Async XLA Ops:
  7.2 47.3 %all-gather.5.cloned.1.call-start = ((), (), s32[]{:S(2)}) async-start(), calls=%async_computation.4 | async-start | bytes 3981312 | tf_op jit(solution)/shard_map/all_gather | solution.py:334
  9.8 97.5 %all-gather.7.cloned.1.call-start = ((), (), s32[]{:S(2)}) async-start(), calls=%async_computation.5 | async-start | bytes 5308416 | tf_op jit(solution)/shard_map/all_gather | solution.py:340
  54.6 191.5 %all-gather.9.cloned.1.call-start = ((), (), s32[]{:S(2)}) async-start(), calls=%async_computation.6 | async-start | bytes 10616832 | tf_op jit(solution)/shard_map/all_gather | solution.py:342
  107.4 232.7 %all-gather.11.cloned.1.call-start = ((), (), s32[]{:S(2)}) async-start(), calls=%async_computation.7 | async-start | bytes 5308416 | tf_op jit(solution)/shard_map/all_gather | solution.py:343
  109.5 20.0 %collective-permute-start.1 = (bf16[256,1536]{1,0:T(8,128)(2,1)}, bf16[256,1536]{1,0:T(8,128)(2,1)}, u32[]{:S(2)}, u32[]{:S(2)}) collective-permute-start(bf16[256,1536]{1,0:T(8,128)(2,1)} %get-tuple-element.132), channel_id=1, source_target_pairs={{0,2},{1,3},{2,0},{3,1},{4,6},{5,7},{6,4},{7,5},{8,10},{9,11},{10,... | collective-permute-start | bytes 2359304 | tf_op jit(solution)/shard_map/ppermute | solution.py:217
  111.0 21.1 %collective-permute-start = (bf16[256,1536]{1,0:T(8,128)(2,1)}, bf16[256,1536]{1,0:T(8,128)(2,1)}, u32[]{:S(2)}, u32[]{:S(2)}) collective-permute-start(bf16[256,1536]{1,0:T(8,128)(2,1)} %get-tuple-element.132), channel_id=1, source_target_pairs={{0,1},{1,0},{2,3},{3,2},{4,5},{5,4},{6,7},{7,6},{8,9},{9,8},{10,11... | collective-permute-start | bytes 2359304 | tf_op jit(solution)/shard_map/ppermute | solution.py:217
  182.4 16.8 %collective-permute-start.7 = (bf16[256,1536]{1,0:T(8,128)(2,1)S(1)}, bf16[256,1536]{1,0:T(8,128)(2,1)S(1)}, u32[]{:S(2)}, u32[]{:S(2)}) collective-permute-start(bf16[256,1536]{1,0:T(8,128)(2,1)S(1)} %pad_maximum_fusion.6), channel_id=1, source_target_pairs={{0,2},{1,3},{2,0},{3,1},{4,6},{5,7},{6,4},{7,5},{8,10},{9,11},{10,... | collective-permute-start | bytes 2359304 | tf_op jit(solution)/shard_map/ppermute | solution.py:217
  184.1 16.5 %collective-permute-start.5 = (bf16[256,1536]{1,0:T(8,128)(2,1)S(1)}, bf16[256,1536]{1,0:T(8,128)(2,1)S(1)}, u32[]{:S(2)}, u32[]{:S(2)}) collective-permute-start(bf16[256,1536]{1,0:T(8,128)(2,1)S(1)} %pad_maximum_fusion.5), channel_id=1, source_target_pairs={{0,1},{1,0},{2,3},{3,2},{4,5},{5,4},{6,7},{7,6},{8,9},{9,8},{10,11... | collective-permute-start | bytes 2359304 | tf_op jit(solution)/shard_map/ppermute | solution.py:217
  204.3 17.8 %collective-permute-start.8 = (bf16[256,1536]{1,0:T(8,128)(2,1)}, bf16[256,1536]{1,0:T(8,128)(2,1)}, u32[]{:S(2)}, u32[]{:S(2)}) collective-permute-start(bf16[256,1536]{1,0:T(8,128)(2,1)} %get-tuple-element.128), channel_id=1, source_target_pairs={{0,1},{1,0},{2,3},{3,2},{4,5},{5,4},{6,7},{7,6},{8,9},{9,8},{10,11... | collective-permute-start | bytes 2359304 | tf_op jit(solution)/shard_map/ppermute | solution.py:217
  246.1 169.5 %reduce-scatter.7.cloned.1.call-start = ((), (), s32[]{:S(2)}) async-start(), calls=%async_computation.9 | async-start | bytes 5308416 | tf_op jit(solution)/shard_map/reduce_scatter | solution.py:304
  250.7 26.1 %collective-permute-start.24 = (bf16[256,1536]{1,0:T(8,128)(2,1)S(1)}, bf16[256,1536]{1,0:T(8,128)(2,1)S(1)}, u32[]{:S(2)}, u32[]{:S(2)}) collective-permute-start(bf16[256,1536]{1,0:T(8,128)(2,1)S(1)} %copy-done.23), channel_id=1, source_target_pairs={{0,1},{1,0},{2,3},{3,2},{4,5},{5,4},{6,7},{7,6},{8,9},{9,8},{10,11... | collective-permute-start | bytes 2359304 | tf_op jit(solution)/shard_map/ppermute | solution.py:217
  251.3 27.0 %collective-permute-start.25 = (bf16[256,1536]{1,0:T(8,128)(2,1)S(1)}, bf16[256,1536]{1,0:T(8,128)(2,1)S(1)}, u32[]{:S(2)}, u32[]{:S(2)}) collective-permute-start(bf16[256,1536]{1,0:T(8,128)(2,1)S(1)} %copy-done.23), channel_id=1, source_target_pairs={{0,2},{1,3},{2,0},{3,1},{4,6},{5,7},{6,4},{7,5},{8,10},{9,11},{10,... | collective-permute-start | bytes 2359304 | tf_op jit(solution)/shard_map/ppermute | solution.py:217
  262.4 32.0 %collective-permute-start.15 = (bf16[256,1536]{1,0:T(8,128)(2,1)S(1)}, bf16[256,1536]{1,0:T(8,128)(2,1)S(1)}, u32[]{:S(2)}, u32[]{:S(2)}) collective-permute-start(bf16[256,1536]{1,0:T(8,128)(2,1)S(1)} %pad_maximum_fusion.8), channel_id=1, source_target_pairs={{0,2},{1,3},{2,0},{3,1},{4,6},{5,7},{6,4},{7,5},{8,10},{9,11},{10,... | collective-permute-start | bytes 2359304 | tf_op jit(solution)/shard_map/ppermute | solution.py:217
  264.6 29.9 %collective-permute-start.13 = (bf16[256,1536]{1,0:T(8,128)(2,1)S(1)}, bf16[256,1536]{1,0:T(8,128)(2,1)S(1)}, u32[]{:S(2)}, u32[]{:S(2)}) collective-permute-start(bf16[256,1536]{1,0:T(8,128)(2,1)S(1)} %pad_maximum_fusion.7), channel_id=1, source_target_pairs={{0,1},{1,0},{2,3},{3,2},{4,5},{5,4},{6,7},{7,6},{8,9},{9,8},{10,11... | collective-permute-start | bytes 2359304 | tf_op jit(solution)/shard_map/ppermute | solution.py:217
  276.9 26.0 %collective-permute-start.26 = (bf16[128,1536]{1,0:T(8,128)(2,1)S(1)}, bf16[128,1536]{1,0:T(8,128)(2,1)S(1)}, u32[]{:S(2)}, u32[]{:S(2)}) collective-permute-start(bf16[128,1536]{1,0:T(8,128)(2,1)S(1)} %slice.415), channel_id=1, source_target_pairs={{0,2},{1,3},{2,0},{3,1},{4,6},{5,7},{6,4},{7,5},{8,10},{9,11},{10,... | collective-permute-start | bytes 1179656 | tf_op jit(solution)/shard_map/ppermute | solution.py:217
  278.4 24.5 %collective-permute-start.27 = (bf16[128,1536]{1,0:T(8,128)(2,1)S(1)}, bf16[128,1536]{1,0:T(8,128)(2,1)S(1)}, u32[]{:S(2)}, u32[]{:S(2)}) collective-permute-start(bf16[128,1536]{1,0:T(8,128)(2,1)S(1)} %slice.416), channel_id=1, source_target_pairs={{0,1},{1,0},{2,3},{3,2},{4,5},{5,4},{6,7},{7,6},{8,9},{9,8},{10,11... | collective-permute-start | bytes 1179656 | tf_op jit(solution)/shard_map/ppermute | solution.py:217
  297.1 18.0 %collective-permute-start.17 = (bf16[256,1536]{1,0:T(8,128)(2,1)S(1)}, bf16[256,1536]{1,0:T(8,128)(2,1)S(1)}, u32[]{:S(2)}, u32[]{:S(2)}) collective-permute-start(bf16[256,1536]{1,0:T(8,128)(2,1)S(1)} %get-tuple-element.124), channel_id=1, source_target_pairs={{0,2},{1,3},{2,0},{3,1},{4,6},{5,7},{6,4},{7,5},{8,10},{9,11},{10,... | collective-permute-start | bytes 2359304 | tf_op jit(solution)/shard_map/ppermute | solution.py:217
  299.2 18.9 %collective-permute-start.16 = (bf16[256,1536]{1,0:T(8,128)(2,1)S(1)}, bf16[256,1536]{1,0:T(8,128)(2,1)S(1)}, u32[]{:S(2)}, u32[]{:S(2)}) collective-permute-start(bf16[256,1536]{1,0:T(8,128)(2,1)S(1)} %get-tuple-element.124), channel_id=1, source_target_pairs={{0,1},{1,0},{2,3},{3,2},{4,5},{5,4},{6,7},{7,6},{8,9},{9,8},{10,11... | collective-permute-start | bytes 2359304 | tf_op jit(solution)/shard_map/ppermute | solution.py:217
  363.2 225.2 %reduce-scatter.9.cloned.1.call-start = ((), (), s32[]{:S(2)}) async-start(), calls=%async_computation.10 | async-start | bytes 10616832 | tf_op jit(solution)/shard_map/reduce_scatter | solution.py:304
  415.6 239.0 %reduce-scatter.13.cloned.1.call-start = ((), (), s32[]{:S(2)}) async-start(), calls=%async_computation.12 | async-start | bytes 5308416
  444.2 28.1 %collective-permute-start.31 = (bf16[256,1536]{1,0:T(8,128)(2,1)S(1)}, bf16[256,1536]{1,0:T(8,128)(2,1)S(1)}, u32[]{:S(2)}, u32[]{:S(2)}) collective-permute-start(bf16[256,1536]{1,0:T(8,128)(2,1)S(1)} %pad_maximum_fusion.12), channel_id=1, source_target_pairs={{0,2},{1,3},{2,0},{3,1},{4,6},{5,7},{6,4},{7,5},{8,10},{9,11},{10,... | collective-permute-start | bytes 2359304 | tf_op jit(solution)/shard_map/ppermute | solution.py:217
  445.7 26.5 %collective-permute-start.29 = (bf16[256,1536]{1,0:T(8,128)(2,1)S(1)}, bf16[256,1536]{1,0:T(8,128)(2,1)S(1)}, u32[]{:S(2)}, u32[]{:S(2)}) collective-permute-start(bf16[256,1536]{1,0:T(8,128)(2,1)S(1)} %pad_maximum_fusion.11), channel_id=1, source_target_pairs={{0,1},{1,0},{2,3},{3,2},{4,5},{5,4},{6,7},{7,6},{8,9},{9,8},{10,11... | collective-permute-start | bytes 2359304 | tf_op jit(solution)/shard_map/ppermute | solution.py:217
  455.7 29.2 %collective-permute-start.23 = (bf16[256,1536]{1,0:T(8,128)(2,1)S(1)}, bf16[256,1536]{1,0:T(8,128)(2,1)S(1)}, u32[]{:S(2)}, u32[]{:S(2)}) collective-permute-start(bf16[256,1536]{1,0:T(8,128)(2,1)S(1)} %pad_maximum_fusion.10), channel_id=1, source_target_pairs={{0,2},{1,3},{2,0},{3,1},{4,6},{5,7},{6,4},{7,5},{8,10},{9,11},{10,... | collective-permute-start | bytes 2359304 | tf_op jit(solution)/shard_map/ppermute | solution.py:217
  456.4 28.5 %collective-permute-start.21 = (bf16[256,1536]{1,0:T(8,128)(2,1)S(1)}, bf16[256,1536]{1,0:T(8,128)(2,1)S(1)}, u32[]{:S(2)}, u32[]{:S(2)}) collective-permute-start(bf16[256,1536]{1,0:T(8,128)(2,1)S(1)} %pad_maximum_fusion.9), channel_id=1, source_target_pairs={{0,1},{1,0},{2,3},{3,2},{4,5},{5,4},{6,7},{7,6},{8,9},{9,8},{10,11... | collective-permute-start | bytes 2359304 | tf_op jit(solution)/shard_map/ppermute | solution.py:217
  488.8 16.0 %collective-permute-start.33 = (bf16[256,1536]{1,0:T(8,128)(2,1)S(1)}, bf16[256,1536]{1,0:T(8,128)(2,1)S(1)}, u32[]{:S(2)}, u32[]{:S(2)}) collective-permute-start(bf16[256,1536]{1,0:T(8,128)(2,1)S(1)} %get-tuple-element.120), channel_id=1, source_target_pairs={{0,2},{1,3},{2,0},{3,1},{4,6},{5,7},{6,4},{7,5},{8,10},{9,11},{10,... | collective-permute-start | bytes 2359304 | tf_op jit(solution)/shard_map/ppermute | solution.py:217
  490.0 19.2 %collective-permute-start.32 = (bf16[256,1536]{1,0:T(8,128)(2,1)S(1)}, bf16[256,1536]{1,0:T(8,128)(2,1)S(1)}, u32[]{:S(2)}, u32[]{:S(2)}) collective-permute-start(bf16[256,1536]{1,0:T(8,128)(2,1)S(1)} %get-tuple-element.120), channel_id=1, source_target_pairs={{0,1},{1,0},{2,3},{3,2},{4,5},{5,4},{6,7},{7,6},{8,9},{9,8},{10,11... | collective-permute-start | bytes 2359304 | tf_op jit(solution)/shard_map/ppermute | solution.py:217
  537.2 17.1 %collective-permute-start.39 = (bf16[256,1536]{1,0:T(8,128)(2,1)}, bf16[256,1536]{1,0:T(8,128)(2,1)}, u32[]{:S(2)}, u32[]{:S(2)}) collective-permute-start(bf16[256,1536]{1,0:T(8,128)(2,1)} %pad_maximum_fusion.14), channel_id=1, source_target_pairs={{0,2},{1,3},{2,0},{3,1},{4,6},{5,7},{6,4},{7,5},{8,10},{9,11},{10,... | collective-permute-start | bytes 2359304 | tf_op jit(solution)/shard_map/ppermute | solution.py:217
  559.3 16.1 %collective-permute-start.41 = (bf16[256,1536]{1,0:T(8,128)(2,1)S(1)}, bf16[256,1536]{1,0:T(8,128)(2,1)S(1)}, u32[]{:S(2)}, u32[]{:S(2)}) collective-permute-start(bf16[256,1536]{1,0:T(8,128)(2,1)S(1)} %get-tuple-element.116), channel_id=1, source_target_pairs={{0,2},{1,3},{2,0},{3,1},{4,6},{5,7},{6,4},{7,5},{8,10},{9,11},{10,... | collective-permute-start | bytes 2359304 | tf_op jit(solution)/shard_map/ppermute | solution.py:217
  595.1 105.3 %all-reduce.2.cloned.1.call-start = ((), (), s32[]{:S(2)}) async-start(), calls=%async_computation.8 | async-start | bytes 417792 | tf_op jit(solution)/shard_map/psum | solution.py:416
  597.7 161.1 %reduce-scatter.11.cloned.1.call-start = ((), (), s32[]{:S(2)}) async-start(), calls=%async_computation.11 | async-start | bytes 3981312 | tf_op jit(solution)/shard_map/reduce_scatter | solution.py:304
  674.7 27.7 %collective-permute-start.47 = (bf16[256,1536]{1,0:T(8,128)(2,1)}, bf16[256,1536]{1,0:T(8,128)(2,1)}, u32[]{:S(2)}, u32[]{:S(2)}) collective-permute-start(bf16[256,1536]{1,0:T(8,128)(2,1)} %pad_maximum_fusion.16), channel_id=1, source_target_pairs={{0,2},{1,3},{2,0},{3,1},{4,6},{5,7},{6,4},{7,5},{8,10},{9,11},{10,... | collective-permute-start | bytes 2359304 | tf_op jit(solution)/shard_map/ppermute | solution.py:217
  676.9 25.5 %collective-permute-start.45 = (bf16[256,1536]{1,0:T(8,128)(2,1)}, bf16[256,1536]{1,0:T(8,128)(2,1)}, u32[]{:S(2)}, u32[]{:S(2)}) collective-permute-start(bf16[256,1536]{1,0:T(8,128)(2,1)} %pad_maximum_fusion.15), channel_id=1, source_target_pairs={{0,1},{1,0},{2,3},{3,2},{4,5},{5,4},{6,7},{7,6},{8,9},{9,8},{10,11... | collective-permute-start | bytes 2359304 | tf_op jit(solution)/shard_map/ppermute | solution.py:217
  (93 other events, 1518.6 us)
Sparse Core Ops, SparseCore 0:
  10.3 44.2 all-gather.4
  56.7 50.5 all-gather.6
  109.6 89.5 all-gather.8
  246.2 50.3 all-gather.10
  363.3 52.2 reduce-scatter.6
  417.8 97.8 reduce-scatter.8
  595.2 59.3 reduce-scatter.12
  658.1 42.2 all-reduce.1
  702.9 45.0 reduce-scatter.10

commit v2 on v1

--- a/solution.py
+++ b/solution.py
@@ -1,3 +1,4 @@
+import math
 from functools import reduce
 
 import jax
@@ -12,7 +13,7 @@
 LENGTH = 1024
 PAIR = 2 * DH
 ROWS = 256
-VMEM_BYTES = 48 * 2**20
+VMEM_BYTES = 58 * 2**20
 
 norm_eps = 1e-05
 rope_base = 10000.0
@@ -308,7 +309,625 @@
     return lax.optimization_barrier((value, earlier))[0]
 
 
+MESH = pl.DeviceIdType.MESH
+BLOCK = LENGTH // 4
+HALF = BLOCK // 2
+FULL = 256
+
+
+class Links:
+    def __init__(self, send, recv, local):
+        self.send, self.recv, self.local = send, recv, local
+        self.used = self.used_local = 0
+        self.pending, self.pending_local = [], []
+        self.dp, self.tensor = lax.axis_index("dp"), lax.axis_index("tensor")
+
+    def remote(self, src, dst, dp_bit, tensor_bit):
+        at = self.used
+        self.used += 1
+        return pltpu.make_async_remote_copy(
+            src_ref=src,
+            dst_ref=dst,
+            send_sem=self.send.at[at],
+            recv_sem=self.recv.at[at],
+            device_id=(self.dp ^ dp_bit, self.tensor ^ tensor_bit),
+            device_id_type=MESH,
+        )
+
+    def go(self, src, dst, dp_bit, tensor_bit):
+        copy = self.remote(src, dst, dp_bit, tensor_bit)
+        copy.start()
+        self.pending.append(copy)
+        return copy
+
+    def store(self, src, dst):
+        copy = pltpu.make_async_copy(src, dst, self.local.at[self.used_local])
+        self.used_local += 1
+        copy.start()
+        self.pending_local.append(copy)
+        return copy
+
+    def settle(self, copy):
+        copy.wait()
+        self.pending_local = [other for other in self.pending_local if other is not copy]
+
+    def greet(self, partners):
+        barrier = pltpu.get_barrier_semaphore()
+        for dp_bit, tensor_bit in partners:
+            pl.semaphore_signal(
+                barrier, inc=1, device_id=(self.dp ^ dp_bit, self.tensor ^ tensor_bit), device_id_type=MESH
+            )
+        pl.semaphore_wait(barrier, len(partners))
+
+    def finish(self):
+        for copy in self.pending:
+            copy.wait_send()
+        for copy in self.pending_local:
+            copy.wait()
+
+
+class Spread:
+    def __init__(self, links, rows):
+        self.links, self.rows = links, rows
+        self.near = links.go(rows.at[0], rows.at[1], 0, 1)
+        self.far = links.go(rows.at[0], rows.at[2], 0, 2)
+        self.stage = 0
+
+    def wait(self, block):
+        rows, links = self.rows, self.links
+        if block >= 1 and self.stage == 0:
+            self.near.wait_recv()
+            low = pl.ds(0, HALF)
+            self.last_low = links.go(rows.at[1, low], rows.at[3, low], 0, 2)
+            self.stage = 1
+        if block >= 2 and self.stage == 1:
+            self.far.wait_recv()
+            high = pl.ds(HALF, HALF)
+            self.last_high = links.go(rows.at[2, high], rows.at[3, high], 0, 1)
+            self.stage = 2
+        if block >= 3 and self.stage == 2:
+            self.last_low.wait_recv()
+            self.last_high.wait_recv()
+            self.stage = 3
+
+
+class Gather:
+    def __init__(self, links, shard, whole):
+        self.links, self.whole = links, whole
+        self.size = shard.shape[0]
+        self.place = links.dp // 2
+        self.middle = (self.place == 1) | (self.place == 2)
+        own = self.rows(0)
+        self.own = links.store(shard, own)
+        self.core = [links.go(shard, own, 1, 0)]
+        self.beside = links.go(shard, own, 2, 0)
+        self.skip = links.go(shard, own, 4, 0)
+        self.third_at = links.used
+        self.third = links.remote(shard, own, 6, 0)
+
+        @pl.when(self.middle)
+        def _():
+            self.third.start()
+
+    def rows(self, step):
+        start = pl.multiple_of((self.links.dp ^ (2 * step)) * self.size, self.size)
+        return self.whole.at[pl.ds(start, self.size)]
+
+    def forward(self):
+        links = self.links
+        block = self.rows(2)
+        self.skip.wait_recv()
+        self.onward = pltpu.make_async_remote_copy(
+            src_ref=block,
+            dst_ref=block,
+            send_sem=links.send.at[links.used],
+            recv_sem=links.recv.at[self.third_at],
+            device_id=(links.dp ^ 2, links.tensor),
+            device_id_type=MESH,
+        )
+        links.used += 1
+
+        @pl.when(self.middle)
+        def _():
+            self.onward.start()
+
+        self.core.append(links.go(block, block, 1, 0))
+
+    def arrive(self):
+        links = self.links
+        self.beside.wait_recv()
+        block = self.rows(1)
+        self.core.append(links.go(block, block, 1, 0))
+        self.third.wait_recv()
+        block = self.rows(3)
+        self.core.append(links.go(block, block, 1, 0))
+        links.settle(self.own)
+        for copy in self.core:
+            copy.wait_recv()
+
+    def finish(self):
+        @pl.when(self.middle)
+        def _():
+            self.third.wait_send()
+            self.onward.wait_send()
+
+
+class Sums:
+    def __init__(self, links, parts, half_near, half_far, near, far):
+        self.links, self.parts = links, parts
+        self.half_near, self.half_far, self.near, self.far = half_near, half_far, near, far
+        self.low, self.high = pl.ds(0, HALF), pl.ds(HALF, HALF)
+
+    def ready(self, block):
+        links, parts, low, high = self.links, self.parts, self.low, self.high
+        if block == 3:
+            self.first = links.go(parts.at[3, low], self.half_near, 0, 1)
+            self.second = links.go(parts.at[3, high], self.half_far, 0, 2)
+        if block == 1:
+            self.near_low = links.go(parts.at[1, low], self.near.at[low], 0, 1)
+        if block == 2:
+            self.far_high = links.go(parts.at[2, high], self.far.at[high], 0, 2)
+
+    def add(self):
+        links, parts, low, high = self.links, self.parts, self.low, self.high
+        self.first.wait_recv()
+        parts[2, low] = (parts[2, low].astype(jnp.float32) + self.half_near[...].astype(jnp.float32)).astype(
+            jnp.bfloat16
+        )
+        self.far_low = links.go(parts.at[2, low], self.far.at[low], 0, 2)
+        self.second.wait_recv()
+        parts[1, high] = (parts[1, high].astype(jnp.float32) + self.half_far[...].astype(jnp.float32)).astype(
+            jnp.bfloat16
+        )
+        self.near_high = links.go(parts.at[1, high], self.near.at[high], 0, 1)
+
+    def arrive(self):
+        for copy in (self.near_low, self.far_high, self.far_low, self.near_high):
+            copy.wait_recv()
+
+    def sent(self):
+        links = self.links
+        mine = (self.first, self.second, self.near_low, self.far_high, self.far_low, self.near_high)
+        for copy in mine:
+            copy.wait_send()
+        links.pending = [copy for copy in links.pending if all(copy is not other for other in mine)]
+
+    def total(self, rows):
+        return self.near[rows].astype(jnp.float32) + self.far[rows].astype(jnp.float32)
+def columns(total, width, body):
+    def step(index, carry):
+        body(pl.ds(pl.multiple_of(index * width, width), width))
+        return carry
+
+    lax.fori_loop(0, total // width, step, 0)
+
+
+def split_heads(array, at, axis):
+    wide = array.astype(jnp.float32)
+    for which in range(2):
+        at[which] = jnp.where(half_mask(array.shape, axis, which), wide, 0.0).astype(jnp.bfloat16)
+
+
+def attend_rows(block, keys_t, values, limit):
+    outs, logs = [], []
+    for which in range(2):
+        scores = jnp.dot(block, keys_t[which], preferred_element_type=jnp.float32)
+        if limit is not None:
+            scores = jnp.where(lax.broadcasted_iota(jnp.int32, scores.shape, 1) < limit, scores, -jnp.inf)
+        peak = jnp.max(scores, axis=1, keepdims=True)
+        shifted = jnp.exp(scores - peak)
+        total = jnp.sum(shifted, axis=1, keepdims=True)
+        product = jnp.dot(shifted.astype(jnp.bfloat16), values[which], preferred_element_type=jnp.float32)
+        outs.append(product * (1.0 / total))
+        logs.append(peak + jnp.log(total))
+    low = half_mask(block.shape, 1, 0)
+    return outs[0] + outs[1], jnp.where(low, logs[0], logs[1])
+
+
+def block_rows(block):
+    return pl.ds(block * BLOCK, BLOCK)
+
+
+def two_heads(weights, part, parts, pair):
+    starts = [((2 * pair + which) * parts + part) * DH for which in range(2)]
+    return jnp.concatenate([weights[:, start : start + DH] for start in starts], axis=1).astype(jnp.bfloat16)
+
+
+def fill_tables(cosine, minus_sine, plus_sine, member):
+    quarter = DH // 4
+    shape = (BLOCK, PAIR)
+    lane = lax.broadcasted_iota(jnp.int32, shape, 1) % DH
+    frequency = jnp.exp((lane % quarter).astype(jnp.float32) * (-math.log(rope_base) / quarter))
+    for block in range(4):
+        place = (member ^ block) * BLOCK + lax.broadcasted_iota(jnp.int32, shape, 0)
+        angle = place.astype(jnp.float32) * frequency
+        turned, sine = jnp.cos(angle), jnp.sin(angle)
+        rows = block_rows(block)
+        cosine[rows] = jnp.where(lane < 2 * quarter, turned, 1.0)
+        minus_sine[rows] = jnp.where(lane < quarter, -sine, 0.0)
+        plus_sine[rows] = jnp.where((lane >= quarter) & (lane < 2 * quarter), sine, 0.0)
+
+
+def forward_kernel(
+    latents, gains, conditioning, f32_qkv,
+    f32_attn_out, f32_cross_q, f32_cross_kv, f32_cross_out, f32_gate, f32_up, f32_down, cotangent,
+    rows_one_out, rows_two_out, rows_three_out, seeds_out, qkv_out, attn_out_out, cross_out, keyval_w_out, mlp_out,
+    down_out, rotated_out, attended_out, logs_out,
+    query_out, keyval_out, crossed_out, cross_logs_out, resid_one_out, resid_two_out, tables_out,
+    rows_one, rows_two, rows_three, w_qkv, w_attn_out, w_cross, w_keyval, rotated, attended, logs, query, keyval,
+    crossed, cross_logs, keys_t, values, cross_keys_t, cross_values, parts, got_one, got_two, resid_one, resid_two,
+    packed, tables, context, raw_attn_out, raw_cross_q, raw_cross_kv, raw_cross_out, raw_gate, raw_up, raw_down,
+    own_qkv, own_attn_out, own_cross, own_keyval, own_mlp, own_down, send, recv, local,
+):
+    low = jnp.bfloat16
+    pairs = attended.shape[1] // PAIR
+    width = pairs * PAIR
+    links = Links(send, recv, local)
+    loads = [
+        links.store(source, target)
+        for source, target in (
+            (f32_attn_out, raw_attn_out), (f32_cross_q, raw_cross_q), (f32_cross_kv, raw_cross_kv),
+            (f32_cross_out, raw_cross_out), (f32_gate, raw_gate), (f32_up, raw_up), (f32_down, raw_down),
+        )
+    ]
+    seed_own = links.store(cotangent, seeds_out.at[0])
+    for part in range(3):
+        for pair in range(pairs):
+            at = part * width + pair * PAIR
+            own_qkv[:, at : at + PAIR] = two_heads(f32_qkv, part, 3, pair)
+    links.greet([(1, 0), (2, 0), (4, 0), (6, 0), (0, 1), (0, 2)])
+    gather_qkv = Gather(links, own_qkv, w_qkv)
+    resid = latents[...].astype(jnp.float32)
+    rows_one[0] = layer_norm(resid, gains[0:1])[0].astype(low)
+    spread_one = Spread(links, rows_one)
+    cosine, minus_sine, plus_sine = (tables.at[part] for part in range(3))
+    fill_tables(cosine, minus_sine, plus_sine, links.tensor)
+    links.store(tables, tables_out)
+    for load in loads:
+        links.settle(load)
+    own_attn_out[...] = raw_attn_out[...].T.astype(low)
+    own_cross[:, :width] = raw_cross_q[...].astype(low)
+    own_cross[:, width:] = raw_cross_out[...].T.astype(low)
+    for part in range(2):
+        for pair in range(pairs):
+            at = part * width + pair * PAIR
+            own_keyval[:, at : at + PAIR] = two_heads(raw_cross_kv, part, 2, pair)
+    hidden = raw_gate.shape[1]
+    own_mlp[:, :hidden] = raw_gate[...].astype(low)
+    own_mlp[:, hidden:] = raw_up[...].astype(low)
+    own_down[...] = raw_down[...].T.astype(low)
+    context[...] = jnp.zeros_like(context)
+    context[:CTX] = conditioning[0]
+    spread_one.wait(1)
+    gather_qkv.forward()
+    gather_attn_out = Gather(links, own_attn_out, w_attn_out)
+    gather_cross = Gather(links, own_cross, w_cross)
+    gather_keyval = Gather(links, own_keyval, w_keyval)
+    spread_one.wait(2)
+    gather_qkv.arrive()
+    links.store(w_qkv, qkv_out)
+
+    for block in range(4):
+        spread_one.wait(block)
+        rows = block_rows(block)
+        turn = (cosine[rows], minus_sine[rows], plus_sine[rows])
+
+        def project(cols):
+            packed[:, cols] = dot_plain(rows_one[block], w_qkv[:, cols])
+
+        columns(3 * width, width, project)
+        for part in range(3):
+            for pair in range(pairs):
+                at = slice(part * width + pair * PAIR, part * width + (pair + 1) * PAIR)
+                value = packed[:, at]
+                rotated[rows, at] = (value if part == 2 else head_turn(value, *turn)).astype(low)
+    links.store(rows_one, rows_one_out)
+    links.store(rotated, rotated_out)
+    for pair in range(pairs):
+        key = rotated[:, width + pair * PAIR : width + (pair + 1) * PAIR]
+        split_heads(key.astype(jnp.float32).T, keys_t.at[pair], 0)
+        split_heads(rotated[:, 2 * width + pair * PAIR : 2 * width + (pair + 1) * PAIR], values.at[pair], 1)
+
+    def out_project(source, block, weight, sums):
+        def project(cols):
+            parts[block, :, cols] = dot_cols(source[block_rows(block)], weight(cols)).astype(low)
+
+        columns(parts.shape[2], 512, project)
+        sums.ready(block)
+
+    sums_one = Sums(links, parts, *got_one)
+    for block in (3, 1, 2, 0):
+        rows = block_rows(block)
+
+        def one_pair(pair, carry):
+            at = pl.ds(pl.multiple_of(pair * PAIR, PAIR), PAIR)
+            out, log = attend_rows(rotated[rows, at] * low(DH**-0.5), keys_t.at[pair], values.at[pair], None)
+            attended[rows, at] = out.astype(low)
+            logs[rows, at] = log
+            return carry
+
+        lax.fori_loop(0, pairs, one_pair, 0)
+        if block == 3:
+            gather_attn_out.forward()
+            gather_attn_out.arrive()
+            links.store(w_attn_out, attn_out_out)
+        out_project(attended, block, lambda cols: w_attn_out[cols, :], sums_one)
+        if block == 1:
+            gather_cross.forward()
+            gather_keyval.forward()
+            gather_mlp = Gather(links, own_mlp, mlp_out)
+        if block == 2:
+            sums_one.add()
+    links.store(attended, attended_out)
+    links.store(logs, logs_out)
+    sums_one.arrive()
+    resid_one[...] = resid + parts[0].astype(jnp.float32) + sums_one.total(slice(None))
+    links.store(resid_one, resid_one_out)
+    rows_two[0] = layer_norm(resid_one[...], gains[1:2])[0].astype(low)
+    spread_two = Spread(links, rows_two)
+    gather_keyval.arrive()
+    links.store(w_keyval, keyval_w_out)
+    for part in range(2):
+        keyval[part] = dot_plain(context[...], w_keyval[:, part * width : (part + 1) * width]).astype(low)
+    for pair in range(pairs):
+        at = slice(pair * PAIR, (pair + 1) * PAIR)
+        split_heads(keyval[0, :, at].astype(jnp.float32).T, cross_keys_t.at[pair], 0)
+        split_heads(keyval[1, :, at], cross_values.at[pair], 1)
+    links.store(keyval, keyval_out)
+    gather_cross.arrive()
+    links.store(w_cross, cross_out)
+    sums_one.sent()
+    sums_two = Sums(links, parts, *got_two)
+    for block in range(4):
+        spread_two.wait(block)
+        rows = block_rows(block)
+        query[rows] = dot_plain(rows_two[block], w_cross[:, :width]).astype(low)
+        for pair in range(pairs):
+            at = slice(pair * PAIR, (pair + 1) * PAIR)
+            out, log = attend_rows(query[rows, at] * low(DH**-0.5), cross_keys_t.at[pair], cross_values.at[pair], CTX)
+            crossed[rows, at] = out.astype(low)
+            cross_logs[rows, at] = log
+        out_project(crossed, block, lambda cols: w_cross[cols, width:], sums_two)
+    sums_two.add()
+    links.store(rows_two, rows_two_out)
+    links.store(query, query_out)
+    links.store(crossed, crossed_out)
+    links.store(cross_logs, cross_logs_out)
+    links.settle(seed_own)
+    spread_seed = Spread(links, seeds_out)
+    gather_mlp.forward()
+    gather_down = Gather(links, own_down, down_out)
+    sums_two.arrive()
+    resid_two[...] = resid_one[...] + parts[0].astype(jnp.float32) + sums_two.total(slice(None))
+    links.store(resid_two, resid_two_out)
+    rows_three[0] = layer_norm(resid_two[...], gains[2:3])[0].astype(low)
+    spread_three = Spread(links, rows_three)
+    spread_seed.wait(2)
+    spread_three.wait(2)
+    gather_down.forward()
+    gather_mlp.arrive()
+    spread_seed.wait(3)
+    spread_three.wait(3)
+    links.store(rows_three, rows_three_out)
+    gather_down.arrive()
+    links.finish()
+    for gather in (gather_qkv, gather_attn_out, gather_cross, gather_keyval, gather_mlp, gather_down):
+        gather.finish()
+
+
+def whole_vmem():
+    return pl.BlockSpec(memory_space=pltpu.VMEM)
+
+
+def anywhere():
+    return pl.BlockSpec(memory_space=pl.ANY)
+
+
+def sum_buffers(model):
+    return [
+        pltpu.VMEM((HALF, model), jnp.bfloat16),
+        pltpu.VMEM((HALF, model), jnp.bfloat16),
+        pltpu.VMEM((BLOCK, model), jnp.bfloat16),
+        pltpu.VMEM((BLOCK, model), jnp.bfloat16),
+    ]
+
+
+def forward_part(latents, gains, conditioning, weights, cotangent):
+    w_qkv, w_attn_out, w_cross_q, w_cross_kv, w_cross_out, w_gate, w_up, w_down = weights
+    model = latents.shape[1]
+    depth = conditioning.shape[2]
+    wide = w_qkv.shape[1]
+    width = wide // 3
+    hidden = w_gate.shape[1]
+    pairs = width // PAIR
+    low, high = jnp.bfloat16, jnp.float32
+    share = w_qkv.shape[0]
+    outs = [
+        ((4, BLOCK, model), low),
+        ((4, BLOCK, model), low),
+        ((4, BLOCK, model), low),
+        ((4, BLOCK, model), low),
+        ((model, wide), low),
+        ((model, width), low),
+        ((model, 2 * width), low),
+        ((depth, 2 * width), low),
+        ((model, 2 * hidden), low),
+        ((model, hidden), low),
+        ((LENGTH, wide), low),
+        ((LENGTH, width), low),
+        ((LENGTH, width), high),
+        ((LENGTH, width), low),
+        ((2, FULL, width), low),
+        ((LENGTH, width), low),
+        ((LENGTH, width), high),
+        ((BLOCK, model), high),
+        ((BLOCK, model), high),
+        ((3, LENGTH, PAIR), high),
+    ]
+    work = [
+        ((4, BLOCK, model), low),
+        ((4, BLOCK, model), low),
+        ((4, BLOCK, model), low),
+        ((model, wide), low),
+        ((model, width), low),
+        ((model, 2 * width), low),
+        ((depth, 2 * width), low),
+        ((LENGTH, wide), low),
+        ((LENGTH, width), low),
+        ((LENGTH, width), high),
+        ((LENGTH, width), low),
+        ((2, FULL, width), low),
+        ((LENGTH, width), low),
+        ((LENGTH, width), high),
+        ((pairs, 2, PAIR, LENGTH), low),
+        ((pairs, 2, LENGTH, PAIR), low),
+        ((pairs, 2, PAIR, FULL), low),
+        ((pairs, 2, FULL, PAIR), low),
+        ((4, BLOCK, model), low),
+    ]
+    more = [
+        ((BLOCK, model), high),
+        ((BLOCK, model), high),
+        ((BLOCK, wide), high),
+        ((3, LENGTH, PAIR), high),
+        ((FULL, depth), low),
+        (w_attn_out.shape, high),
+        (w_cross_q.shape, high),
+        (w_cross_kv.shape, high),
+        (w_cross_out.shape, high),
+        (w_gate.shape, high),
+        (w_up.shape, high),
+        (w_down.shape, high),
+        ((share, wide), low),
+        ((share, width), low),
+        ((share, 2 * width), low),
+        (w_cross_kv.shape, low),
+        ((share, 2 * hidden), low),
+        ((share, hidden), low),
+    ]
+    scratch = [pltpu.VMEM(*buffer) for buffer in work] + [sum_buffers(model), sum_buffers(model)]
+    scratch += [pltpu.VMEM(*buffer) for buffer in more]
+    scratch += [pltpu.SemaphoreType.DMA((96,)), pltpu.SemaphoreType.DMA((96,)), pltpu.SemaphoreType.DMA((40,))]
+    return pl.pallas_call(
+        forward_kernel,
+        out_shape=[jax.ShapeDtypeStruct(*out) for out in outs],
+        in_specs=[whole_vmem()] * 4 + [anywhere()] * 8,
+        out_specs=[anywhere()] * len(outs),
+        scratch_shapes=scratch,
+        compiler_params=pltpu.CompilerParams(collective_id=1, has_side_effects=True, vmem_limit_bytes=VMEM_BYTES),
+        cost_estimate=pl.CostEstimate(flops=2**37, bytes_accessed=2**26, transcendentals=2**23),
+    )(latents, gains, conditioning, *weights, cotangent)
+
+
 def per_device(
+    latents,
+    conditioning,
+    gain_attn,
+    w_qkv,
+    w_attn_out,
+    gain_cross,
+    w_cross_q,
+    w_cross_kv,
+    w_cross_out,
+    gain_mlp,
+    w_gate,
+    w_up,
+    w_down,
+    cotangent,
+):
+    low = jnp.bfloat16
+    heads_wide = w_cross_q.shape[1]
+    hidden_wide = w_gate.shape[1]
+    members = lax.axis_size("dp")
+    context = conditioning[0]
+    (
+        rows_one, rows_two, rows_three, mlp_seed, qkv_all, attn_out_t, cross_all, cross_kv, mlp_all, down_all,
+        rotated, attended, logs, cross_query, keyval, crossed, cross_logs, resid_one, resid_two, tables,
+    ) = forward_part(
+        latents,
+        jnp.stack([gain_attn, gain_cross, gain_mlp]),
+        conditioning,
+        (w_qkv, w_attn_out, w_cross_q, w_cross_kv, w_cross_out, w_gate, w_up, w_down),
+        cotangent,
+    )
+    rows_one, rows_two, rows_three, mlp_seed = (
+        array.reshape(LENGTH, -1) for array in (rows_one, rows_two, rows_three, mlp_seed)
+    )
+    cross_q, cross_out_t = cross_all[:, :heads_wide], cross_all[:, heads_wide:]
+    head_shape = (-1, heads_wide // DH, DH)
+    both = dot_plain(rows_three, mlp_all)
+    gate_pre, up_pre = both[:, :hidden_wide], both[:, hidden_wide:]
+    sigma_gate = jax.nn.sigmoid(gate_pre)
+    swish = gate_pre * sigma_gate
+    hidden = (swish * up_pre).astype(low)
+    sum_down = dp_sum(dot_rows(mlp_seed, hidden))
+    d_hidden = dot_plain(mlp_seed, down_all)
+    d_gate = (d_hidden * up_pre * sigma_gate * (1.0 + gate_pre * (1.0 - sigma_gate))).astype(low)
+    d_up = (d_hidden * swish).astype(low)
+    d_both = jnp.concatenate([d_gate, d_up], axis=1)
+    sum_mlp = dp_sum(after(dot_rows(rows_three, d_both), sum_down))
+    d_normed = sum_rows(dot_cols(d_both, mlp_all))
+    _, scaled_three, inverse_three = layer_norm(resid_two, gain_mlp)
+    d_part, gain_grad_three = norm_backward(d_normed, scaled_three, inverse_three, gain_mlp)
+    d_resid = cotangent.astype(jnp.float32) + d_part
+    block_out = resid_two + sum_rows(dot_cols(hidden, down_all))
+    cross_seed = spread_rows(d_resid.astype(low))
+    grad_cross_out = dot_rows(cross_seed, crossed)
+    d_crossed = dot_plain(cross_seed, cross_out_t).astype(low).reshape(head_shape)
+    cross_log_heads = cross_logs.reshape(LENGTH, -1, DH)[:, :, 0].T[:, :, None]
+    d_query, d_key, d_value = cross_backward(
+        cross_query.reshape(head_shape),
+        keyval[0, :CTX].reshape(head_shape),
+        keyval[1, :CTX].reshape(head_shape),
+        d_crossed,
+        cross_log_heads,
+    )
+    d_query = d_query.reshape(-1, heads_wide).astype(low)
+    d_key, d_value = (array.reshape(CTX, -1).astype(low) for array in (d_key, d_value))
+    grad_cross_q = dot_rows(rows_two, d_query)
+    d_keyval = jnp.concatenate([d_key, d_value], axis=1)
+    grad_kv = dot_rows(context, d_keyval).astype(low)
+    grad_kv = jnp.concatenate([grad_kv.reshape(members, -1, 2, heads_wide)[:, :, part] for part in range(2)], axis=1)
+    context_part = dot_cols(d_keyval, cross_kv)
+    d_normed = sum_rows(dot_cols(d_query, cross_q))
+    _, scaled_two, inverse_two = layer_norm(resid_one, gain_cross)
+    d_part, gain_grad_two = norm_backward(d_normed, scaled_two, inverse_two, gain_cross)
+    d_resid = d_resid + d_part
+    self_seed = spread_rows(d_resid.astype(low))
+    grad_attn_out = dot_rows(self_seed, attended)
+    grad_mid = jnp.concatenate([grad.astype(low) for grad in (grad_attn_out, grad_cross_q, grad_cross_out, grad_kv.reshape(-1, heads_wide))], axis=1)
+    sum_mid = dp_sum(after(grad_mid, sum_mlp))
+    d_attended = dot_plain(self_seed, attn_out_t).astype(low)
+    d_packed = attend_back(rotated, d_attended, logs, tables)
+    sum_qkv = dp_sum(after(dot_rows(rows_one, d_packed), sum_mid))
+    d_normed = sum_rows(dot_cols(d_packed, qkv_all))
+    _, scaled_one, inverse_one = layer_norm(latents.astype(jnp.float32), gain_attn)
+    d_part, gain_grad_one = norm_backward(d_normed, scaled_one, inverse_one, gain_attn)
+    grad_latents = d_resid + d_part
+    grad_context = lax.psum(context_part.astype(low), "tensor").astype(jnp.float32)[None]
+    gains = lax.psum(jnp.stack([gain_grad_one, gain_grad_two, gain_grad_three]), ("dp", "tensor"))
+    sums = [sum_mid[:, part * heads_wide : (part + 1) * heads_wide].astype(jnp.float32) for part in range(4)]
+    half = sums[3].shape[0] // 2
+    sum_kv = jnp.concatenate([sums[3][:half], sums[3][half:]], axis=1)
+    return (
+        block_out,
+        grad_latents,
+        grad_context,
+        gains[0],
+        by_head(sum_qkv, 3).astype(jnp.float32),
+        sums[0].T,
+        gains[1],
+        sums[1],
+        by_head(sum_kv, 2),
+        sums[2].T,
+        gains[2],
+        sum_mlp[:, :hidden_wide].astype(jnp.float32),
+        sum_mlp[:, hidden_wide:].astype(jnp.float32),
+        sum_down.astype(jnp.float32).T,
+    )
+
+
+def per_device_general(
     latents,
     conditioning,
     gain_attn,
@@ -470,6 +1089,7 @@
         P("dp", "tensor"),
         P("tensor", "dp"),
     )
+    special = dict(mesh.shape) == {"dp": 8, "tensor": 4}
     return jax.shard_map(
-        per_device, mesh=mesh, in_specs=in_specs, out_specs=out_specs, check_vma=False
-    )
+        per_device if special else per_device_general, mesh=mesh, in_specs=in_specs, out_specs=out_specs, check_vma=False
+    )

time: 777 us -> 669 us (0.86)
  waiting for transfers between devices: 370 us -> 135 us
  Pallas kernels: 47.7 us -> 239 us
  starting transfers between devices: 59.1 us -> 30.2 us
  local copies, waits for them, and re-layouts: 66.3 us -> 47 us
  matrix products: 123 us -> 111 us
  other arithmetic: 44.6 us -> 35.8 us
    pallas_call x1, Pallas kernels: 19.3 us -> 211 us  [forward_part(): pl.pallas_call(forward_kernel, out_shape=[jax.ShapeDtypeStruct(*out) for...]
    ppermute x48 -> x24, waiting for transfers between devices: 203 us -> 88.2 us  [swap(): lax.ppermute(values, 'tensor', [(member, member ^ bit) for member in rang...]
    all_gather x4 -> x0, waiting for transfers between devices: 91.4 us -> none  [the longest x1 50.1 us: per_device(): mid_all = lax.all_gather(after(own_mid, qkv_all), 'dp', axis=0, tiled=True)]
    ppermute x48 -> x24, starting transfers between devices: 58.1 us -> 30 us  [swap(): lax.ppermute(values, 'tensor', [(member, member ^ bit) for member in rang...]
    psum x1, waiting for transfers between devices: 22.9 us -> 0.03 us  [per_device(): lax.psum(context_part.astype(low), 'tensor').astype(jnp.float32)[None]]
    unnamed x167 -> x116, local copies, waits for them, and re-layouts: 38.4 us -> 25.1 us
    dot_general x7 -> x5, matrix products: 40.2 us -> 35.2 us  [dot_cols(): lax.dot_general(left_op, right_op, (((1,), (1,)), ((), ())), preferred_el...]
    dot_general x7 -> x4, matrix products: 41.9 us -> 39 us  [dot_plain(): return jnp.dot(left_op, right_op, preferred_element_type=jnp.float32)]
  transfers between devices with their start and end apart: 57 -> 29, of which waited for: 33 -> 21; matrix products, arithmetic and copies ran while one was open for 24% -> 20% of each run, Pallas kernels for 6% -> 4%
where the time goes in v2:
time: 669 us; the launch traced here: 659 us
  Pallas kernels  239 us (36%)
  waiting for transfers between devices  135 us (20%)
  matrix products  111 us (17%)
  local copies, waits for them, and re-layouts  47 us (7%)
  blocking collectives  43.7 us (7%)
  other arithmetic  35.8 us (5%)
  starting transfers between devices  30.2 us (5%)
  between operations  16.5 us (2%)
    pallas_call x1, Pallas kernels, forward_part(): pl.pallas_call(forward_kernel, out_shape=[jax.ShapeDtypeStruct(*out) for...  211 us
    ppermute x24, waiting for transfers between devices, swap(): lax.ppermute(values, 'tensor', [(member, member ^ bit) for member in rang...  88.2 us
    psum x1, blocking collectives, per_device(): lax.psum(jnp.stack([gain_grad_one, gain_grad_two, gain_grad_three]), ('dp...  43.7 us
    dot_general x4, matrix products, dot_plain(): return jnp.dot(left_op, right_op, preferred_element_type=jnp.float32)  39 us
    dot_general x5, matrix products, dot_cols(): lax.dot_general(left_op, right_op, (((1,), (1,)), ((), ())), preferred_el...  35.2 us
    dot_general x7, matrix products, dot_rows(): lax.dot_general(left_op, right_op, (((0,), (0,)), ((), ())), preferred_el...  33.4 us
    reduce_scatter x3, waiting for transfers between devices, dp_sum(): lax.psum_scatter(grads.astype(jnp.bfloat16), 'dp', scatter_dimension=0, t...  31.7 us
    ppermute x24, starting transfers between devices, swap(): lax.ppermute(values, 'tensor', [(member, member ^ bit) for member in rang...  30 us
  transfers between devices with their start and end apart: 29, of which 21 were waited for; matrix products, arithmetic and copies ran while one was open for 20% of the time, Pallas kernels for 4%

profile of v2, /device:TPU:0, one launch (start us, length us, event | category | flops | bytes accessed | tf_op | source)
XLA Modules:
  0.0 659.1 jit_solution(18054830769108954407)
XLA Ops:
  8.1 2.9 copy.103.f32_down
  13.6 210.5 %shard_map.245 = (bf16[4,256,1536]{2,1,0:T(8,128)(2,1)}, bf16[4,256,1536]{2,1,0:T(8,128)(2,1)}, bf16[4,256,1536]{2,1,0:T(8,128)(2,1)}, bf16[4,256,1536]{2,1,0:T(...) custom-call(bf16[256,1536]{1,0:T(8,128)(2,1)} %latents.1, ...), custom_call_target="tpu_custom_call" | custom-call | flops 137438953472 | bytes 67108864 | tf_op jit(solution)/shard_map/pallas_call | solution.py:811
  224.1 13.5 %fusion.62 = f32[1024,3072]{1,0:T(8,128)S(1)} fusion(bf16[1024,1536]{1,0:T(8,128)(2,1)} %bitcast.118, bf16[1536,3072]{1,0:T(8,128)(2,1)} %get-tuple-element.39), kind=kOutput, calls=%fused_computation.153 | convolution fusion | flops 9663676416 | bytes 25165824 | tf_op jit(solution)/shard_map/dot_general | solution.py:186
  237.7 19.1 %multiply_convert_fusion.1 = (bf16[1024,1536]{1,0:T(8,128)(2,1)}, bf16[1024,1536]{1,0:T(8,128)(2,1)}, bf16[1024,1536]{1,0:T(8,128)(2,1)}) fusion(f32[1024,3072]{1,0:T(8,128)S(1)} %fusion.62, bf16[1024,1536]{1,0:T(8,128)(2,1)S(1)} %bitcast.120, bf16[1536,1536]{1,0:T(8,128)(2,1)S(1)} %copy-done.44), kind=kOutput, calls=%fused_computation.3 | convolution fusion | flops 4855431168 | bytes 29884416 | tf_op jit(solution)/shard_map/dot_general | solution.py:186
  256.8 8.6 %convolution_convert_fusion = bf16[1536,1536]{1,0:T(8,128)(2,1)} fusion(bf16[1024,1536]{1,0:T(8,128)(2,1)S(1)} %bitcast.121, bf16[1024,1536]{1,0:T(8,128)(2,1)} %get-tuple-element.153), kind=kOutput, calls=%fused_computation | convolution fusion | flops 4834197504 | bytes 11010048 | tf_op jit(solution)/shard_map/dot_general | solution.py:190
  265.5 9.9 %fusion.59 = (bf16[1024,1536]{1,0:T(8,128)(2,1)S(1)}, f32[1024,1536]{1,0:T(8,128)}) fusion(bf16[1024,1536]{1,0:T(8,128)(2,1)} %get-tuple-element.153, bf16[1536,1536]{1,0:T(8,128)(2,1)} %get-tuple-element.40), kind=kOutput, calls=%fused_computation.150 | convolution fusion | flops 4833411072 | bytes 17301504 | tf_op jit(solution)/shard_map/dot_general | solution.py:196
  275.5 12.6 %fusion.1 = bf16[1536,3072]{1,0:T(8,128)(2,1)} fusion(bf16[1024,1536]{1,0:T(8,128)(2,1)S(1)} %bitcast.119, bf16[1024,1536]{1,0:T(8,128)(2,1)S(1)} %copy-done.47, bf16[1024,1536]{1,0:T(8,128)(2,1)S(1)} %copy-done.45), kind=kOutput, calls=%fused_computation.8 | convolution fusion | flops 9676259328 | bytes 18874368 | tf_op jit(solution)/shard_map/dot_general | solution.py:190
  288.0 31.7 %reduce-scatter.7.cloned.1.call-done = bf16[192,1536]{1,0:T(8,128)(2,1)} async-done(((bf16[1536,1536]{1,0:T(8,128)(2,1)}), bf16[192,1536]{1,0:T(8,128)(2,1)}) %reduce-scatter.7.cloned.1.call-update) | async-done | bytes 589840 | tf_op jit(solution)/shard_map/reduce_scatter | solution.py:305
  323.9 15.3 %fusion.58 = (bf16[1024,1536]{1,0:T(8,128)(2,1)S(1)}, f32[1024,1536]{1,0:T(8,128)}) fusion(bf16[1536,3072]{1,0:T(8,128)(2,1)} %get-tuple-element.39, bf16[1024,1536]{1,0:T(8,128)(2,1)} %get-tuple-element.152, bf16[1024,1536]{1,0:T(8,128)(2,1)S(1)} %copy-done.46), kind=kOutput, calls=%fused_computation.149 | convolution fusion | flops 9677832192 | bytes 25165824 | tf_op jit(solution)/shard_map/dot_general | solution.py:196
  357.2 12.0 %collective-permute-done.1 = bf16[256,1536]{1,0:T(8,128)(2,1)S(1)} collective-permute-done((bf16[256,1536]{1,0:T(8,128)(2,1)S(1)}, bf16[256,1536]{1,0:T(8,128)(2,1)S(1)}, u32[]{:S(2)}, u32[]{:S(2)}) %collective-permute-start.1) | collective-permute-done | bytes 786464 | tf_op jit(solution)/shard_map/ppermute | solution.py:218
  369.3 12.9 %collective-permute-done.5 = bf16[256,1536]{1,0:T(8,128)(2,1)S(1)} collective-permute-done((bf16[256,1536]{1,0:T(8,128)(2,1)S(1)}, bf16[256,1536]{1,0:T(8,128)(2,1)S(1)}, u32[]{:S(2)}, u32[]{:S(2)}) %collective-permute-start.5) | collective-permute-done | bytes 786464 | tf_op jit(solution)/shard_map/ppermute | solution.py:218
  382.2 3.5 multiply_reduce_fusion.1
  391.7 3.0 copy.106
  398.9 6.0 collective-permute-done.8
  407.7 2.6 collective-permute-start.11
  426.1 4.0 collective-permute-done.12
  430.2 3.1 collective-permute-done.14
  441.1 2.8 reshape.147
  450.9 3.2 multiply_reduce_fusion.2
  460.8 10.2 %collective-permute-done.16 = bf16[256,1536]{1,0:T(8,128)(2,1)S(1)} collective-permute-done((bf16[256,1536]{1,0:T(8,128)(2,1)S(1)}, bf16[256,1536]{1,0:T(8,128)(2,1)S(1)}, u32[]{:S(2)}, u32[]{:S(2)}) %collective-permute-start.16) | collective-permute-done | bytes 786464 | tf_op jit(solution)/shard_map/ppermute | solution.py:218
  473.7 5.5 collective-permute-done.18
  485.9 6.6 %copy.121 = bf16[1536,1536]{1,0:T(8,128)(2,1)} copy(bf16[1536,1536]{0,1:T(8,128)(2,1)} %pad_maximum_fusion.1) | data formatting | bytes 9437184
  496.4 4.9 convolution_convert_fusion.5.grad_ref
  501.2 28.7 %shard_map.246 = bf16[1024,1152]{1,0:T(8,128)(2,1)} custom-call(bf16[1024,1152]{1,0:T(8,128)(2,1)} %get-tuple-element.47.q_ref.k_ref.v_ref, bf16[1024,1152]{1,0:T(8,128)(2,1)} %get-tuple-element.47.q_ref.k_ref.v_ref, bf16[1024,1152]{1,0:T(8,128)(2,1)} %get-tuple-element.47.q_ref.k_ref.v_ref, bf16[1024,384]{1,0:T(8,128)(2,1)} %convolution_convert_fusion.5.grad_ref, ...), custom_call_target="tpu_custom_call" | custom-call | flops 25769803776 | bytes 16777216 | tf_op jit(solution)/shard_map/pallas_call | solution.py:148
  530.0 7.5 %fusion.64 = bf16[1536,1152]{1,0:T(8,128)(2,1)} fusion(bf16[1024,1536]{1,0:T(8,128)(2,1)S(1)} %bitcast.116, bf16[1024,1152]{1,0:T(8,128)(2,1)} %shard_map.246), kind=kOutput, calls=%fused_computation.155 | convolution fusion | flops 3623878656 | bytes 9043968 | tf_op jit(solution)/shard_map/dot_general | solution.py:190
  537.5 15.1 %reduce-scatter.13.cloned.1.call-done = bf16[192,1536]{1,0:T(8,128)(2,1)} async-done(((bf16[1536,1536]{1,0:T(8,128)(2,1)}), bf16[192,1536]{1,0:T(8,128)(2,1)}) %reduce-scatter.13.cloned.1.call-update) | async-done | bytes 589840
  554.0 7.0 %fusion.61 = (bf16[1024,1536]{1,0:T(8,128)(2,1)S(1)}, f32[1024,1536]{1,0:T(8,128)S(1)}) fusion(bf16[1024,1152]{1,0:T(8,128)(2,1)} %shard_map.246, bf16[1536,1152]{1,0:T(8,128)(2,1)} %get-tuple-element.51), kind=kOutput, calls=%fused_computation.152 | convolution fusion | flops 3625451520 | bytes 15335424 | tf_op jit(solution)/shard_map/dot_general | solution.py:196
  564.1 5.8 collective-permute-done.20
  577.8 10.8 %collective-permute-done.21 = bf16[256,1536]{1,0:T(8,128)(2,1)} collective-permute-done((bf16[256,1536]{1,0:T(8,128)(2,1)}, bf16[256,1536]{1,0:T(8,128)(2,1)}, u32[]{:S(2)}, u32[]{:S(2)}) %collective-permute-start.21) | collective-permute-done | bytes 786464 | tf_op jit(solution)/shard_map/ppermute | solution.py:218
  590.8 3.7 fusion.18
  594.5 43.7 %psum.15 = f32[3,1536]{1,0:T(4,128)S(1)} all-reduce(f32[3,1536]{1,0:T(4,128)S(1)} %pad_maximum_fusion.18), channel_id=1, replica_groups=mesh['dp'=8,'tensor'=4] {'dp','tensor'}, use_global_device_ids=true, to_apply=%region_17.0 | all-reduce | flops 4608 | bytes 36864 | tf_op jit(solution)/shard_map/psum | solution.py:908
  638.9 3.3 fusion.17
  (247 shorter events, 112.2 us)
Async XLA Ops:
  8.1 311.6 %reduce-scatter.7.cloned.1.call-start = ((), (), s32[]{:S(2)}) async-start(), calls=%async_computation.5 | async-start | bytes 5308416 | tf_op jit(solution)/shard_map/reduce_scatter | solution.py:305
  265.5 220.4 %reduce-scatter.9.cloned.1.call-start = ((), (), s32[]{:S(2)}) async-start(), calls=%async_computation.6 | async-start | bytes 10616832 | tf_op jit(solution)/shard_map/reduce_scatter | solution.py:305
  319.7 232.9 %reduce-scatter.13.cloned.1.call-start = ((), (), s32[]{:S(2)}) async-start(), calls=%async_computation.8 | async-start | bytes 5308416
  320.9 20.7 %collective-permute-start = (bf16[128,1536]{1,0:T(8,128)(2,1)}, bf16[128,1536]{1,0:T(8,128)(2,1)}, u32[]{:S(2)}, u32[]{:S(2)}) collective-permute-start(bf16[128,1536]{1,0:T(8,128)(2,1)} %get-tuple-element.177), channel_id=1, source_target_pairs={{0,2},{1,3},{2,0},{3,1},{4,6},{5,7},{6,4},{7,5},{8,10},{9,11},{10,... | collective-permute-start | bytes 1179656 | tf_op jit(solution)/shard_map/ppermute | solution.py:218
  322.4 19.3 %collective-permute-start.2 = (bf16[128,1536]{1,0:T(8,128)(2,1)}, bf16[128,1536]{1,0:T(8,128)(2,1)}, u32[]{:S(2)}, u32[]{:S(2)}) collective-permute-start(bf16[128,1536]{1,0:T(8,128)(2,1)} %get-tuple-element.176), channel_id=1, source_target_pairs={{0,1},{1,0},{2,3},{3,2},{4,5},{5,4},{6,7},{7,6},{8,9},{9,8},{10,11... | collective-permute-start | bytes 1179656 | tf_op jit(solution)/shard_map/ppermute | solution.py:218
  340.2 10.0 %collective-permute-start.4 = (bf16[128,1536]{1,0:T(8,128)(2,1)}, bf16[128,1536]{1,0:T(8,128)(2,1)}, u32[]{:S(2)}, u32[]{:S(2)}) collective-permute-start(bf16[128,1536]{1,0:T(8,128)(2,1)} %get-tuple-element.173), channel_id=1, source_target_pairs={{0,2},{1,3},{2,0},{3,1},{4,6},{5,7},{6,4},{7,5},{8,10},{9,11},{10,... | collective-permute-start | bytes 1179656 | tf_op jit(solution)/shard_map/ppermute | solution.py:218
  340.4 12.1 %collective-permute-start.6 = (bf16[128,1536]{1,0:T(8,128)(2,1)}, bf16[128,1536]{1,0:T(8,128)(2,1)}, u32[]{:S(2)}, u32[]{:S(2)}) collective-permute-start(bf16[128,1536]{1,0:T(8,128)(2,1)} %get-tuple-element.172), channel_id=1, source_target_pairs={{0,1},{1,0},{2,3},{3,2},{4,5},{5,4},{6,7},{7,6},{8,9},{9,8},{10,11... | collective-permute-start | bytes 1179656 | tf_op jit(solution)/shard_map/ppermute | solution.py:218
  345.1 24.2 %collective-permute-start.1 = (bf16[256,1536]{1,0:T(8,128)(2,1)S(1)}, bf16[256,1536]{1,0:T(8,128)(2,1)S(1)}, u32[]{:S(2)}, u32[]{:S(2)}) collective-permute-start(bf16[256,1536]{1,0:T(8,128)(2,1)S(1)} %pad_maximum_fusion.5), channel_id=1, source_target_pairs={{0,1},{1,0},{2,3},{3,2},{4,5},{5,4},{6,7},{7,6},{8,9},{9,8},{10,11... | collective-permute-start | bytes 2359304 | tf_op jit(solution)/shard_map/ppermute | solution.py:218
  347.3 22.0 %collective-permute-start.3 = (bf16[256,1536]{1,0:T(8,128)(2,1)S(1)}, bf16[256,1536]{1,0:T(8,128)(2,1)S(1)}, u32[]{:S(2)}, u32[]{:S(2)}) collective-permute-start(bf16[256,1536]{1,0:T(8,128)(2,1)S(1)} %pad_maximum_fusion.6), channel_id=1, source_target_pairs={{0,2},{1,3},{2,0},{3,1},{4,6},{5,7},{6,4},{7,5},{8,10},{9,11},{10,... | collective-permute-start | bytes 2359304 | tf_op jit(solution)/shard_map/ppermute | solution.py:218
  353.9 28.3 %copy-start.29 = (f32[1536]{0:T(1024)S(1)}, f32[1536]{0:T(1024)}, u32[]{:S(2)}) copy-start(f32[1536]{0:T(1024)} %param.23) | copy-start | bytes 18436
  354.0 28.2 %collective-permute-start.5 = (bf16[256,1536]{1,0:T(8,128)(2,1)S(1)}, bf16[256,1536]{1,0:T(8,128)(2,1)S(1)}, u32[]{:S(2)}, u32[]{:S(2)}) collective-permute-start(bf16[256,1536]{1,0:T(8,128)(2,1)S(1)} %pad_maximum_fusion.7), channel_id=1, source_target_pairs={{0,1},{1,0},{2,3},{3,2},{4,5},{5,4},{6,7},{7,6},{8,9},{9,8},{10,11... | collective-permute-start | bytes 2359304 | tf_op jit(solution)/shard_map/ppermute | solution.py:218
  355.1 27.1 %collective-permute-start.7 = (bf16[256,1536]{1,0:T(8,128)(2,1)S(1)}, bf16[256,1536]{1,0:T(8,128)(2,1)S(1)}, u32[]{:S(2)}, u32[]{:S(2)}) collective-permute-start(bf16[256,1536]{1,0:T(8,128)(2,1)S(1)} %pad_maximum_fusion.8), channel_id=1, source_target_pairs={{0,2},{1,3},{2,0},{3,1},{4,6},{5,7},{6,4},{7,5},{8,10},{9,11},{10,... | collective-permute-start | bytes 2359304 | tf_op jit(solution)/shard_map/ppermute | solution.py:218
  357.2 28.5 %copy-start.14 = (bf16[256,1536]{1,0:T(8,128)(2,1)S(1)}, bf16[256,1536]{1,0:T(8,128)(2,1)}, u32[]{:S(2)}) copy-start(bf16[256,1536]{1,0:T(8,128)(2,1)} %cotangent.1) | copy-start | bytes 2359300
  388.0 16.8 %collective-permute-start.8 = (bf16[256,1536]{1,0:T(8,128)(2,1)}, bf16[256,1536]{1,0:T(8,128)(2,1)S(1)}, u32[]{:S(2)}, u32[]{:S(2)}) collective-permute-start(bf16[256,1536]{1,0:T(8,128)(2,1)} %get-tuple-element.148), channel_id=1, source_target_pairs={{0,1},{1,0},{2,3},{3,2},{4,5},{5,4},{6,7},{7,6},{8,9},{9,8},{10,11... | collective-permute-start | bytes 2359304 | tf_op jit(solution)/shard_map/ppermute | solution.py:218
  389.3 17.4 %collective-permute-start.9 = (bf16[256,1536]{1,0:T(8,128)(2,1)}, bf16[256,1536]{1,0:T(8,128)(2,1)}, u32[]{:S(2)}, u32[]{:S(2)}) collective-permute-start(bf16[256,1536]{1,0:T(8,128)(2,1)} %get-tuple-element.148), channel_id=1, source_target_pairs={{0,2},{1,3},{2,0},{3,1},{4,6},{5,7},{6,4},{7,5},{8,10},{9,11},{10,... | collective-permute-start | bytes 2359304 | tf_op jit(solution)/shard_map/ppermute | solution.py:218
  404.9 8.8 %collective-permute-start.10 = (bf16[128,1536]{1,0:T(8,128)(2,1)S(1)}, bf16[128,1536]{1,0:T(8,128)(2,1)S(1)}, u32[]{:S(2)}, u32[]{:S(2)}) collective-permute-start(bf16[128,1536]{1,0:T(8,128)(2,1)S(1)} %slice.277), channel_id=1, source_target_pairs={{0,2},{1,3},{2,0},{3,1},{4,6},{5,7},{6,4},{7,5},{8,10},{9,11},{10,... | collective-permute-start | bytes 1179656 | tf_op jit(solution)/shard_map/ppermute | solution.py:218
  407.7 8.3 %collective-permute-start.11 = (bf16[128,1536]{1,0:T(8,128)(2,1)S(1)}, bf16[128,1536]{1,0:T(8,128)(2,1)S(1)}, u32[]{:S(2)}, u32[]{:S(2)}) collective-permute-start(bf16[128,1536]{1,0:T(8,128)(2,1)S(1)} %slice.278), channel_id=1, source_target_pairs={{0,1},{1,0},{2,3},{3,2},{4,5},{5,4},{6,7},{7,6},{8,9},{9,8},{10,11... | collective-permute-start | bytes 1179656 | tf_op jit(solution)/shard_map/ppermute | solution.py:218
  422.3 7.8 %collective-permute-start.12 = (bf16[128,1536]{1,0:T(8,128)(2,1)S(1)}, bf16[128,1536]{1,0:T(8,128)(2,1)S(1)}, u32[]{:S(2)}, u32[]{:S(2)}) collective-permute-start(bf16[128,1536]{1,0:T(8,128)(2,1)S(1)} %get-tuple-element.169), channel_id=1, source_target_pairs={{0,2},{1,3},{2,0},{3,1},{4,6},{5,7},{6,4},{7,5},{8,10},{9,11},{10,... | collective-permute-start | bytes 1179656 | tf_op jit(solution)/shard_map/ppermute | solution.py:218
  423.5 9.8 %collective-permute-start.14 = (bf16[128,1536]{1,0:T(8,128)(2,1)S(1)}, bf16[128,1536]{1,0:T(8,128)(2,1)S(1)}, u32[]{:S(2)}, u32[]{:S(2)}) collective-permute-start(bf16[128,1536]{1,0:T(8,128)(2,1)S(1)} %get-tuple-element.168), channel_id=1, source_target_pairs={{0,1},{1,0},{2,3},{3,2},{4,5},{5,4},{6,7},{7,6},{8,9},{9,8},{10,11... | collective-permute-start | bytes 1179656 | tf_op jit(solution)/shard_map/ppermute | solution.py:218
  434.5 14.0 %collective-permute-start.13 = (bf16[256,1536]{1,0:T(8,128)(2,1)}, bf16[256,1536]{1,0:T(8,128)(2,1)}, u32[]{:S(2)}, u32[]{:S(2)}) collective-permute-start(bf16[256,1536]{1,0:T(8,128)(2,1)} %pad_maximum_fusion.9), channel_id=1, source_target_pairs={{0,1},{1,0},{2,3},{3,2},{4,5},{5,4},{6,7},{7,6},{8,9},{9,8},{10,11... | collective-permute-start | bytes 2359304 | tf_op jit(solution)/shard_map/ppermute | solution.py:218
  437.0 13.9 %collective-permute-start.15 = (bf16[256,1536]{1,0:T(8,128)(2,1)}, bf16[256,1536]{1,0:T(8,128)(2,1)}, u32[]{:S(2)}, u32[]{:S(2)}) collective-permute-start(bf16[256,1536]{1,0:T(8,128)(2,1)} %pad_maximum_fusion.10), channel_id=1, source_target_pairs={{0,2},{1,3},{2,0},{3,1},{4,6},{5,7},{6,4},{7,5},{8,10},{9,11},{10,... | collective-permute-start | bytes 2359304 | tf_op jit(solution)/shard_map/ppermute | solution.py:218
  454.7 16.3 %collective-permute-start.16 = (bf16[256,1536]{1,0:T(8,128)(2,1)S(1)}, bf16[256,1536]{1,0:T(8,128)(2,1)S(1)}, u32[]{:S(2)}, u32[]{:S(2)}) collective-permute-start(bf16[256,1536]{1,0:T(8,128)(2,1)S(1)} %get-tuple-element.144), channel_id=1, source_target_pairs={{0,1},{1,0},{2,3},{3,2},{4,5},{5,4},{6,7},{7,6},{8,9},{9,8},{10,11... | collective-permute-start | bytes 2359304 | tf_op jit(solution)/shard_map/ppermute | solution.py:218
  454.8 18.7 %collective-permute-start.17 = (bf16[256,1536]{1,0:T(8,128)(2,1)S(1)}, bf16[256,1536]{1,0:T(8,128)(2,1)S(1)}, u32[]{:S(2)}, u32[]{:S(2)}) collective-permute-start(bf16[256,1536]{1,0:T(8,128)(2,1)S(1)} %get-tuple-element.144), channel_id=1, source_target_pairs={{0,2},{1,3},{2,0},{3,1},{4,6},{5,7},{6,4},{7,5},{8,10},{9,11},{10,... | collective-permute-start | bytes 2359304 | tf_op jit(solution)/shard_map/ppermute | solution.py:218
  471.0 8.2 %collective-permute-start.18 = (bf16[128,1536]{1,0:T(8,128)(2,1)S(1)}, bf16[128,1536]{1,0:T(8,128)(2,1)S(1)}, u32[]{:S(2)}, u32[]{:S(2)}) collective-permute-start(bf16[128,1536]{1,0:T(8,128)(2,1)S(1)} %slice.286), channel_id=1, source_target_pairs={{0,2},{1,3},{2,0},{3,1},{4,6},{5,7},{6,4},{7,5},{8,10},{9,11},{10,... | collective-permute-start | bytes 1179656 | tf_op jit(solution)/shard_map/ppermute | solution.py:218
  473.5 7.8 %collective-permute-start.19 = (bf16[128,1536]{1,0:T(8,128)(2,1)S(1)}, bf16[128,1536]{1,0:T(8,128)(2,1)S(1)}, u32[]{:S(2)}, u32[]{:S(2)}) collective-permute-start(bf16[128,1536]{1,0:T(8,128)(2,1)S(1)} %slice.287), channel_id=1, source_target_pairs={{0,1},{1,0},{2,3},{3,2},{4,5},{5,4},{6,7},{7,6},{8,9},{9,8},{10,11... | collective-permute-start | bytes 1179656 | tf_op jit(solution)/shard_map/ppermute | solution.py:218
  492.5 83.3 %all-reduce.2.cloned.1.call-start = ((), (), s32[]{:S(2)}) async-start(), calls=%async_computation.4 | async-start | bytes 417792 | tf_op jit(solution)/shard_map/psum | solution.py:907
  496.3 152.6 %reduce-scatter.11.cloned.1.call-start = ((), (), s32[]{:S(2)}) async-start(), calls=%async_computation.7 | async-start | bytes 3981312 | tf_op jit(solution)/shard_map/reduce_scatter | solution.py:305
  501.2 28.7 %copy-start.38 = (bf16[4,256,1536]{2,1,0:T(8,128)(2,1)S(1)}, bf16[4,256,1536]{2,1,0:T(8,128)(2,1)}, u32[]{:S(2)}) copy-start(bf16[4,256,1536]{2,1,0:T(8,128)(2,1)} %get-tuple-element.53) | copy-start | bytes 9437188
  561.1 8.8 %collective-permute-start.20 = (bf16[128,1536]{1,0:T(8,128)(2,1)S(1)}, bf16[128,1536]{1,0:T(8,128)(2,1)S(1)}, u32[]{:S(2)}, u32[]{:S(2)}) collective-permute-start(bf16[128,1536]{1,0:T(8,128)(2,1)S(1)} %get-tuple-element.165), channel_id=1, source_target_pairs={{0,2},{1,3},{2,0},{3,1},{4,6},{5,7},{6,4},{7,5},{8,10},{9,11},{10,... | collective-permute-start | bytes 1179656 | tf_op jit(solution)/shard_map/ppermute | solution.py:218
  562.6 8.4 %collective-permute-start.22 = (bf16[128,1536]{1,0:T(8,128)(2,1)S(1)}, bf16[128,1536]{1,0:T(8,128)(2,1)S(1)}, u32[]{:S(2)}, u32[]{:S(2)}) collective-permute-start(bf16[128,1536]{1,0:T(8,128)(2,1)S(1)} %get-tuple-element.164), channel_id=1, source_target_pairs={{0,1},{1,0},{2,3},{3,2},{4,5},{5,4},{6,7},{7,6},{8,9},{9,8},{10,11... | collective-permute-start | bytes 1179656 | tf_op jit(solution)/shard_map/ppermute | solution.py:218
  572.3 16.4 %collective-permute-start.21 = (bf16[256,1536]{1,0:T(8,128)(2,1)}, bf16[256,1536]{1,0:T(8,128)(2,1)}, u32[]{:S(2)}, u32[]{:S(2)}) collective-permute-start(bf16[256,1536]{1,0:T(8,128)(2,1)} %pad_maximum_fusion.11), channel_id=1, source_target_pairs={{0,1},{1,0},{2,3},{3,2},{4,5},{5,4},{6,7},{7,6},{8,9},{9,8},{10,11... | collective-permute-start | bytes 2359304 | tf_op jit(solution)/shard_map/ppermute | solution.py:218
  574.7 16.1 %collective-permute-start.23 = (bf16[256,1536]{1,0:T(8,128)(2,1)}, bf16[256,1536]{1,0:T(8,128)(2,1)}, u32[]{:S(2)}, u32[]{:S(2)}) collective-permute-start(bf16[256,1536]{1,0:T(8,128)(2,1)} %pad_maximum_fusion.12), channel_id=1, source_target_pairs={{0,2},{1,3},{2,0},{3,1},{4,6},{5,7},{6,4},{7,5},{8,10},{9,11},{10,... | collective-permute-start | bytes 2359304 | tf_op jit(solution)/shard_map/ppermute | solution.py:218
  (45 other events, 261.6 us)
Sparse Core Ops, SparseCore 0:
  265.6 54.0 reduce-scatter.6
  322.1 97.8 reduce-scatter.8
  492.6 59.9 reduce-scatter.12
  554.9 42.1 reduce-scatter.10
Sparse Core Ops, SparseCore 1:
  496.5 47.1 all-reduce.1

commit v3 on v2

--- a/solution.py
+++ b/solution.py
@@ -13,17 +13,18 @@
 LENGTH = 1024
 PAIR = 2 * DH
 ROWS = 256
-VMEM_BYTES = 58 * 2**20
+VMEM_BYTES = 62 * 2**20
 
 norm_eps = 1e-05
 rope_base = 10000.0
 
 
-def head_turn(values, cosine, minus_sine, plus_sine):
+def head_turn(values, cosine, sine):
     quarter = DH // 4
     ahead = pltpu.roll(values, PAIR - quarter, 1)
     behind = pltpu.roll(values, quarter, 1)
-    return values * cosine + ahead * minus_sine + behind * plus_sine
+    lane = lax.broadcasted_iota(jnp.int32, values.shape, 1) % DH
+    return values * cosine + jnp.where(lane < quarter, -ahead, behind) * sine
 
 
 def half_mask(shape, axis, which):
@@ -31,10 +32,10 @@
     return (place >= DH) if which else (place < DH)
 
 
-def attend_kernel(q_ref, k_ref, v_ref, cos_ref, msin_ref, psin_ref, out_ref, rot_ref, log_ref, kt_ref, vm_ref):
+def attend_kernel(q_ref, k_ref, v_ref, cos_ref, sin_ref, out_ref, rot_ref, log_ref, kt_ref, vm_ref):
     pairs = pl.num_programs(0)
     pair = pl.program_id(0)
-    turn = (cos_ref[...], msin_ref[...], psin_ref[...])
+    turn = (cos_ref[...], sin_ref[...])
     query = head_turn(q_ref[...], *turn).astype(jnp.bfloat16)
     key = head_turn(k_ref[...], *turn).astype(jnp.bfloat16)
     value = v_ref[...].astype(jnp.bfloat16)
@@ -68,7 +69,7 @@
 
 
 def attend_back_kernel(
-    q_ref, k_ref, v_ref, grad_ref, log_ref, cos_ref, msin_ref, psin_ref, out_ref,
+    q_ref, k_ref, v_ref, grad_ref, log_ref, cos_ref, sin_ref, out_ref,
     kt_ref, vt_ref, km_ref, qt_ref, gt_ref, dq_ref, dk_ref, dv_ref,
 ):
     pairs = pl.num_programs(0)
@@ -107,7 +108,7 @@
         return carry
 
     lax.fori_loop(0, LENGTH // ROWS, one_block, 0)
-    turn = (cos_ref[...], -msin_ref[...], -psin_ref[...])
+    turn = (cos_ref[...], -sin_ref[...])
     results = (head_turn(dq_ref[...], *turn), head_turn(dk_ref[...].T, *turn), dv_ref[...].T)
     for part, array in enumerate(results):
         start = pl.multiple_of((part * pairs + pair) * PAIR, PAIR)
@@ -128,7 +129,7 @@
     return pl.pallas_call(
         attend_kernel,
         grid=(pairs,),
-        in_specs=[column_block(part * pairs) for part in range(3)] + [whole_block(PAIR)] * 3,
+        in_specs=[column_block(part * pairs) for part in range(3)] + [whole_block(PAIR)] * 2,
         out_specs=[column_block(0), whole_block(columns), column_block(0)],
         out_shape=[
             jax.ShapeDtypeStruct((LENGTH, pairs * PAIR), jnp.bfloat16),
@@ -150,7 +151,7 @@
         grid=(pairs,),
         in_specs=[column_block(part * pairs) for part in range(3)]
         + [column_block(0), column_block(0)]
-        + [whole_block(PAIR)] * 3,
+        + [whole_block(PAIR)] * 2,
         out_specs=whole_block(columns),
         out_shape=jax.ShapeDtypeStruct((LENGTH, columns), jnp.bfloat16),
         scratch_shapes=[
@@ -176,8 +177,7 @@
     zeros, ones = jnp.zeros_like(sine), jnp.ones_like(sine)
     rows = (
         jnp.concatenate([cosine, cosine, ones, ones], axis=1),
-        jnp.concatenate([-sine, zeros, zeros, zeros], axis=1),
-        jnp.concatenate([zeros, sine, zeros, zeros], axis=1),
+        jnp.concatenate([sine, sine, zeros, zeros], axis=1),
     )
     return tuple(jnp.concatenate([row, row], axis=1) for row in rows)
 
@@ -351,6 +351,11 @@
         copy.wait()
         self.pending_local = [other for other in self.pending_local if other is not copy]
 
+    def settle_sends(self, copies):
+        for copy in copies:
+            copy.wait_send()
+        self.pending = [copy for copy in self.pending if all(copy is not other for other in copies)]
+
     def greet(self, partners):
         barrier = pltpu.get_barrier_semaphore()
         for dp_bit, tensor_bit in partners:
@@ -390,6 +395,9 @@
             self.last_high.wait_recv()
             self.stage = 3
 
+    def sent(self):
+        self.links.settle_sends((self.near, self.far, self.last_low, self.last_high))
+
 
 class Gather:
     def __init__(self, links, shard, whole):
@@ -486,11 +494,9 @@
             copy.wait_recv()
 
     def sent(self):
-        links = self.links
-        mine = (self.first, self.second, self.near_low, self.far_high, self.far_low, self.near_high)
-        for copy in mine:
-            copy.wait_send()
-        links.pending = [copy for copy in links.pending if all(copy is not other for other in mine)]
+        self.links.settle_sends(
+            (self.first, self.second, self.near_low, self.far_high, self.far_low, self.near_high)
+        )
 
     def total(self, rows):
         return self.near[rows].astype(jnp.float32) + self.far[rows].astype(jnp.float32)
@@ -502,26 +508,29 @@
     lax.fori_loop(0, total // width, step, 0)
 
 
-def split_heads(array, at, axis):
-    wide = array.astype(jnp.float32)
-    for which in range(2):
-        at[which] = jnp.where(half_mask(array.shape, axis, which), wide, 0.0).astype(jnp.bfloat16)
-
-
 def attend_rows(block, keys_t, values, limit):
     outs, logs = [], []
     for which in range(2):
-        scores = jnp.dot(block, keys_t[which], preferred_element_type=jnp.float32)
+        part = jnp.where(half_mask(block.shape, 1, which), block, jnp.zeros_like(block))
+        scores = jnp.dot(part, keys_t, preferred_element_type=jnp.float32)
         if limit is not None:
             scores = jnp.where(lax.broadcasted_iota(jnp.int32, scores.shape, 1) < limit, scores, -jnp.inf)
         peak = jnp.max(scores, axis=1, keepdims=True)
         shifted = jnp.exp(scores - peak)
         total = jnp.sum(shifted, axis=1, keepdims=True)
-        product = jnp.dot(shifted.astype(jnp.bfloat16), values[which], preferred_element_type=jnp.float32)
+        product = jnp.dot(shifted.astype(jnp.bfloat16), values, preferred_element_type=jnp.float32)
         outs.append(product * (1.0 / total))
         logs.append(peak + jnp.log(total))
     low = half_mask(block.shape, 1, 0)
-    return outs[0] + outs[1], jnp.where(low, logs[0], logs[1])
+    return jnp.where(low, outs[0], outs[1]), jnp.where(low, logs[0], logs[1])
+
+
+def row_steps(total, body):
+    def step(index, carry):
+        body(pl.ds(pl.multiple_of(index * 32, 32), 32))
+        return carry
+
+    lax.fori_loop(0, total // 32, step, 0)
 
 
 def block_rows(block):
@@ -533,7 +542,7 @@
     return jnp.concatenate([weights[:, start : start + DH] for start in starts], axis=1).astype(jnp.bfloat16)
 
 
-def fill_tables(cosine, minus_sine, plus_sine, member):
+def fill_tables(cosine, sine, member):
     quarter = DH // 4
     shape = (BLOCK, PAIR)
     lane = lax.broadcasted_iota(jnp.int32, shape, 1) % DH
@@ -541,11 +550,9 @@
     for block in range(4):
         place = (member ^ block) * BLOCK + lax.broadcasted_iota(jnp.int32, shape, 0)
         angle = place.astype(jnp.float32) * frequency
-        turned, sine = jnp.cos(angle), jnp.sin(angle)
         rows = block_rows(block)
-        cosine[rows] = jnp.where(lane < 2 * quarter, turned, 1.0)
-        minus_sine[rows] = jnp.where(lane < quarter, -sine, 0.0)
-        plus_sine[rows] = jnp.where((lane >= quarter) & (lane < 2 * quarter), sine, 0.0)
+        cosine[rows] = jnp.where(lane < 2 * quarter, jnp.cos(angle), 1.0)
+        sine[rows] = jnp.where(lane < 2 * quarter, jnp.sin(angle), 0.0)
 
 
 def forward_kernel(
@@ -555,7 +562,7 @@
     down_out, rotated_out, attended_out, logs_out,
     query_out, keyval_out, crossed_out, cross_logs_out, resid_one_out, resid_two_out, tables_out,
     rows_one, rows_two, rows_three, w_qkv, w_attn_out, w_cross, w_keyval, rotated, attended, logs, query, keyval,
-    crossed, cross_logs, keys_t, values, cross_keys_t, cross_values, parts, got_one, got_two, resid_one, resid_two,
+    crossed, cross_logs, keys_t, cross_keys_t, parts, got_one, got_two, resid_one, resid_two,
     packed, tables, context, raw_attn_out, raw_cross_q, raw_cross_kv, raw_cross_out, raw_gate, raw_up, raw_down,
     own_qkv, own_attn_out, own_cross, own_keyval, own_mlp, own_down, send, recv, local,
 ):
@@ -577,17 +584,20 @@
             own_qkv[:, at : at + PAIR] = two_heads(f32_qkv, part, 3, pair)
     links.greet([(1, 0), (2, 0), (4, 0), (6, 0), (0, 1), (0, 2)])
     gather_qkv = Gather(links, own_qkv, w_qkv)
-    resid = latents[...].astype(jnp.float32)
-    rows_one[0] = layer_norm(resid, gains[0:1])[0].astype(low)
+
+    def norm_one(rows):
+        rows_one[0, rows] = layer_norm(latents[rows].astype(jnp.float32), gains[0:1])[0].astype(low)
+
+    row_steps(BLOCK, norm_one)
     spread_one = Spread(links, rows_one)
-    cosine, minus_sine, plus_sine = (tables.at[part] for part in range(3))
-    fill_tables(cosine, minus_sine, plus_sine, links.tensor)
+    cosine, sine = (tables.at[part] for part in range(2))
+    fill_tables(cosine, sine, links.tensor)
     links.store(tables, tables_out)
     for load in loads:
         links.settle(load)
-    own_attn_out[...] = raw_attn_out[...].T.astype(low)
+    own_attn_out[...] = raw_attn_out[...].astype(low)
     own_cross[:, :width] = raw_cross_q[...].astype(low)
-    own_cross[:, width:] = raw_cross_out[...].T.astype(low)
+    own_cross[:, width:] = raw_cross_out[...].astype(low)
     for part in range(2):
         for pair in range(pairs):
             at = part * width + pair * PAIR
@@ -595,7 +605,7 @@
     hidden = raw_gate.shape[1]
     own_mlp[:, :hidden] = raw_gate[...].astype(low)
     own_mlp[:, hidden:] = raw_up[...].astype(low)
-    own_down[...] = raw_down[...].T.astype(low)
+    own_down[...] = raw_down[...].astype(low)
     context[...] = jnp.zeros_like(context)
     context[:CTX] = conditioning[0]
     spread_one.wait(1)
@@ -610,7 +620,7 @@
     for block in range(4):
         spread_one.wait(block)
         rows = block_rows(block)
-        turn = (cosine[rows], minus_sine[rows], plus_sine[rows])
+        turn = (cosine[rows], sine[rows])
 
         def project(cols):
             packed[:, cols] = dot_plain(rows_one[block], w_qkv[:, cols])
@@ -625,8 +635,7 @@
     links.store(rotated, rotated_out)
     for pair in range(pairs):
         key = rotated[:, width + pair * PAIR : width + (pair + 1) * PAIR]
-        split_heads(key.astype(jnp.float32).T, keys_t.at[pair], 0)
-        split_heads(rotated[:, 2 * width + pair * PAIR : 2 * width + (pair + 1) * PAIR], values.at[pair], 1)
+        keys_t[pair] = key.astype(jnp.float32).T.astype(low)
 
     def out_project(source, block, weight, sums):
         def project(cols):
@@ -641,7 +650,8 @@
 
         def one_pair(pair, carry):
             at = pl.ds(pl.multiple_of(pair * PAIR, PAIR), PAIR)
-            out, log = attend_rows(rotated[rows, at] * low(DH**-0.5), keys_t.at[pair], values.at[pair], None)
+            values_at = pl.ds(pl.multiple_of(2 * width + pair * PAIR, PAIR), PAIR)
+            out, log = attend_rows(rotated[rows, at] * low(DH**-0.5), keys_t[pair], rotated[:, values_at], None)
             attended[rows, at] = out.astype(low)
             logs[rows, at] = log
             return carry
@@ -661,18 +671,22 @@
     links.store(attended, attended_out)
     links.store(logs, logs_out)
     sums_one.arrive()
-    resid_one[...] = resid + parts[0].astype(jnp.float32) + sums_one.total(slice(None))
+
+    def norm_two(rows):
+        value = latents[rows].astype(jnp.float32) + parts[0, rows].astype(jnp.float32) + sums_one.total(rows)
+        resid_one[rows] = value
+        rows_two[0, rows] = layer_norm(value, gains[1:2])[0].astype(low)
+
+    row_steps(BLOCK, norm_two)
+    spread_two = Spread(links, rows_two)
     links.store(resid_one, resid_one_out)
-    rows_two[0] = layer_norm(resid_one[...], gains[1:2])[0].astype(low)
-    spread_two = Spread(links, rows_two)
     gather_keyval.arrive()
     links.store(w_keyval, keyval_w_out)
     for part in range(2):
         keyval[part] = dot_plain(context[...], w_keyval[:, part * width : (part + 1) * width]).astype(low)
     for pair in range(pairs):
         at = slice(pair * PAIR, (pair + 1) * PAIR)
-        split_heads(keyval[0, :, at].astype(jnp.float32).T, cross_keys_t.at[pair], 0)
-        split_heads(keyval[1, :, at], cross_values.at[pair], 1)
+        cross_keys_t[pair] = keyval[0, :, at].astype(jnp.float32).T.astype(low)
     links.store(keyval, keyval_out)
     gather_cross.arrive()
     links.store(w_cross, cross_out)
@@ -684,7 +698,7 @@
         query[rows] = dot_plain(rows_two[block], w_cross[:, :width]).astype(low)
         for pair in range(pairs):
             at = slice(pair * PAIR, (pair + 1) * PAIR)
-            out, log = attend_rows(query[rows, at] * low(DH**-0.5), cross_keys_t.at[pair], cross_values.at[pair], CTX)
+            out, log = attend_rows(query[rows, at] * low(DH**-0.5), cross_keys_t[pair], keyval[1, :, at], CTX)
             crossed[rows, at] = out.astype(low)
             cross_logs[rows, at] = log
         out_project(crossed, block, lambda cols: w_cross[cols, width:], sums_two)
@@ -698,10 +712,15 @@
     gather_mlp.forward()
     gather_down = Gather(links, own_down, down_out)
     sums_two.arrive()
-    resid_two[...] = resid_one[...] + parts[0].astype(jnp.float32) + sums_two.total(slice(None))
+
+    def norm_three(rows):
+        value = resid_one[rows] + parts[0, rows].astype(jnp.float32) + sums_two.total(rows)
+        resid_two[rows] = value
+        rows_three[0, rows] = layer_norm(value, gains[2:3])[0].astype(low)
+
+    row_steps(BLOCK, norm_three)
+    spread_three = Spread(links, rows_three)
     links.store(resid_two, resid_two_out)
-    rows_three[0] = layer_norm(resid_two[...], gains[2:3])[0].astype(low)
-    spread_three = Spread(links, rows_three)
     spread_seed.wait(2)
     spread_three.wait(2)
     gather_down.forward()
@@ -762,7 +781,7 @@
         ((LENGTH, width), high),
         ((BLOCK, model), high),
         ((BLOCK, model), high),
-        ((3, LENGTH, PAIR), high),
+        ((2, LENGTH, PAIR), high),
     ]
     work = [
         ((4, BLOCK, model), low),
@@ -779,17 +798,15 @@
         ((2, FULL, width), low),
         ((LENGTH, width), low),
         ((LENGTH, width), high),
-        ((pairs, 2, PAIR, LENGTH), low),
-        ((pairs, 2, LENGTH, PAIR), low),
-        ((pairs, 2, PAIR, FULL), low),
-        ((pairs, 2, FULL, PAIR), low),
+        ((pairs, PAIR, LENGTH), low),
+        ((pairs, PAIR, FULL), low),
         ((4, BLOCK, model), low),
     ]
     more = [
         ((BLOCK, model), high),
         ((BLOCK, model), high),
         ((BLOCK, wide), high),
-        ((3, LENGTH, PAIR), high),
+        ((2, LENGTH, PAIR), high),
         ((FULL, depth), low),
         (w_attn_out.shape, high),
         (w_cross_q.shape, high),
@@ -819,6 +836,441 @@
     )(latents, gains, conditioning, *weights, cotangent)
 
 
+class Scatter:
+    def __init__(self, links, grads, got_core, extra, got, core_bit):
+        self.links, self.grads, self.got_core, self.extra, self.got = links, grads, got_core, extra, got
+        self.size = got.shape[1]
+        self.place, self.which = links.dp // 2, links.dp % 2
+        self.middle = (self.place == 1) | (self.place == 2)
+
+    def rows(self, place, which):
+        start = pl.multiple_of((2 * place + which) * self.size, self.size)
+        return pl.ds(start, self.size)
+
+    def pair_up(self):
+        self.core = [
+            self.links.go(self.grads.at[self.rows(place, 1 - self.which)], self.got_core.at[place], 1, 0)
+            for place in range(4)
+        ]
+
+    def combine(self):
+        links, grads = self.links, self.grads
+        for copy in self.core:
+            copy.wait_recv()
+
+        def add(place, carry):
+            rows = self.rows(place, self.which)
+            grads[rows] = (grads[rows].astype(jnp.float32) + self.got_core[place].astype(jnp.float32)).astype(
+                jnp.bfloat16
+            )
+            return carry
+
+        lax.fori_loop(0, 4, add, 0)
+        block = [grads.at[self.rows(self.place ^ step, self.which)] for step in range(4)]
+        self.to_extra = links.remote(block[3], self.extra, 2, 0)
+        self.to_third = links.remote(block[3], self.got.at[2], 6, 0)
+        self.to_skip = links.remote(block[2], self.got.at[1], 4, 0)
+
+        @pl.when(self.middle)
+        def _():
+            self.to_third.start()
+
+        @pl.when(jnp.logical_not(self.middle))
+        def _():
+            self.to_extra.start()
+            self.to_skip.start()
+
+        self.beside = links.go(block[1], self.got.at[0], 2, 0)
+
+    def relay(self):
+        @pl.when(self.middle)
+        def _():
+            self.to_extra.wait_recv()
+            rows = self.rows(self.place ^ 2, self.which)
+            self.grads[rows] = (
+                self.grads[rows].astype(jnp.float32) + self.extra[...].astype(jnp.float32)
+            ).astype(jnp.bfloat16)
+            self.to_skip.start()
+
+    def arrive(self):
+        self.beside.wait_recv()
+        self.to_skip.wait_recv()
+
+        @pl.when(self.middle)
+        def _():
+            self.to_third.wait_recv()
+
+    def total(self, out, cols):
+        mine = self.grads[self.rows(self.place, self.which), cols].astype(jnp.float32)
+        out[...] = mine + self.got[0, :, cols].astype(jnp.float32) + self.got[1, :, cols].astype(jnp.float32)
+
+        @pl.when(self.middle)
+        def _():
+            out[...] += self.got[2, :, cols].astype(jnp.float32)
+
+    def finish(self):
+        self.to_skip.wait_send()
+
+        @pl.when(self.middle)
+        def _():
+            self.to_third.wait_send()
+
+        @pl.when(jnp.logical_not(self.middle))
+        def _():
+            self.to_extra.wait_send()
+
+
+def attend_rows_back(block, grads, log, keys_t, values_t, keys, d_keys_t, d_values_t, limit):
+    block_t = block.astype(jnp.float32).T.astype(jnp.bfloat16)
+    grads_t = grads.astype(jnp.float32).T.astype(jnp.bfloat16)
+    outs = []
+    for which in range(2):
+        half = slice(which * DH, (which + 1) * DH)
+        keep = half_mask(block.shape, 1, which)
+        scores = jnp.dot(jnp.where(keep, block, jnp.zeros_like(block)), keys_t, preferred_element_type=jnp.float32)
+        probs = jnp.exp(scores - log[:, which * DH : which * DH + 1])
+        if limit is not None:
+            probs = jnp.where(lax.broadcasted_iota(jnp.int32, probs.shape, 1) < limit, probs, 0.0)
+        d_prob = jnp.dot(jnp.where(keep, grads, jnp.zeros_like(grads)), values_t, preferred_element_type=jnp.float32)
+        center = jnp.sum(probs * d_prob, axis=1, keepdims=True)
+        d_score = (probs * (d_prob - center)).astype(jnp.bfloat16)
+        outs.append(jnp.dot(d_score, keys, preferred_element_type=jnp.float32))
+        d_keys_t[half, :] += jnp.dot(block_t[half], d_score, preferred_element_type=jnp.float32)
+        d_values_t[half, :] += jnp.dot(grads_t[half], probs.astype(jnp.bfloat16), preferred_element_type=jnp.float32)
+    return jnp.where(half_mask(block.shape, 1, 0), outs[0], outs[1]) * DH**-0.5
+
+
+def backward_kernel(
+    latents, gains, conditioning, cotangent,
+    in_parts, in_last, in_resid_one, in_resid_two, in_qkv, in_attn_out, in_cross, in_keyval_w, in_rows_one, in_rows_two,
+    in_rotated, in_attended, in_logs, in_query, in_keyval, in_crossed, in_cross_logs, in_tables,
+    block_out, grad_latents, grad_context, grad_gains, grad_qkv, grad_attn_out, grad_cross_q, grad_keyval,
+    grad_cross_out,
+    parts, rows_two, seed_one, seed_two, w_qkv, w_attn_out, w_cross, w_keyval, rotated, attended, crossed, query,
+    d_attended, logs, keys_t, values_t, d_keys_t, d_values_t, cross_keys_t, cross_values_t, d_cross_keys_t,
+    d_cross_values_t, keyval, d_keyval, context, context_sum, context_got, resid, d_resid, tables,
+    gain_rows, gain_got, got_one, got_two, core_qkv, core_attn_out, core_cross, core_keyval,
+    extra_qkv, extra_attn_out, extra_cross, extra_keyval, far_qkv, far_attn_out, far_cross, far_keyval,
+    sum_keyval, sum_last, out_qkv, out_keyval,
+    send, recv, local,
+):
+    low = jnp.bfloat16
+    width = attended.shape[1]
+    pairs = width // PAIR
+    model = latents.shape[1]
+    links = Links(send, recv, local)
+    load_parts = [links.store(in_parts.at[block], parts.at[block]) for block in (3, 1, 2, 0)]
+    load_resid = links.store(in_resid_two, resid)
+    load_cross = [
+        links.store(source, target)
+        for source, target in (
+            (in_cross, w_cross), (in_keyval, keyval), (in_query, query), (in_crossed, crossed), (in_cross_logs, logs),
+        )
+    ]
+    load_mid = [links.store(in_rows_two, rows_two), links.store(in_keyval_w, w_keyval)]
+    load_self = [
+        links.store(source, target)
+        for source, target in (
+            (in_attn_out, w_attn_out), (in_rotated, rotated), (in_attended, attended), (in_tables, tables),
+            (in_qkv, w_qkv),
+        )
+    ]
+    links.greet([(1, 0), (2, 0), (4, 0), (6, 0), (0, 1), (0, 2)])
+    sums_one = Sums(links, parts, *got_one)
+    for load, block in zip(load_parts, (3, 1, 2, 0)):
+        links.settle(load)
+        sums_one.ready(block)
+    gain_rows[...] = jnp.zeros_like(gain_rows)
+    context[...] = jnp.zeros_like(context)
+    context[:CTX] = conditioning[0]
+    links.settle(load_resid)
+    for load in load_cross:
+        links.settle(load)
+    for pair in range(pairs):
+        at = slice(pair * PAIR, (pair + 1) * PAIR)
+        cross_keys_t[pair] = keyval[0, :, at].astype(jnp.float32).T.astype(low)
+        cross_values_t[pair] = keyval[1, :, at].astype(jnp.float32).T.astype(low)
+    d_cross_keys_t[...] = jnp.zeros_like(d_cross_keys_t)
+    d_cross_values_t[...] = jnp.zeros_like(d_cross_values_t)
+    d_keys_t[...] = jnp.zeros_like(d_keys_t)
+    d_values_t[...] = jnp.zeros_like(d_values_t)
+    sums_one.add()
+    sums_one.arrive()
+
+    def norm_back(which, values, sums):
+        def step(rows):
+            gain = gains[which : which + 1]
+            _, scaled, inverse = layer_norm(values[rows].astype(jnp.float32), gain)
+            d_normed = parts[0, rows].astype(jnp.float32) + sums.total(rows)
+            d_part, gain_grad = norm_backward(d_normed, scaled, inverse, gain)
+            gain_rows[which : which + 1] += gain_grad[None]
+            earlier = cotangent[rows].astype(jnp.float32) if which == 2 else d_resid[rows]
+            d_resid[rows] = earlier + d_part
+            if which > 0:
+                (seed_one if which == 2 else seed_two)[0, rows] = d_resid[rows].astype(low)
+
+        row_steps(BLOCK, step)
+
+    norm_back(2, resid, sums_one)
+    spread_one = Spread(links, seed_one)
+    load_resid = links.store(in_resid_one, resid)
+    sums_one.sent()
+
+    def back_project(source, weight, block, sums):
+        def project(cols):
+            parts[block, :, cols] = dot_cols(source, weight(cols)).astype(low)
+
+        columns(model, 512, project)
+        sums.ready(block)
+
+    sums_two = Sums(links, parts, *got_two)
+    for block in range(4):
+        spread_one.wait(block)
+        rows = block_rows(block)
+        d_crossed = dot_plain(seed_one[block], w_cross[:, width:]).astype(low)
+        for pair in range(pairs):
+            at = slice(pair * PAIR, (pair + 1) * PAIR)
+            out = attend_rows_back(
+                query[rows, at] * low(DH**-0.5), d_crossed[:, at], logs[rows, at], cross_keys_t[pair],
+                cross_values_t[pair], keyval[0, :, at], d_cross_keys_t.at[pair], d_cross_values_t.at[pair], CTX,
+            )
+            query[rows, at] = out.astype(low)
+        back_project(query[rows], lambda cols: w_cross[cols, :width], block, sums_two)
+    sums_two.add()
+    load_logs = links.store(in_logs, logs)
+    for load in load_mid:
+        links.settle(load)
+
+    def whole(rows, cols):
+        return rows[:, :, cols].reshape(LENGTH, -1)
+
+    def grads_into(target, rows, cols, right):
+        def product(part):
+            target[part, cols] = dot_rows(whole(rows, part), right).astype(low)
+
+        columns(model, 384, product)
+
+    for pair in range(pairs):
+        at = slice(pair * PAIR, (pair + 1) * PAIR)
+        d_keyval[:, at] = d_cross_keys_t[pair].T.astype(low)
+        d_keyval[:, width + pair * PAIR : width + (pair + 1) * PAIR] = d_cross_values_t[pair].T.astype(low)
+    context_sum[...] = dot_cols(d_keyval[...], w_keyval[...]).astype(low)
+    context_near = links.go(context_sum, context_got.at[0], 0, 1)
+    w_keyval[...] = dot_rows(context[...], d_keyval[...]).astype(low)
+    scatter_keyval = Scatter(links, w_keyval, core_keyval, extra_keyval, far_keyval, 1)
+    scatter_keyval.pair_up()
+    grads_into(w_cross, rows_two, slice(0, width), query[...])
+    grads_into(w_cross, seed_one, slice(width, 2 * width), crossed[...])
+    scatter_cross = Scatter(links, w_cross, core_cross, extra_cross, far_cross, 1)
+    scatter_cross.pair_up()
+    links.settle(load_resid)
+    context_near.wait_recv()
+    links.settle_sends((context_near,))
+    context_sum[...] = (context_sum[...].astype(jnp.float32) + context_got[0].astype(jnp.float32)).astype(low)
+    scatter_keyval.combine()
+    scatter_cross.combine()
+    load_last = links.store(in_last, rows_two)
+    sums_two.arrive()
+    norm_back(1, resid, sums_two)
+    spread_two = Spread(links, seed_two)
+    sums_two.sent()
+    spread_one.sent()
+    load_rows = links.store(in_rows_one, seed_one)
+    context_far = links.go(context_sum, context_got.at[1], 0, 2)
+    for load in load_self:
+        links.settle(load)
+    links.settle(load_logs)
+    for pair in range(pairs):
+        key = rotated[:, width + pair * PAIR : width + (pair + 1) * PAIR]
+        value = rotated[:, 2 * width + pair * PAIR : 2 * width + (pair + 1) * PAIR]
+        keys_t[pair] = key.astype(jnp.float32).T.astype(low)
+        values_t[pair] = value.astype(jnp.float32).T.astype(low)
+    cosine, sine = (tables.at[part] for part in range(2))
+    sums_last = Sums(links, rows_two, *got_one)
+
+    for block in range(4):
+        spread_two.wait(block)
+        rows = block_rows(block)
+        d_attended[rows] = dot_plain(seed_two[block], w_attn_out[...]).astype(low)
+        turn = (cosine[rows], -sine[rows])
+
+        def one_pair(pair, carry):
+            at = pl.ds(pl.multiple_of(pair * PAIR, PAIR), PAIR)
+            keys_at = pl.ds(pl.multiple_of(width + pair * PAIR, PAIR), PAIR)
+            out = attend_rows_back(
+                rotated[rows, at] * low(DH**-0.5), d_attended[rows, at], logs[rows, at], keys_t[pair],
+                values_t[pair], rotated[:, keys_at], d_keys_t.at[pair], d_values_t.at[pair], None,
+            )
+            rotated[rows, at] = head_turn(out, *turn).astype(low)
+            return carry
+
+        lax.fori_loop(0, pairs, one_pair, 0)
+        if block == 0:
+            scatter_keyval.relay()
+        if block == 1:
+            scatter_cross.relay()
+        if block == 2:
+            links.settle(load_last)
+            for last in (3, 1, 2):
+                sums_last.ready(last)
+    grads_into(w_attn_out, seed_two, slice(None), attended[...])
+    scatter_attn_out = Scatter(links, w_attn_out, core_attn_out, extra_attn_out, far_attn_out, 1)
+    scatter_attn_out.pair_up()
+    for pair in range(pairs):
+        for block in range(4):
+            rows = block_rows(block)
+            turn = (cosine[rows], -sine[rows])
+            at = slice(width + pair * PAIR, width + (pair + 1) * PAIR)
+            rotated[rows, at] = head_turn(d_keys_t[pair, :, rows].T, *turn).astype(low)
+            at = slice(2 * width + pair * PAIR, 2 * width + (pair + 1) * PAIR)
+            rotated[rows, at] = d_values_t[pair, :, rows].T.astype(low)
+    sums_last.add()
+    sums_three = Sums(links, parts, *got_two)
+    for block in (3, 1, 2, 0):
+        back_project(rotated[block_rows(block)], lambda cols: w_qkv[cols, :], block, sums_three)
+    links.settle(load_rows)
+    scatter_attn_out.combine()
+    grads_into(w_qkv, seed_one, slice(None), rotated[...])
+    scatter_qkv = Scatter(links, w_qkv, core_qkv, extra_qkv, far_qkv, 1)
+    scatter_qkv.pair_up()
+    sums_three.add()
+    scatter_qkv.combine()
+    load_resid = links.store(in_resid_two, resid)
+    sums_last.arrive()
+    links.settle(load_resid)
+
+    def add_last(rows):
+        resid[rows] += rows_two[0, rows].astype(jnp.float32) + sums_last.total(rows)
+
+    row_steps(BLOCK, add_last)
+    links.store(resid, block_out)
+    context_far.wait_recv()
+    context_total = context_sum[...].astype(jnp.float32) + context_got[1].astype(jnp.float32)
+    grad_context[0] = context_total[:CTX]
+    scatter_attn_out.relay()
+    scatter_keyval.arrive()
+    scatter_keyval.total(sum_keyval, slice(None))
+    heads = width // DH
+    for head in range(heads):
+        pieces = [sum_keyval[:, start + head * DH : start + (head + 1) * DH] for start in (0, width)]
+        out_keyval[:, 2 * head * DH : 2 * (head + 1) * DH] = jnp.concatenate(pieces, axis=1)
+    links.store(out_keyval, grad_keyval)
+    scatter_cross.arrive()
+    share = out_qkv.shape[0]
+    spot = [logs.at[pl.ds(step * share, share)] for step in range(5)]
+    qkv_spot = spot[3:5] + [sum_last]
+    scatter_cross.total(spot[0], slice(0, width))
+    links.store(spot[0], grad_cross_q)
+    scatter_cross.total(spot[1], slice(width, 2 * width))
+    links.store(spot[1], grad_cross_out)
+    sums_three.arrive()
+    norm_back(0, latents, sums_three)
+    links.store(d_resid, grad_latents)
+    for step, (dp_bit, tensor_bit) in enumerate(((1, 0), (0, 1), (0, 2), (2, 0), (4, 0))):
+        trade = links.remote(gain_rows, gain_got.at[step], dp_bit, tensor_bit)
+        trade.start()
+        if step == 2:
+            scatter_qkv.relay()
+        trade.wait()
+        gain_rows[...] += gain_got[step]
+    grad_gains[...] = gain_rows[...]
+    scatter_attn_out.arrive()
+    scatter_attn_out.total(spot[2], slice(None))
+    links.store(spot[2], grad_attn_out)
+    scatter_qkv.arrive()
+    for part in range(3):
+        scatter_qkv.total(qkv_spot[part], slice(part * width, (part + 1) * width))
+    for pair in range(pairs):
+        heads_of = [qkv_spot[part][:, (2 * pair + which) * DH : (2 * pair + which + 1) * DH] for which in range(2) for part in range(3)]
+        for step in range(3):
+            start = (3 * pair + step) * PAIR
+            out_qkv[:, start : start + PAIR] = jnp.concatenate(heads_of[2 * step : 2 * step + 2], axis=1)
+    links.store(out_qkv, grad_qkv)
+    links.finish()
+    for scatter in (scatter_keyval, scatter_cross, scatter_attn_out, scatter_qkv):
+        scatter.finish()
+
+
+def backward_part(latents, gains, conditioning, cotangent, parts, last, kept):
+    (
+        resid_one, resid_two, w_qkv, w_attn_out, w_cross, w_keyval, rows_one, rows_two, rotated, attended, logs, query,
+        keyval, crossed, cross_logs, tables,
+    ) = kept
+    model = latents.shape[1]
+    depth = conditioning.shape[2]
+    wide = w_qkv.shape[1]
+    width = wide // 3
+    pairs = width // PAIR
+    members = lax.axis_size("dp")
+    share, span = model // members, depth // members
+    low, high = jnp.bfloat16, jnp.float32
+    outs = [
+        ((BLOCK, model), high),
+        ((BLOCK, model), high),
+        (conditioning.shape, high),
+        ((8, model), high),
+        ((share, wide), high),
+        ((share, width), high),
+        ((share, width), high),
+        ((span, 2 * width), high),
+        ((share, width), high),
+    ]
+    work = [
+        ((4, BLOCK, model), low),
+        ((4, BLOCK, model), low),
+        ((4, BLOCK, model), low),
+        ((4, BLOCK, model), low),
+        ((model, wide), low),
+        ((model, width), low),
+        ((model, 2 * width), low),
+        ((depth, 2 * width), low),
+        ((LENGTH, wide), low),
+        ((LENGTH, width), low),
+        ((LENGTH, width), low),
+        ((LENGTH, width), low),
+        ((LENGTH, width), low),
+        ((LENGTH, width), high),
+        ((pairs, PAIR, LENGTH), low),
+        ((pairs, PAIR, LENGTH), low),
+        ((pairs, PAIR, LENGTH), high),
+        ((pairs, PAIR, LENGTH), high),
+        ((pairs, PAIR, FULL), low),
+        ((pairs, PAIR, FULL), low),
+        ((pairs, PAIR, FULL), high),
+        ((pairs, PAIR, FULL), high),
+        ((2, FULL, width), low),
+        ((FULL, 2 * width), low),
+        ((FULL, depth), low),
+        ((FULL, depth), low),
+        ((2, FULL, depth), low),
+        ((BLOCK, model), high),
+        ((BLOCK, model), high),
+        ((2, LENGTH, PAIR), high),
+        ((8, model), high),
+        ((5, 8, model), high),
+    ]
+    groups = [(share, wide), (share, width), (share, 2 * width), (span, 2 * width)]
+    scratch = [pltpu.VMEM(*buffer) for buffer in work] + [sum_buffers(model), sum_buffers(model)]
+    scratch += [pltpu.VMEM((4, *group), low) for group in groups]
+    scratch += [pltpu.VMEM(group, low) for group in groups]
+    scratch += [pltpu.VMEM((3, *group), low) for group in groups]
+    scratch += [pltpu.VMEM(groups[3], high), pltpu.VMEM((share, width), high)]
+    scratch += [pltpu.VMEM(shape, high) for shape in ((share, wide), (span, 2 * width))]
+    scratch += [pltpu.SemaphoreType.DMA((96,)), pltpu.SemaphoreType.DMA((96,)), pltpu.SemaphoreType.DMA((48,))]
+    return pl.pallas_call(
+        backward_kernel,
+        out_shape=[jax.ShapeDtypeStruct(*out) for out in outs],
+        in_specs=[whole_vmem()] * 4 + [anywhere()] * 18,
+        out_specs=[anywhere()] * 2 + [whole_vmem()] * 2 + [anywhere()] * 5,
+        scratch_shapes=scratch,
+        compiler_params=pltpu.CompilerParams(collective_id=2, has_side_effects=True, vmem_limit_bytes=VMEM_BYTES),
+        cost_estimate=pl.CostEstimate(flops=2**37, bytes_accessed=2**26, transcendentals=2**23),
+    )(
+        latents, gains, conditioning, cotangent, parts, last, resid_one, resid_two, w_qkv, w_attn_out, w_cross,
+        w_keyval, rows_one, rows_two, rotated, attended, logs, query, keyval, crossed, cross_logs, tables,
+    )
+
+
 def per_device(
     latents,
     conditioning,
@@ -836,25 +1288,19 @@
     cotangent,
 ):
     low = jnp.bfloat16
-    heads_wide = w_cross_q.shape[1]
     hidden_wide = w_gate.shape[1]
-    members = lax.axis_size("dp")
-    context = conditioning[0]
+    gains = jnp.stack([gain_attn, gain_cross, gain_mlp])
     (
         rows_one, rows_two, rows_three, mlp_seed, qkv_all, attn_out_t, cross_all, cross_kv, mlp_all, down_all,
         rotated, attended, logs, cross_query, keyval, crossed, cross_logs, resid_one, resid_two, tables,
     ) = forward_part(
         latents,
-        jnp.stack([gain_attn, gain_cross, gain_mlp]),
+        gains,
         conditioning,
-        (w_qkv, w_attn_out, w_cross_q, w_cross_kv, w_cross_out, w_gate, w_up, w_down),
+        (w_qkv, w_attn_out.T, w_cross_q, w_cross_kv, w_cross_out.T, w_gate, w_up, w_down.T),
         cotangent,
     )
-    rows_one, rows_two, rows_three, mlp_seed = (
-        array.reshape(LENGTH, -1) for array in (rows_one, rows_two, rows_three, mlp_seed)
-    )
-    cross_q, cross_out_t = cross_all[:, :heads_wide], cross_all[:, heads_wide:]
-    head_shape = (-1, heads_wide // DH, DH)
+    rows_three, mlp_seed = (array.reshape(LENGTH, -1) for array in (rows_three, mlp_seed))
     both = dot_plain(rows_three, mlp_all)
     gate_pre, up_pre = both[:, :hidden_wide], both[:, hidden_wide:]
     sigma_gate = jax.nn.sigmoid(gate_pre)
@@ -865,62 +1311,30 @@
     d_gate = (d_hidden * up_pre * sigma_gate * (1.0 + gate_pre * (1.0 - sigma_gate))).astype(low)
     d_up = (d_hidden * swish).astype(low)
     d_both = jnp.concatenate([d_gate, d_up], axis=1)
-    sum_mlp = dp_sum(after(dot_rows(rows_three, d_both), sum_down))
-    d_normed = sum_rows(dot_cols(d_both, mlp_all))
-    _, scaled_three, inverse_three = layer_norm(resid_two, gain_mlp)
-    d_part, gain_grad_three = norm_backward(d_normed, scaled_three, inverse_three, gain_mlp)
-    d_resid = cotangent.astype(jnp.float32) + d_part
-    block_out = resid_two + sum_rows(dot_cols(hidden, down_all))
-    cross_seed = spread_rows(d_resid.astype(low))
-    grad_cross_out = dot_rows(cross_seed, crossed)
-    d_crossed = dot_plain(cross_seed, cross_out_t).astype(low).reshape(head_shape)
-    cross_log_heads = cross_logs.reshape(LENGTH, -1, DH)[:, :, 0].T[:, :, None]
-    d_query, d_key, d_value = cross_backward(
-        cross_query.reshape(head_shape),
-        keyval[0, :CTX].reshape(head_shape),
-        keyval[1, :CTX].reshape(head_shape),
-        d_crossed,
-        cross_log_heads,
-    )
-    d_query = d_query.reshape(-1, heads_wide).astype(low)
-    d_key, d_value = (array.reshape(CTX, -1).astype(low) for array in (d_key, d_value))
-    grad_cross_q = dot_rows(rows_two, d_query)
-    d_keyval = jnp.concatenate([d_key, d_value], axis=1)
-    grad_kv = dot_rows(context, d_keyval).astype(low)
-    grad_kv = jnp.concatenate([grad_kv.reshape(members, -1, 2, heads_wide)[:, :, part] for part in range(2)], axis=1)
-    context_part = dot_cols(d_keyval, cross_kv)
-    d_normed = sum_rows(dot_cols(d_query, cross_q))
-    _, scaled_two, inverse_two = layer_norm(resid_one, gain_cross)
-    d_part, gain_grad_two = norm_backward(d_normed, scaled_two, inverse_two, gain_cross)
-    d_resid = d_resid + d_part
-    self_seed = spread_rows(d_resid.astype(low))
-    grad_attn_out = dot_rows(self_seed, attended)
-    grad_mid = jnp.concatenate([grad.astype(low) for grad in (grad_attn_out, grad_cross_q, grad_cross_out, grad_kv.reshape(-1, heads_wide))], axis=1)
-    sum_mid = dp_sum(after(grad_mid, sum_mlp))
-    d_attended = dot_plain(self_seed, attn_out_t).astype(low)
-    d_packed = attend_back(rotated, d_attended, logs, tables)
-    sum_qkv = dp_sum(after(dot_rows(rows_one, d_packed), sum_mid))
-    d_normed = sum_rows(dot_cols(d_packed, qkv_all))
-    _, scaled_one, inverse_one = layer_norm(latents.astype(jnp.float32), gain_attn)
-    d_part, gain_grad_one = norm_backward(d_normed, scaled_one, inverse_one, gain_attn)
-    grad_latents = d_resid + d_part
-    grad_context = lax.psum(context_part.astype(low), "tensor").astype(jnp.float32)[None]
-    gains = lax.psum(jnp.stack([gain_grad_one, gain_grad_two, gain_grad_three]), ("dp", "tensor"))
-    sums = [sum_mid[:, part * heads_wide : (part + 1) * heads_wide].astype(jnp.float32) for part in range(4)]
-    half = sums[3].shape[0] // 2
-    sum_kv = jnp.concatenate([sums[3][:half], sums[3][half:]], axis=1)
+    sum_mlp = dp_sum(dot_rows(rows_three, d_both))
+    block_shape = (4, latents.shape[0], -1)
+    parts = dot_cols(d_both, mlp_all).astype(low).reshape(block_shape)
+    last = dot_cols(hidden, down_all).astype(low).reshape(block_shape)
+    kept = (
+        resid_one, resid_two, qkv_all, attn_out_t, cross_all, cross_kv, rows_one, rows_two, rotated, attended, logs,
+        cross_query, keyval, crossed, cross_logs, tables,
+    )
+    (
+        block_out, grad_latents, grad_context, grad_gains, grad_qkv, grad_attn_out, grad_cross_q, grad_cross_kv,
+        grad_cross_out,
+    ) = backward_part(latents, gains, conditioning, cotangent, parts, last, kept)
     return (
         block_out,
         grad_latents,
         grad_context,
-        gains[0],
-        by_head(sum_qkv, 3).astype(jnp.float32),
-        sums[0].T,
-        gains[1],
-        sums[1],
-        by_head(sum_kv, 2),
-        sums[2].T,
-        gains[2],
+        grad_gains[0],
+        grad_qkv,
+        grad_attn_out.T,
+        grad_gains[1],
+        grad_cross_q,
+        grad_cross_kv,
+        grad_cross_out.T,
+        grad_gains[2],
         sum_mlp[:, :hidden_wide].astype(jnp.float32),
         sum_mlp[:, hidden_wide:].astype(jnp.float32),
         sum_down.astype(jnp.float32).T,

time: 669 us -> 542 us (0.81)
  Pallas kernels: 239 us -> 429 us
  waiting for transfers between devices: 135 us -> 0.04 us
  blocking collectives: 43.7 us -> 0 us
  matrix products: 111 us -> 69.7 us
  local copies, waits for them, and re-layouts: 47 us -> 13.9 us
  starting transfers between devices: 30.2 us -> 0.08 us
  other arithmetic: 35.8 us -> 5.89 us
    pallas_call x1, Pallas kernels: 28.7 us -> 217 us  [backward_part(): pl.pallas_call(backward_kernel, out_shape=[jax.ShapeDtypeStruct(*out) for...]
    ppermute x24 -> x0, waiting for transfers between devices: 88.2 us -> none  [swap(): lax.ppermute(values, 'tensor', [(member, member ^ bit) for member in rang...]
    psum x1 -> x0, blocking collectives: 43.7 us -> none  [per_device(): lax.psum(jnp.stack([gain_grad_one, gain_grad_two, gain_grad_three]), ('dp...]
    reduce_scatter x3 -> x2, waiting for transfers between devices: 31.7 us -> 0.01 us  [dp_sum(): lax.psum_scatter(grads.astype(jnp.bfloat16), 'dp', scatter_dimension=0, t...]
    ppermute x24 -> x0, starting transfers between devices: 30 us -> none  [swap(): lax.ppermute(values, 'tensor', [(member, member ^ bit) for member in rang...]
    dot_general x4 -> x2, matrix products: 39 us -> 23.1 us  [dot_plain(): return jnp.dot(left_op, right_op, preferred_element_type=jnp.float32)]
    unnamed x6 -> x2, waiting for transfers between devices: 15.2 us -> 0.03 us
    unnamed x116 -> x36, local copies, waits for them, and re-layouts: 25.1 us -> 10.2 us
  transfers between devices with their start and end apart: 29 -> 2, of which waited for: 21 -> 0; matrix products, arithmetic and copies ran while one was open for 20% -> 8% of each run, Pallas kernels for 4% -> 41%
where the time goes in v3:
time: 542 us; the launch traced here: 533 us
  Pallas kernels  429 us (79%)
  matrix products  69.7 us (13%)
  between operations  14.4 us (3%)
  local copies, waits for them, and re-layouts  13.9 us (3%)
  other arithmetic  5.89 us (1%)
    pallas_call x1, Pallas kernels, backward_part(): pl.pallas_call(backward_kernel, out_shape=[jax.ShapeDtypeStruct(*out) for...  217 us
    pallas_call x1, Pallas kernels, forward_part(): pl.pallas_call(forward_kernel, out_shape=[jax.ShapeDtypeStruct(*out) for...  212 us
    dot_general x2, matrix products, dot_rows(): lax.dot_general(left_op, right_op, (((0,), (0,)), ((), ())), preferred_el...  23.9 us
    dot_general x2, matrix products, dot_plain(): return jnp.dot(left_op, right_op, preferred_element_type=jnp.float32)  23.1 us
    dot_general x2, matrix products, dot_cols(): lax.dot_general(left_op, right_op, (((1,), (1,)), ((), ())), preferred_el...  22.6 us
  transfers between devices with their start and end apart: 2, of which 0 were waited for; matrix products, arithmetic and copies ran while one was open for 8% of the time, Pallas kernels for 41%

profile of v3, /device:TPU:0, one launch (start us, length us, event | category | flops | bytes accessed | tf_op | source)
XLA Modules:
  0.0 532.9 jit_solution(9385604549846345045)
XLA Ops:
  7.2 0.0 reduce-scatter.5.cloned.1.call-start
  7.2 0.7 stack.12
  7.9 0.7 stack.13
  8.6 0.7 stack.14
  9.3 0.6 pad_maximum_fusion.5.gains
  10.0 212.0 %shard_map.245 = (bf16[4,256,1536]{2,1,0:T(8,128)(2,1)}, bf16[4,256,1536]{2,1,0:T(8,128)(2,1)}, bf16[4,256,1536]{2,1,0:T(8,128)(2,1)}, bf16[4,256,1536]{2,1,0:T(...) custom-call(bf16[256,1536]{1,0:T(8,128)(2,1)} %latents.3, ...), custom_call_target="tpu_custom_call" | custom-call | flops 137438953472 | bytes 67108864 | tf_op jit(solution)/shard_map/pallas_call | solution.py:828
  222.0 13.5 %fusion.5 = f32[1024,3072]{1,0:T(8,128)S(1)} fusion(bf16[1024,1536]{1,0:T(8,128)(2,1)} %bitcast.26, bf16[1536,3072]{1,0:T(8,128)(2,1)} %get-tuple-element.46), kind=kOutput, calls=%fused_computation.20 | convolution fusion | flops 9663676416 | bytes 25165824 | tf_op jit(solution)/shard_map/dot_general | solution.py:186
  235.5 0.0 copy-done.8
  235.5 0.0 copy-done.10
  235.5 9.6 %multiply_convert_fusion.2 = (bf16[1024,1536]{1,0:T(8,128)(2,1)}, bf16[1024,1536]{1,0:T(8,128)(2,1)}, bf16[1024,1536]{1,0:T(8,128)(2,1)}) fusion(f32[1024,3072]{1,0:T(8,128)S(1)} %fusion.5, bf16[1024,1536]{1,0:T(8,128)(2,1)S(1)} %bitcast.30, bf16[1536,1536]{1,0:T(8,128)(2,1)S(1)} %copy-done.10), kind=kOutput, calls=%fused_computation.5 | convolution fusion | flops 4855431168 | bytes 29884416 | tf_op jit(solution)/shard_map/dot_general | solution.py:186
  245.1 8.7 %convolution_convert_fusion.1 = bf16[1536,1536]{1,0:T(8,128)(2,1)} fusion(bf16[1024,1536]{1,0:T(8,128)(2,1)S(1)} %bitcast.31, bf16[1024,1536]{1,0:T(8,128)(2,1)} %get-tuple-element.91), kind=kOutput, calls=%fused_computation.1 | convolution fusion | flops 4834197504 | bytes 11010048 | tf_op jit(solution)/shard_map/dot_general | solution.py:190
  253.8 0.0 reduce-scatter.5.cloned.1.call-update
  253.8 0.0 reduce-scatter.3.cloned.1.call-start
  253.9 1.8 copy-done.7
  255.7 15.2 %convolution_convert_fusion = bf16[1536,3072]{1,0:T(8,128)(2,1)} fusion(bf16[1024,1536]{1,0:T(8,128)(2,1)S(1)} %bitcast.27, bf16[1024,1536]{1,0:T(8,128)(2,1)} %get-tuple-element.90, bf16[1024,1536]{1,0:T(8,128)(2,1)} %get-tuple-element.89), kind=kOutput, calls=%fused_computation | convolution fusion | flops 9680977920 | bytes 18874368 | tf_op jit(solution)/shard_map/dot_general | solution.py:190
  270.9 0.0 reduce-scatter.3.cloned.1.call-update
  270.9 0.0 slice-start.1
  271.0 0.0 slice-start.2
  271.0 9.5 %convolution_convert_fusion.2 = bf16[1024,1536]{1,0:T(8,128)(2,1)} fusion(bf16[1024,1536]{1,0:T(8,128)(2,1)} %get-tuple-element.91, bf16[1536,1536]{1,0:T(8,128)(2,1)} %get-tuple-element.44), kind=kOutput, calls=%fused_computation.9 | convolution fusion | flops 4833411072 | bytes 11010048 | tf_op jit(solution)/shard_map/dot_general | solution.py:196
  280.5 13.2 %fusion.2 = bf16[1024,1536]{1,0:T(8,128)(2,1)} fusion(bf16[1536,3072]{1,0:T(8,128)(2,1)S(1)} %bitcast.33, bf16[1024,1536]{1,0:T(8,128)(2,1)} %get-tuple-element.90, bf16[1024,1536]{1,0:T(8,128)(2,1)S(1)} %copy-done.9), kind=kOutput, calls=%fused_computation.10 | convolution fusion | flops 9677832192 | bytes 18874368 | tf_op jit(solution)/shard_map/dot_general | solution.py:196
  293.6 217.0 %shard_map.246 = (f32[256,1536]{1,0:T(8,128)}, f32[256,1536]{1,0:T(8,128)}, f32[1,130,768]{2,1,0:T(8,128)}, f32[8,1536]{1,0:T(8,128)}, f32[192,1152]{1,0:T(8,128...) custom-call(bf16[256,1536]{1,0:T(8,128)(2,1)} %latents.3, ...), custom_call_target="tpu_custom_call" | custom-call | flops 137438953472 | bytes 67108864 | tf_op jit(solution)/shard_map/pallas_call | solution.py:1260
  510.7 2.3 copy.28
  513.0 1.6 slice_reduce_fusion
  514.5 2.2 convert_bitcast_fusion
  516.8 3.1 slice_convert_fusion
  519.8 1.1 copy.36
  521.0 1.1 copy.37
  522.1 0.9 copy.38
  523.0 0.7 copy.39
  523.8 0.7 copy.40
  524.5 0.7 copy.41
  525.2 0.7 copy.42
  (26 shorter events, 0.0 us)
Async XLA Ops:
  7.2 507.4 %reduce-scatter.5.cloned.1.call-start = ((), (), s32[]{:S(2)}) async-start(), calls=%async_computation.3 | async-start | bytes 5308416 | tf_op jit(solution)/shard_map/reduce_scatter | solution.py:305
  221.9 13.6 %copy-start.8 = (bf16[4,256,1536]{2,1,0:T(8,128)(2,1)S(1)}, bf16[4,256,1536]{2,1,0:T(8,128)(2,1)}, u32[]{:S(2)}) copy-start(bf16[4,256,1536]{2,1,0:T(8,128)(2,1)} %get-tuple-element.43) | copy-start | bytes 9437188
  222.0 13.6 %copy-start.10 = (bf16[1536,1536]{1,0:T(8,128)(2,1)S(1)}, bf16[1536,1536]{1,0:T(8,128)(2,1)}, u32[]{:S(2)}) copy-start(bf16[1536,1536]{1,0:T(8,128)(2,1)} %get-tuple-element.44) | copy-start | bytes 14155780
  253.8 1.9 copy-start.7
  253.8 262.9 %reduce-scatter.3.cloned.1.call-start = ((), (), s32[]{:S(2)}) async-start(), calls=%async_computation.2 | async-start | bytes 10616832 | tf_op jit(solution)/shard_map/reduce_scatter | solution.py:305
  270.9 9.5 %slice-start = ((s8[9437184]{0:T(1024)(128)(4,1)}), s8[1048576]{0:T(1024)(128)(4,1)S(1)}, s32[]{:S(2)}) async-start(s8[9437184]{0:T(1024)(128)(4,1)} %bitcast.32), calls=%async_computation.4 | async-start | bytes 2097152
  270.9 9.5 %slice-start.1 = ((s8[9437184]{0:T(1024)(128)(4,1)}), s8[4194304]{0:T(1024)(128)(4,1)S(1)}, s32[]{:S(2)}) async-start(s8[9437184]{0:T(1024)(128)(4,1)} %bitcast.32), calls=%async_computation.5 | async-start | bytes 8388608
  271.0 9.5 %slice-start.2 = ((s8[9437184]{0:T(1024)(128)(4,1)}), s8[4194304]{0:T(1024)(128)(4,1)S(1)}, s32[]{:S(2)}) async-start(s8[9437184]{0:T(1024)(128)(4,1)} %bitcast.32), calls=%async_computation.6 | async-start | bytes 8388608
  271.0 9.5 %copy-start.9 = (bf16[1024,1536]{1,0:T(8,128)(2,1)S(1)}, bf16[1024,1536]{1,0:T(8,128)(2,1)}, u32[]{:S(2)}) copy-start(bf16[1024,1536]{1,0:T(8,128)(2,1)} %get-tuple-element.89) | copy-start | bytes 9437188
  510.7 9.1 %copy-start.1 = (f32[256,1536]{1,0:T(8,128)S(1)}, f32[256,1536]{1,0:T(8,128)}, u32[]{:S(2)}) copy-start(f32[256,1536]{1,0:T(8,128)} %get-tuple-element.108) | copy-start | bytes 4718596
  516.8 4.2 copy-start
  519.8 2.3 copy-start.2
  521.0 2.1 copy-start.6
  521.0 2.8 copy-start.5
  521.0 3.5 copy-start.4
  521.0 4.2 copy-start.3
Sparse Core Ops, SparseCore 0:
  253.9 54.0 reduce-scatter.4
  310.4 104.9 reduce-scatter.2

commit v4 on v3

--- a/solution.py
+++ b/solution.py
@@ -312,7 +312,7 @@
 MESH = pl.DeviceIdType.MESH
 BLOCK = LENGTH // 4
 HALF = BLOCK // 2
-FULL = 256
+FULL = 160
 
 
 class Links:
@@ -374,21 +374,25 @@
 class Spread:
     def __init__(self, links, rows):
         self.links, self.rows = links, rows
-        self.near = links.go(rows.at[0], rows.at[1], 0, 1)
-        self.far = links.go(rows.at[0], rows.at[2], 0, 2)
+        half = rows.shape[1] // 2
+        self.low, self.high = pl.ds(0, half), pl.ds(half, half)
+        self.near_low = links.go(rows.at[0, self.low], rows.at[1, self.low], 0, 1)
+        self.far_high = links.go(rows.at[0, self.high], rows.at[2, self.high], 0, 2)
+        self.near_high = links.go(rows.at[0, self.high], rows.at[1, self.high], 0, 1)
+        self.far_low = links.go(rows.at[0, self.low], rows.at[2, self.low], 0, 2)
         self.stage = 0
 
     def wait(self, block):
-        rows, links = self.rows, self.links
+        rows, links, low, high = self.rows, self.links, self.low, self.high
         if block >= 1 and self.stage == 0:
-            self.near.wait_recv()
-            low = pl.ds(0, HALF)
+            self.near_low.wait_recv()
             self.last_low = links.go(rows.at[1, low], rows.at[3, low], 0, 2)
+            self.far_high.wait_recv()
+            self.last_high = links.go(rows.at[2, high], rows.at[3, high], 0, 1)
+            self.near_high.wait_recv()
             self.stage = 1
         if block >= 2 and self.stage == 1:
-            self.far.wait_recv()
-            high = pl.ds(HALF, HALF)
-            self.last_high = links.go(rows.at[2, high], rows.at[3, high], 0, 1)
+            self.far_low.wait_recv()
             self.stage = 2
         if block >= 3 and self.stage == 2:
             self.last_low.wait_recv()
@@ -396,18 +400,53 @@
             self.stage = 3
 
     def sent(self):
-        self.links.settle_sends((self.near, self.far, self.last_low, self.last_high))
+        self.links.settle_sends(
+            (self.near_low, self.far_high, self.near_high, self.far_low, self.last_low, self.last_high)
+        )
+
+
+class SpreadCross:
+    def __init__(self, links, weights):
+        self.links, self.weights = links, weights
+        self.which = links.dp % 2
+        self.near = links.go(self.half(0), self.half(1), 0, 1)
+        self.far = links.go(self.half(0), self.half(2), 0, 2)
+        self.core = [self.cross(0)]
+
+    def half(self, member, places=slice(None)):
+        return self.weights.at[member, places, self.which]
+
+    def cross(self, member):
+        return self.links.go(self.half(member), self.half(member), 1, 0)
+
+    def pump(self):
+        links = self.links
+        first, second = pl.ds(0, 2), pl.ds(2, 2)
+        self.near.wait_recv()
+        self.last_low = links.go(self.half(1, first), self.half(3, first), 0, 2)
+        self.core.append(self.cross(1))
+        self.far.wait_recv()
+        self.last_high = links.go(self.half(2, second), self.half(3, second), 0, 1)
+        self.core.append(self.cross(2))
+
+    def wait(self, member):
+        if member == 3:
+            self.last_low.wait_recv()
+            self.last_high.wait_recv()
+            self.core.append(self.cross(3))
+        self.core[member].wait_recv()
 
 
 class Gather:
-    def __init__(self, links, shard, whole):
-        self.links, self.whole = links, whole
+    def __init__(self, links, shard, whole, both_cores=True):
+        self.links, self.whole, self.both_cores = links, whole, both_cores
         self.size = shard.shape[0]
         self.place = links.dp // 2
         self.middle = (self.place == 1) | (self.place == 2)
         own = self.rows(0)
         self.own = links.store(shard, own)
-        self.core = [links.go(shard, own, 1, 0)]
+        self.core = []
+        self.pass_on(shard, own)
         self.beside = links.go(shard, own, 2, 0)
         self.skip = links.go(shard, own, 4, 0)
         self.third_at = links.used
@@ -417,7 +456,13 @@
         def _():
             self.third.start()
 
+    def pass_on(self, src, dst):
+        if self.both_cores:
+            self.core.append(self.links.go(src, dst, 1, 0))
+
     def rows(self, step):
+        if len(self.whole.shape) == 4:
+            return self.whole.at[self.place ^ step, self.links.dp % 2]
         start = pl.multiple_of((self.links.dp ^ (2 * step)) * self.size, self.size)
         return self.whole.at[pl.ds(start, self.size)]
 
@@ -439,16 +484,16 @@
         def _():
             self.onward.start()
 
-        self.core.append(links.go(block, block, 1, 0))
+        self.pass_on(block, block)
 
     def arrive(self):
         links = self.links
         self.beside.wait_recv()
         block = self.rows(1)
-        self.core.append(links.go(block, block, 1, 0))
+        self.pass_on(block, block)
         self.third.wait_recv()
         block = self.rows(3)
-        self.core.append(links.go(block, block, 1, 0))
+        self.pass_on(block, block)
         links.settle(self.own)
         for copy in self.core:
             copy.wait_recv()
@@ -464,7 +509,8 @@
     def __init__(self, links, parts, half_near, half_far, near, far):
         self.links, self.parts = links, parts
         self.half_near, self.half_far, self.near, self.far = half_near, half_far, near, far
-        self.low, self.high = pl.ds(0, HALF), pl.ds(HALF, HALF)
+        half = parts.shape[1] // 2
+        self.low, self.high = pl.ds(0, half), pl.ds(half, half)
 
     def ready(self, block):
         links, parts, low, high = self.links, self.parts, self.low, self.high
@@ -476,17 +522,29 @@
         if block == 2:
             self.far_high = links.go(parts.at[2, high], self.far.at[high], 0, 2)
 
+    def add_half(self, block, start, got):
+        def add(rows, from_rows):
+            total = self.parts[block, rows].astype(jnp.float32) + got[from_rows].astype(jnp.float32)
+            self.parts[block, rows] = total.astype(jnp.bfloat16)
+
+        half = got.shape[0]
+        step = math.gcd(half, 32)
+
+        def body(index, carry):
+            at = index * step if step == 1 else pl.multiple_of(index * step, step)
+            add(pl.ds(start + at, step), pl.ds(at, step))
+            return carry
+
+        lax.fori_loop(0, half // step, body, 0)
+
     def add(self):
         links, parts, low, high = self.links, self.parts, self.low, self.high
+        half = parts.shape[1] // 2
         self.first.wait_recv()
-        parts[2, low] = (parts[2, low].astype(jnp.float32) + self.half_near[...].astype(jnp.float32)).astype(
-            jnp.bfloat16
-        )
+        self.add_half(2, 0, self.half_near)
         self.far_low = links.go(parts.at[2, low], self.far.at[low], 0, 2)
         self.second.wait_recv()
-        parts[1, high] = (parts[1, high].astype(jnp.float32) + self.half_far[...].astype(jnp.float32)).astype(
-            jnp.bfloat16
-        )
+        self.add_half(1, half, self.half_far)
         self.near_high = links.go(parts.at[1, high], self.near.at[high], 0, 1)
 
     def arrive(self):
@@ -525,6 +583,16 @@
     return jnp.where(low, outs[0], outs[1]), jnp.where(low, logs[0], logs[1])
 
 
+def cross_tile(weights, member, place, cols):
+    tile = weights[member, place, :, :, cols]
+    return tile.reshape(-1, tile.shape[-1])
+
+
+def cross_columns(weights, member, cols):
+    whole = weights[member, :, :, :, cols]
+    return whole.reshape(-1, whole.shape[-1])
+
+
 def row_steps(total, body):
     def step(index, carry):
         body(pl.ds(pl.multiple_of(index * 32, 32), 32))
@@ -558,17 +626,18 @@
 def forward_kernel(
     latents, gains, conditioning, f32_qkv,
     f32_attn_out, f32_cross_q, f32_cross_kv, f32_cross_out, f32_gate, f32_up, f32_down, cotangent,
-    rows_one_out, rows_two_out, rows_three_out, seeds_out, qkv_out, attn_out_out, cross_out, keyval_w_out, mlp_out,
+    rows_one_out, normed_two_out, rows_three_out, seeds_out, qkv_out, attn_out_out, cross_out, keyval_w_out, mlp_out,
     down_out, rotated_out, attended_out, logs_out,
     query_out, keyval_out, crossed_out, cross_logs_out, resid_one_out, resid_two_out, tables_out,
-    rows_one, rows_two, rows_three, w_qkv, w_attn_out, w_cross, w_keyval, rotated, attended, logs, query, keyval,
-    crossed, cross_logs, keys_t, cross_keys_t, parts, got_one, got_two, resid_one, resid_two,
+    rows_one, normed_two, rows_three, w_qkv, w_attn_out, w_cross, w_keyval, rotated, attended, logs, query, keyval,
+    crossed, cross_logs, keys_t, parts, got_one, resid_one, resid_two,
     packed, tables, context, raw_attn_out, raw_cross_q, raw_cross_kv, raw_cross_out, raw_gate, raw_up, raw_down,
     own_qkv, own_attn_out, own_cross, own_keyval, own_mlp, own_down, send, recv, local,
 ):
     low = jnp.bfloat16
     pairs = attended.shape[1] // PAIR
     width = pairs * PAIR
+    share = own_qkv.shape[0]
     links = Links(send, recv, local)
     loads = [
         links.store(source, target)
@@ -611,7 +680,7 @@
     spread_one.wait(1)
     gather_qkv.forward()
     gather_attn_out = Gather(links, own_attn_out, w_attn_out)
-    gather_cross = Gather(links, own_cross, w_cross)
+    gather_cross = Gather(links, own_cross, w_cross.at[0], False)
     gather_keyval = Gather(links, own_keyval, w_keyval)
     spread_one.wait(2)
     gather_qkv.arrive()
@@ -668,6 +737,8 @@
             gather_mlp = Gather(links, own_mlp, mlp_out)
         if block == 2:
             sums_one.add()
+    gather_cross.arrive()
+    spread_cross = SpreadCross(links, w_cross)
     links.store(attended, attended_out)
     links.store(logs, logs_out)
     sums_one.arrive()
@@ -675,52 +746,53 @@
     def norm_two(rows):
         value = latents[rows].astype(jnp.float32) + parts[0, rows].astype(jnp.float32) + sums_one.total(rows)
         resid_one[rows] = value
-        rows_two[0, rows] = layer_norm(value, gains[1:2])[0].astype(low)
+        normed_two[rows] = layer_norm(value, gains[1:2])[0].astype(low)
 
     row_steps(BLOCK, norm_two)
-    spread_two = Spread(links, rows_two)
     links.store(resid_one, resid_one_out)
+    links.store(normed_two, normed_two_out)
     gather_keyval.arrive()
     links.store(w_keyval, keyval_w_out)
-    for part in range(2):
-        keyval[part] = dot_plain(context[...], w_keyval[:, part * width : (part + 1) * width]).astype(low)
-    for pair in range(pairs):
-        at = slice(pair * PAIR, (pair + 1) * PAIR)
-        cross_keys_t[pair] = keyval[0, :, at].astype(jnp.float32).T.astype(low)
+    keyval[0] = dot_plain(context[...], w_keyval[...]).astype(low)
+    spread_keyval = Spread(links, keyval)
+    spread_cross.pump()
+    resid_two[...] = resid_one[...]
+    for member in range(4):
+        spread_cross.wait(member)
+        spread_keyval.wait(member)
+        at_member = slice(member * width, (member + 1) * width)
+        query[:, at_member] = dot_plain(normed_two[...], cross_columns(w_cross, member, slice(0, width))).astype(low)
+        for pair in range(pairs):
+            at = slice(member * width + pair * PAIR, member * width + (pair + 1) * PAIR)
+            keys_at = slice(pair * PAIR, (pair + 1) * PAIR)
+            values_at = slice(width + pair * PAIR, width + (pair + 1) * PAIR)
+            key_t = keyval[member, :, keys_at].astype(jnp.float32).T.astype(low)
+            out, log = attend_rows(query[:, at] * low(DH**-0.5), key_t, keyval[member, :, values_at], CTX)
+            crossed[:, at] = out.astype(low)
+            cross_logs[:, at] = log
+        for place in range(4):
+            at = slice(place * 2 * share, (place + 1) * 2 * share)
+            tile = cross_tile(w_cross, member, place, slice(width, 2 * width))
+            resid_two[:, at] += dot_cols(crossed[:, at_member], tile)
+        if member == 1:
+            gather_mlp.forward()
+            gather_down = Gather(links, own_down, down_out)
+    links.store(w_cross, cross_out)
     links.store(keyval, keyval_out)
-    gather_cross.arrive()
-    links.store(w_cross, cross_out)
-    sums_one.sent()
-    sums_two = Sums(links, parts, *got_two)
-    for block in range(4):
-        spread_two.wait(block)
-        rows = block_rows(block)
-        query[rows] = dot_plain(rows_two[block], w_cross[:, :width]).astype(low)
-        for pair in range(pairs):
-            at = slice(pair * PAIR, (pair + 1) * PAIR)
-            out, log = attend_rows(query[rows, at] * low(DH**-0.5), cross_keys_t[pair], keyval[1, :, at], CTX)
-            crossed[rows, at] = out.astype(low)
-            cross_logs[rows, at] = log
-        out_project(crossed, block, lambda cols: w_cross[cols, width:], sums_two)
-    sums_two.add()
-    links.store(rows_two, rows_two_out)
     links.store(query, query_out)
     links.store(crossed, crossed_out)
     links.store(cross_logs, cross_logs_out)
+    links.store(resid_two, resid_two_out)
+
+    def norm_three(rows):
+        rows_three[0, rows] = layer_norm(resid_two[rows], gains[2:3])[0].astype(low)
+
+    row_steps(BLOCK, norm_three)
+    spread_three = Spread(links, rows_three)
     links.settle(seed_own)
     spread_seed = Spread(links, seeds_out)
-    gather_mlp.forward()
-    gather_down = Gather(links, own_down, down_out)
-    sums_two.arrive()
-
-    def norm_three(rows):
-        value = resid_one[rows] + parts[0, rows].astype(jnp.float32) + sums_two.total(rows)
-        resid_two[rows] = value
-        rows_three[0, rows] = layer_norm(value, gains[2:3])[0].astype(low)
-
-    row_steps(BLOCK, norm_three)
-    spread_three = Spread(links, rows_three)
-    links.store(resid_two, resid_two_out)
+    spread_three.wait(1)
+    spread_seed.wait(1)
     spread_seed.wait(2)
     spread_three.wait(2)
     gather_down.forward()
@@ -763,43 +835,42 @@
     share = w_qkv.shape[0]
     outs = [
         ((4, BLOCK, model), low),
-        ((4, BLOCK, model), low),
+        ((BLOCK, model), low),
         ((4, BLOCK, model), low),
         ((4, BLOCK, model), low),
         ((model, wide), low),
         ((model, width), low),
-        ((model, 2 * width), low),
+        ((4, 4, 2, share, 2 * width), low),
         ((depth, 2 * width), low),
         ((model, 2 * hidden), low),
         ((model, hidden), low),
         ((LENGTH, wide), low),
         ((LENGTH, width), low),
         ((LENGTH, width), high),
-        ((LENGTH, width), low),
-        ((2, FULL, width), low),
-        ((LENGTH, width), low),
-        ((LENGTH, width), high),
+        ((BLOCK, model), low),
+        ((4, FULL, 2 * width), low),
+        ((BLOCK, model), low),
+        ((BLOCK, model), high),
         ((BLOCK, model), high),
         ((BLOCK, model), high),
         ((2, LENGTH, PAIR), high),
     ]
     work = [
         ((4, BLOCK, model), low),
-        ((4, BLOCK, model), low),
+        ((BLOCK, model), low),
         ((4, BLOCK, model), low),
         ((model, wide), low),
         ((model, width), low),
-        ((model, 2 * width), low),
+        ((4, 4, 2, share, 2 * width), low),
         ((depth, 2 * width), low),
         ((LENGTH, wide), low),
         ((LENGTH, width), low),
         ((LENGTH, width), high),
-        ((LENGTH, width), low),
-        ((2, FULL, width), low),
-        ((LENGTH, width), low),
-        ((LENGTH, width), high),
+        ((BLOCK, model), low),
+        ((4, FULL, 2 * width), low),
+        ((BLOCK, model), low),
+        ((BLOCK, model), high),
         ((pairs, PAIR, LENGTH), low),
-        ((pairs, PAIR, FULL), low),
         ((4, BLOCK, model), low),
     ]
     more = [
@@ -822,7 +893,7 @@
         ((share, 2 * hidden), low),
         ((share, hidden), low),
     ]
-    scratch = [pltpu.VMEM(*buffer) for buffer in work] + [sum_buffers(model), sum_buffers(model)]
+    scratch = [pltpu.VMEM(*buffer) for buffer in work] + [sum_buffers(model)]
     scratch += [pltpu.VMEM(*buffer) for buffer in more]
     scratch += [pltpu.SemaphoreType.DMA((96,)), pltpu.SemaphoreType.DMA((96,)), pltpu.SemaphoreType.DMA((40,))]
     return pl.pallas_call(
@@ -837,13 +908,15 @@
 
 
 class Scatter:
-    def __init__(self, links, grads, got_core, extra, got, core_bit):
+    def __init__(self, links, grads, got_core, extra, got):
         self.links, self.grads, self.got_core, self.extra, self.got = links, grads, got_core, extra, got
         self.size = got.shape[1]
         self.place, self.which = links.dp // 2, links.dp % 2
         self.middle = (self.place == 1) | (self.place == 2)
 
     def rows(self, place, which):
+        if self.got_core is None:
+            return place
         start = pl.multiple_of((2 * place + which) * self.size, self.size)
         return pl.ds(start, self.size)
 
@@ -854,18 +927,20 @@
         ]
 
     def combine(self):
-        links, grads = self.links, self.grads
         for copy in self.core:
             copy.wait_recv()
 
         def add(place, carry):
             rows = self.rows(place, self.which)
-            grads[rows] = (grads[rows].astype(jnp.float32) + self.got_core[place].astype(jnp.float32)).astype(
-                jnp.bfloat16
-            )
+            total = self.grads[rows].astype(jnp.float32) + self.got_core[place].astype(jnp.float32)
+            self.grads[rows] = total.astype(jnp.bfloat16)
             return carry
 
         lax.fori_loop(0, 4, add, 0)
+        self.start()
+
+    def start(self):
+        links, grads = self.links, self.grads
         block = [grads.at[self.rows(self.place ^ step, self.which)] for step in range(4)]
         self.to_extra = links.remote(block[3], self.extra, 2, 0)
         self.to_third = links.remote(block[3], self.got.at[2], 6, 0)
@@ -901,7 +976,9 @@
             self.to_third.wait_recv()
 
     def total(self, out, cols):
-        mine = self.grads[self.rows(self.place, self.which), cols].astype(jnp.float32)
+        rows = self.rows(self.place, self.which)
+        at = (rows, cols) if self.got_core is not None else (rows, slice(None), cols)
+        mine = self.grads[at].astype(jnp.float32)
         out[...] = mine + self.got[0, :, cols].astype(jnp.float32) + self.got[1, :, cols].astype(jnp.float32)
 
         @pl.when(self.middle)
@@ -941,157 +1018,68 @@
 
 
 def backward_kernel(
-    latents, gains, conditioning, cotangent,
-    in_parts, in_last, in_resid_one, in_resid_two, in_qkv, in_attn_out, in_cross, in_keyval_w, in_rows_one, in_rows_two,
-    in_rotated, in_attended, in_logs, in_query, in_keyval, in_crossed, in_cross_logs, in_tables,
-    block_out, grad_latents, grad_context, grad_gains, grad_qkv, grad_attn_out, grad_cross_q, grad_keyval,
-    grad_cross_out,
-    parts, rows_two, seed_one, seed_two, w_qkv, w_attn_out, w_cross, w_keyval, rotated, attended, crossed, query,
-    d_attended, logs, keys_t, values_t, d_keys_t, d_values_t, cross_keys_t, cross_values_t, d_cross_keys_t,
-    d_cross_values_t, keyval, d_keyval, context, context_sum, context_got, resid, d_resid, tables,
-    gain_rows, gain_got, got_one, got_two, core_qkv, core_attn_out, core_cross, core_keyval,
+    latents, gains, conditioning, in_gain, in_d_resid, in_seed,
+    in_grads_cross, in_d_keyval, in_qkv, in_attn_out, in_keyval_w, in_rows_one, in_rotated, in_attended, in_logs,
+    in_tables,
+    grad_latents, grad_context, grad_gains, grad_qkv, grad_attn_out, grad_cross_q, grad_keyval, grad_cross_out,
+    parts, rows_one, seeds, w_qkv, w_attn_out, w_keyval, rotated, attended, d_attended, logs, keys_t, values_t,
+    d_keys_t, d_values_t, grads_cross, core_cross, got_cross, keyval_parts, got_keyval, context, context_sum,
+    context_got, d_resid, tables, gain_rows, gain_got, got, core_qkv, core_attn_out, core_keyval,
     extra_qkv, extra_attn_out, extra_cross, extra_keyval, far_qkv, far_attn_out, far_cross, far_keyval,
-    sum_keyval, sum_last, out_qkv, out_keyval,
-    send, recv, local,
+    sum_keyval, sum_last, out_qkv, out_keyval, send, recv, local,
 ):
     low = jnp.bfloat16
     width = attended.shape[1]
     pairs = width // PAIR
     model = latents.shape[1]
     links = Links(send, recv, local)
-    load_parts = [links.store(in_parts.at[block], parts.at[block]) for block in (3, 1, 2, 0)]
-    load_resid = links.store(in_resid_two, resid)
-    load_cross = [
-        links.store(source, target)
-        for source, target in (
-            (in_cross, w_cross), (in_keyval, keyval), (in_query, query), (in_crossed, crossed), (in_cross_logs, logs),
-        )
-    ]
-    load_mid = [links.store(in_rows_two, rows_two), links.store(in_keyval_w, w_keyval)]
+    which = links.dp % 2
+    load_seed = links.store(in_seed, seeds.at[0])
     load_self = [
         links.store(source, target)
         for source, target in (
-            (in_attn_out, w_attn_out), (in_rotated, rotated), (in_attended, attended), (in_tables, tables),
-            (in_qkv, w_qkv),
+            (in_attn_out, w_attn_out), (in_rotated, rotated), (in_logs, logs), (in_tables, tables),
+            (in_attended, attended),
         )
     ]
+    load_keyval = [links.store(in_d_keyval, keyval_parts), links.store(in_keyval_w, w_keyval)]
+    load_cross = [links.store(in_grads_cross.at[member, :, which], grads_cross.at[member]) for member in range(4)]
+    load_late = [links.store(in_qkv, w_qkv), links.store(in_rows_one, rows_one), links.store(in_d_resid, d_resid)]
     links.greet([(1, 0), (2, 0), (4, 0), (6, 0), (0, 1), (0, 2)])
-    sums_one = Sums(links, parts, *got_one)
-    for load, block in zip(load_parts, (3, 1, 2, 0)):
-        links.settle(load)
-        sums_one.ready(block)
-    gain_rows[...] = jnp.zeros_like(gain_rows)
+    links.settle(load_seed)
+    spread = Spread(links, seeds)
+    core_copies = [
+        links.go(in_grads_cross.at[member, :, 1 - which], core_cross.at[member], 1, 0) for member in range(4)
+    ]
+    gain_rows[...] = in_gain[...]
     context[...] = jnp.zeros_like(context)
     context[:CTX] = conditioning[0]
-    links.settle(load_resid)
-    for load in load_cross:
-        links.settle(load)
-    for pair in range(pairs):
-        at = slice(pair * PAIR, (pair + 1) * PAIR)
-        cross_keys_t[pair] = keyval[0, :, at].astype(jnp.float32).T.astype(low)
-        cross_values_t[pair] = keyval[1, :, at].astype(jnp.float32).T.astype(low)
-    d_cross_keys_t[...] = jnp.zeros_like(d_cross_keys_t)
-    d_cross_values_t[...] = jnp.zeros_like(d_cross_values_t)
-    d_keys_t[...] = jnp.zeros_like(d_keys_t)
-    d_values_t[...] = jnp.zeros_like(d_values_t)
-    sums_one.add()
-    sums_one.arrive()
-
-    def norm_back(which, values, sums):
-        def step(rows):
-            gain = gains[which : which + 1]
-            _, scaled, inverse = layer_norm(values[rows].astype(jnp.float32), gain)
-            d_normed = parts[0, rows].astype(jnp.float32) + sums.total(rows)
-            d_part, gain_grad = norm_backward(d_normed, scaled, inverse, gain)
-            gain_rows[which : which + 1] += gain_grad[None]
-            earlier = cotangent[rows].astype(jnp.float32) if which == 2 else d_resid[rows]
-            d_resid[rows] = earlier + d_part
-            if which > 0:
-                (seed_one if which == 2 else seed_two)[0, rows] = d_resid[rows].astype(low)
-
-        row_steps(BLOCK, step)
-
-    norm_back(2, resid, sums_one)
-    spread_one = Spread(links, seed_one)
-    load_resid = links.store(in_resid_one, resid)
-    sums_one.sent()
-
-    def back_project(source, weight, block, sums):
-        def project(cols):
-            parts[block, :, cols] = dot_cols(source, weight(cols)).astype(low)
-
-        columns(model, 512, project)
-        sums.ready(block)
-
-    sums_two = Sums(links, parts, *got_two)
-    for block in range(4):
-        spread_one.wait(block)
-        rows = block_rows(block)
-        d_crossed = dot_plain(seed_one[block], w_cross[:, width:]).astype(low)
-        for pair in range(pairs):
-            at = slice(pair * PAIR, (pair + 1) * PAIR)
-            out = attend_rows_back(
-                query[rows, at] * low(DH**-0.5), d_crossed[:, at], logs[rows, at], cross_keys_t[pair],
-                cross_values_t[pair], keyval[0, :, at], d_cross_keys_t.at[pair], d_cross_values_t.at[pair], CTX,
-            )
-            query[rows, at] = out.astype(low)
-        back_project(query[rows], lambda cols: w_cross[cols, :width], block, sums_two)
-    sums_two.add()
-    load_logs = links.store(in_logs, logs)
-    for load in load_mid:
-        links.settle(load)
-
-    def whole(rows, cols):
-        return rows[:, :, cols].reshape(LENGTH, -1)
-
-    def grads_into(target, rows, cols, right):
-        def product(part):
-            target[part, cols] = dot_rows(whole(rows, part), right).astype(low)
-
-        columns(model, 384, product)
-
-    for pair in range(pairs):
-        at = slice(pair * PAIR, (pair + 1) * PAIR)
-        d_keyval[:, at] = d_cross_keys_t[pair].T.astype(low)
-        d_keyval[:, width + pair * PAIR : width + (pair + 1) * PAIR] = d_cross_values_t[pair].T.astype(low)
-    context_sum[...] = dot_cols(d_keyval[...], w_keyval[...]).astype(low)
-    context_near = links.go(context_sum, context_got.at[0], 0, 1)
-    w_keyval[...] = dot_rows(context[...], d_keyval[...]).astype(low)
-    scatter_keyval = Scatter(links, w_keyval, core_keyval, extra_keyval, far_keyval, 1)
-    scatter_keyval.pair_up()
-    grads_into(w_cross, rows_two, slice(0, width), query[...])
-    grads_into(w_cross, seed_one, slice(width, 2 * width), crossed[...])
-    scatter_cross = Scatter(links, w_cross, core_cross, extra_cross, far_cross, 1)
-    scatter_cross.pair_up()
-    links.settle(load_resid)
-    context_near.wait_recv()
-    links.settle_sends((context_near,))
-    context_sum[...] = (context_sum[...].astype(jnp.float32) + context_got[0].astype(jnp.float32)).astype(low)
-    scatter_keyval.combine()
-    scatter_cross.combine()
-    load_last = links.store(in_last, rows_two)
-    sums_two.arrive()
-    norm_back(1, resid, sums_two)
-    spread_two = Spread(links, seed_two)
-    sums_two.sent()
-    spread_one.sent()
-    load_rows = links.store(in_rows_one, seed_one)
-    context_far = links.go(context_sum, context_got.at[1], 0, 2)
     for load in load_self:
         links.settle(load)
-    links.settle(load_logs)
     for pair in range(pairs):
         key = rotated[:, width + pair * PAIR : width + (pair + 1) * PAIR]
         value = rotated[:, 2 * width + pair * PAIR : 2 * width + (pair + 1) * PAIR]
         keys_t[pair] = key.astype(jnp.float32).T.astype(low)
         values_t[pair] = value.astype(jnp.float32).T.astype(low)
+    d_keys_t[...] = jnp.zeros_like(d_keys_t)
+    d_values_t[...] = jnp.zeros_like(d_values_t)
     cosine, sine = (tables.at[part] for part in range(2))
-    sums_last = Sums(links, rows_two, *got_one)
+    sums_keyval = Sums(links, keyval_parts, *got_keyval)
+    sums_cross = Sums(links, grads_cross, *got_cross)
+
+    def whole(rows, cols):
+        return rows[:, :, cols].reshape(LENGTH, -1)
+
+    def grads_into(target, rows, right):
+        def product(part):
+            target[part, :] = dot_rows(whole(rows, part), right).astype(low)
+
+        columns(model, 384, product)
 
     for block in range(4):
-        spread_two.wait(block)
+        spread.wait(block)
         rows = block_rows(block)
-        d_attended[rows] = dot_plain(seed_two[block], w_attn_out[...]).astype(low)
+        d_attended[rows] = dot_plain(seeds[block], w_attn_out[...]).astype(low)
         turn = (cosine[rows], -sine[rows])
 
         def one_pair(pair, carry):
@@ -1106,15 +1094,28 @@
 
         lax.fori_loop(0, pairs, one_pair, 0)
         if block == 0:
-            scatter_keyval.relay()
+            for load in load_keyval + load_cross:
+                links.settle(load)
+            for copy in core_copies:
+                copy.wait_recv()
+            for member in range(4):
+
+                def add(place, carry):
+                    total = grads_cross[member, place].astype(jnp.float32) + core_cross[member, place].astype(jnp.float32)
+                    grads_cross[member, place] = total.astype(low)
+                    return carry
+
+                lax.fori_loop(0, 4, add, 0)
         if block == 1:
-            scatter_cross.relay()
+            for part in (3, 1, 2):
+                sums_keyval.ready(part)
+            for part in (3, 1, 2):
+                sums_cross.ready(part)
         if block == 2:
-            links.settle(load_last)
-            for last in (3, 1, 2):
-                sums_last.ready(last)
-    grads_into(w_attn_out, seed_two, slice(None), attended[...])
-    scatter_attn_out = Scatter(links, w_attn_out, core_attn_out, extra_attn_out, far_attn_out, 1)
+            sums_keyval.add()
+            sums_cross.add()
+    grads_into(w_attn_out, seeds, attended[...])
+    scatter_attn_out = Scatter(links, w_attn_out, core_attn_out, extra_attn_out, far_attn_out)
     scatter_attn_out.pair_up()
     for pair in range(pairs):
         for block in range(4):
@@ -1124,56 +1125,72 @@
             rotated[rows, at] = head_turn(d_keys_t[pair, :, rows].T, *turn).astype(low)
             at = slice(2 * width + pair * PAIR, 2 * width + (pair + 1) * PAIR)
             rotated[rows, at] = d_values_t[pair, :, rows].T.astype(low)
-    sums_last.add()
-    sums_three = Sums(links, parts, *got_two)
+    for load in load_late:
+        links.settle(load)
+    sums = Sums(links, parts, *got)
     for block in (3, 1, 2, 0):
-        back_project(rotated[block_rows(block)], lambda cols: w_qkv[cols, :], block, sums_three)
-    links.settle(load_rows)
+
+        def project(cols):
+            parts[block, :, cols] = dot_cols(rotated[block_rows(block)], w_qkv[cols, :]).astype(low)
+
+        columns(model, 512, project)
+        sums.ready(block)
     scatter_attn_out.combine()
-    grads_into(w_qkv, seed_one, slice(None), rotated[...])
-    scatter_qkv = Scatter(links, w_qkv, core_qkv, extra_qkv, far_qkv, 1)
+    grads_into(w_qkv, rows_one, rotated[...])
+    scatter_qkv = Scatter(links, w_qkv, core_qkv, extra_qkv, far_qkv)
     scatter_qkv.pair_up()
-    sums_three.add()
+    sums.add()
     scatter_qkv.combine()
-    load_resid = links.store(in_resid_two, resid)
-    sums_last.arrive()
-    links.settle(load_resid)
-
-    def add_last(rows):
-        resid[rows] += rows_two[0, rows].astype(jnp.float32) + sums_last.total(rows)
-
-    row_steps(BLOCK, add_last)
-    links.store(resid, block_out)
+    sums_keyval.arrive()
+    d_keyval = keyval_parts[0].astype(jnp.float32) + sums_keyval.total(slice(None))
+    d_keyval = d_keyval.astype(low)
+    context_sum[...] = dot_cols(d_keyval, w_keyval[...]).astype(low)
+    context_near = links.go(context_sum, context_got.at[0], 0, 1)
+    w_keyval[...] = dot_rows(context[...], d_keyval).astype(low)
+    scatter_keyval = Scatter(links, w_keyval, core_keyval, extra_keyval, far_keyval)
+    scatter_keyval.pair_up()
+    sums_cross.arrive()
+    for place in range(4):
+        total = grads_cross[0, place].astype(jnp.float32) + sums_cross.total(place)
+        grads_cross[0, place] = total.astype(low)
+    scatter_cross = Scatter(links, grads_cross.at[0], None, extra_cross, far_cross)
+    scatter_cross.start()
+    scatter_keyval.combine()
+    context_near.wait_recv()
+    links.settle_sends((context_near,))
+    context_sum[...] = (context_sum[...].astype(jnp.float32) + context_got[0].astype(jnp.float32)).astype(low)
+    context_far = links.go(context_sum, context_got.at[1], 0, 2)
+    scatter_attn_out.relay()
+    sums.arrive()
+
+    def norm_one(rows):
+        gain = gains[0:1]
+        _, scaled, inverse = layer_norm(latents[rows].astype(jnp.float32), gain)
+        d_normed = parts[0, rows].astype(jnp.float32) + sums.total(rows)
+        d_part, gain_grad = norm_backward(d_normed, scaled, inverse, gain)
+        gain_rows[0:1] += gain_grad[None]
+        d_resid[rows] += d_part
+
+    row_steps(BLOCK, norm_one)
+    links.store(d_resid, grad_latents)
+    share = out_qkv.shape[0]
+    spot = [logs.at[pl.ds(step * share, share)] for step in range(5)]
+    qkv_spot = spot[3:5] + [sum_last]
+    for step, (dp_bit, tensor_bit) in enumerate(((1, 0), (0, 1), (0, 2), (2, 0), (4, 0))):
+        trade = links.remote(gain_rows, gain_got.at[step], dp_bit, tensor_bit)
+        trade.start()
+        if step == 1:
+            scatter_qkv.relay()
+        if step == 2:
+            scatter_cross.relay()
+        if step == 3:
+            scatter_keyval.relay()
+        trade.wait()
+        gain_rows[...] += gain_got[step]
+    grad_gains[...] = gain_rows[...]
     context_far.wait_recv()
     context_total = context_sum[...].astype(jnp.float32) + context_got[1].astype(jnp.float32)
     grad_context[0] = context_total[:CTX]
-    scatter_attn_out.relay()
-    scatter_keyval.arrive()
-    scatter_keyval.total(sum_keyval, slice(None))
-    heads = width // DH
-    for head in range(heads):
-        pieces = [sum_keyval[:, start + head * DH : start + (head + 1) * DH] for start in (0, width)]
-        out_keyval[:, 2 * head * DH : 2 * (head + 1) * DH] = jnp.concatenate(pieces, axis=1)
-    links.store(out_keyval, grad_keyval)
-    scatter_cross.arrive()
-    share = out_qkv.shape[0]
-    spot = [logs.at[pl.ds(step * share, share)] for step in range(5)]
-    qkv_spot = spot[3:5] + [sum_last]
-    scatter_cross.total(spot[0], slice(0, width))
-    links.store(spot[0], grad_cross_q)
-    scatter_cross.total(spot[1], slice(width, 2 * width))
-    links.store(spot[1], grad_cross_out)
-    sums_three.arrive()
-    norm_back(0, latents, sums_three)
-    links.store(d_resid, grad_latents)
-    for step, (dp_bit, tensor_bit) in enumerate(((1, 0), (0, 1), (0, 2), (2, 0), (4, 0))):
-        trade = links.remote(gain_rows, gain_got.at[step], dp_bit, tensor_bit)
-        trade.start()
-        if step == 2:
-            scatter_qkv.relay()
-        trade.wait()
-        gain_rows[...] += gain_got[step]
-    grad_gains[...] = gain_rows[...]
     scatter_attn_out.arrive()
     scatter_attn_out.total(spot[2], slice(None))
     links.store(spot[2], grad_attn_out)
@@ -1181,21 +1198,33 @@
     for part in range(3):
         scatter_qkv.total(qkv_spot[part], slice(part * width, (part + 1) * width))
     for pair in range(pairs):
-        heads_of = [qkv_spot[part][:, (2 * pair + which) * DH : (2 * pair + which + 1) * DH] for which in range(2) for part in range(3)]
+        heads_of = [
+            qkv_spot[part][:, (2 * pair + half) * DH : (2 * pair + half + 1) * DH]
+            for half in range(2)
+            for part in range(3)
+        ]
         for step in range(3):
             start = (3 * pair + step) * PAIR
             out_qkv[:, start : start + PAIR] = jnp.concatenate(heads_of[2 * step : 2 * step + 2], axis=1)
     links.store(out_qkv, grad_qkv)
+    scatter_cross.arrive()
+    scatter_cross.total(spot[0], slice(0, width))
+    links.store(spot[0], grad_cross_q)
+    scatter_cross.total(spot[1], slice(width, 2 * width))
+    links.store(spot[1], grad_cross_out)
+    scatter_keyval.arrive()
+    scatter_keyval.total(sum_keyval, slice(None))
+    for head in range(width // DH):
+        pieces = [sum_keyval[:, start + head * DH : start + (head + 1) * DH] for start in (0, width)]
+        out_keyval[:, 2 * head * DH : 2 * (head + 1) * DH] = jnp.concatenate(pieces, axis=1)
+    links.store(out_keyval, grad_keyval)
     links.finish()
     for scatter in (scatter_keyval, scatter_cross, scatter_attn_out, scatter_qkv):
         scatter.finish()
 
 
-def backward_part(latents, gains, conditioning, cotangent, parts, last, kept):
-    (
-        resid_one, resid_two, w_qkv, w_attn_out, w_cross, w_keyval, rows_one, rows_two, rotated, attended, logs, query,
-        keyval, crossed, cross_logs, tables,
-    ) = kept
+def backward_part(latents, gains, conditioning, gain_rows, d_resid, seed, grads_cross, d_keyval, kept):
+    w_qkv, w_attn_out, w_keyval, rows_one, rotated, attended, logs, tables = kept
     model = latents.shape[1]
     depth = conditioning.shape[2]
     wide = w_qkv.shape[1]
@@ -1206,7 +1235,6 @@
     low, high = jnp.bfloat16, jnp.float32
     outs = [
         ((BLOCK, model), high),
-        ((BLOCK, model), high),
         (conditioning.shape, high),
         ((8, model), high),
         ((share, wide), high),
@@ -1215,18 +1243,15 @@
         ((span, 2 * width), high),
         ((share, width), high),
     ]
+    cross_block = (4, share, 2 * width)
     work = [
-        ((4, BLOCK, model), low),
         ((4, BLOCK, model), low),
         ((4, BLOCK, model), low),
         ((4, BLOCK, model), low),
         ((model, wide), low),
         ((model, width), low),
-        ((model, 2 * width), low),
         ((depth, 2 * width), low),
         ((LENGTH, wide), low),
-        ((LENGTH, width), low),
-        ((LENGTH, width), low),
         ((LENGTH, width), low),
         ((LENGTH, width), low),
         ((LENGTH, width), high),
@@ -1234,24 +1259,24 @@
         ((pairs, PAIR, LENGTH), low),
         ((pairs, PAIR, LENGTH), high),
         ((pairs, PAIR, LENGTH), high),
-        ((pairs, PAIR, FULL), low),
-        ((pairs, PAIR, FULL), low),
-        ((pairs, PAIR, FULL), high),
-        ((pairs, PAIR, FULL), high),
-        ((2, FULL, width), low),
-        ((FULL, 2 * width), low),
+        ((4, *cross_block), low),
+        ((4, *cross_block), low),
+    ]
+    cross_got = [pltpu.VMEM((rows, share, 2 * width), low) for rows in (2, 2, 4, 4)]
+    keyval_got = [pltpu.VMEM((rows, 2 * width), low) for rows in (FULL // 2, FULL // 2, FULL, FULL)]
+    more = [
         ((FULL, depth), low),
         ((FULL, depth), low),
         ((2, FULL, depth), low),
-        ((BLOCK, model), high),
         ((BLOCK, model), high),
         ((2, LENGTH, PAIR), high),
         ((8, model), high),
         ((5, 8, model), high),
     ]
     groups = [(share, wide), (share, width), (share, 2 * width), (span, 2 * width)]
-    scratch = [pltpu.VMEM(*buffer) for buffer in work] + [sum_buffers(model), sum_buffers(model)]
-    scratch += [pltpu.VMEM((4, *group), low) for group in groups]
+    scratch = [pltpu.VMEM(*buffer) for buffer in work] + [cross_got, pltpu.VMEM((4, FULL, 2 * width), low), keyval_got]
+    scratch += [pltpu.VMEM(*buffer) for buffer in more] + [sum_buffers(model)]
+    scratch += [pltpu.VMEM((4, *group), low) for group in (groups[0], groups[1], groups[3])]
     scratch += [pltpu.VMEM(group, low) for group in groups]
     scratch += [pltpu.VMEM((3, *group), low) for group in groups]
     scratch += [pltpu.VMEM(groups[3], high), pltpu.VMEM((share, width), high)]
@@ -1260,14 +1285,168 @@
     return pl.pallas_call(
         backward_kernel,
         out_shape=[jax.ShapeDtypeStruct(*out) for out in outs],
-        in_specs=[whole_vmem()] * 4 + [anywhere()] * 18,
-        out_specs=[anywhere()] * 2 + [whole_vmem()] * 2 + [anywhere()] * 5,
+        in_specs=[whole_vmem()] * 4 + [anywhere()] * 12,
+        out_specs=[anywhere()] + [whole_vmem()] * 2 + [anywhere()] * 5,
         scratch_shapes=scratch,
         compiler_params=pltpu.CompilerParams(collective_id=2, has_side_effects=True, vmem_limit_bytes=VMEM_BYTES),
         cost_estimate=pl.CostEstimate(flops=2**37, bytes_accessed=2**26, transcendentals=2**23),
     )(
-        latents, gains, conditioning, cotangent, parts, last, resid_one, resid_two, w_qkv, w_attn_out, w_cross,
-        w_keyval, rows_one, rows_two, rotated, attended, logs, query, keyval, crossed, cross_logs, tables,
+        latents, gains, conditioning, gain_rows, d_resid, seed, grads_cross, d_keyval, w_qkv, w_attn_out, w_keyval,
+        rows_one, rotated, attended, logs, tables,
+    )
+
+
+def cross_back_kernel(
+    cotangent, gains, normed_two, resid_two, resid_one, in_parts, in_last, in_query, in_crossed, in_cross_logs,
+    in_keyval, in_cross,
+    block_out, d_resid_out, seed_out, grads_out, d_keyval_out, gain_out,
+    parts, parts_last, got, got_last, w_cross, query, crossed, cross_logs, keyval, d_keyval, d_keys_t, d_values_t,
+    d_resid, d_normed_two, cross_seed, seed, total, send, recv, local,
+):
+    low = jnp.bfloat16
+    model = cotangent.shape[1]
+    width = model // 4
+    share = w_cross.shape[3]
+    pairs = width // PAIR
+    links = Links(send, recv, local)
+    load_parts = [links.store(in_parts.at[block], parts.at[block]) for block in (3, 1, 2, 0)]
+    load_last = [links.store(in_last.at[block], parts_last.at[block]) for block in (3, 1, 2, 0)]
+    loads = [
+        links.store(source, target)
+        for source, target in (
+            (in_query, query), (in_crossed, crossed), (in_cross_logs, cross_logs), (in_keyval, keyval),
+            (in_cross, w_cross),
+        )
+    ]
+    gain_out[...] = jnp.zeros_like(gain_out)
+    links.greet([(0, 1), (0, 2)])
+    sums = Sums(links, parts, *got)
+    for load, block in zip(load_parts, (3, 1, 2, 0)):
+        links.settle(load)
+        sums.ready(block)
+    for load in loads + load_last:
+        links.settle(load)
+    sums.add()
+    sums_last = Sums(links, parts_last, *got_last)
+    for block in (3, 1, 2):
+        sums_last.ready(block)
+    sums.arrive()
+
+    def norm_three(rows):
+        gain = gains[2:3]
+        _, scaled, inverse = layer_norm(resid_two[rows], gain)
+        d_normed = parts[0, rows].astype(jnp.float32) + sums.total(rows)
+        d_part, gain_grad = norm_backward(d_normed, scaled, inverse, gain)
+        gain_out[2:3] += gain_grad[None]
+        value = cotangent[rows].astype(jnp.float32) + d_part
+        d_resid[rows] = value
+        cross_seed[rows] = value.astype(low)
+
+    row_steps(BLOCK, norm_three)
+    for member in range(4):
+        at_member = slice(member * width, (member + 1) * width)
+        d_crossed = dot_plain(cross_seed[...], cross_columns(w_cross, member, slice(width, 2 * width))).astype(low)
+        for pair in range(pairs):
+            at = slice(member * width + pair * PAIR, member * width + (pair + 1) * PAIR)
+            keys_at = slice(pair * PAIR, (pair + 1) * PAIR)
+            values_at = slice(width + pair * PAIR, width + (pair + 1) * PAIR)
+            key = keyval[member, :, keys_at]
+            key_t = key.astype(jnp.float32).T.astype(low)
+            value_t = keyval[member, :, values_at].astype(jnp.float32).T.astype(low)
+            d_keys_t[...] = jnp.zeros_like(d_keys_t)
+            d_values_t[...] = jnp.zeros_like(d_values_t)
+            out = attend_rows_back(
+                query[:, at] * low(DH**-0.5), d_crossed[:, keys_at], cross_logs[:, at], key_t, value_t, key, d_keys_t,
+                d_values_t, CTX,
+            )
+            query[:, at] = out.astype(low)
+            d_keyval[member, :, keys_at] = d_keys_t[...].T.astype(low)
+            d_keyval[member, :, values_at] = d_values_t[...].T.astype(low)
+        for place in range(4):
+            at = slice(place * 2 * share, (place + 1) * 2 * share)
+            part = dot_cols(query[:, at_member], cross_tile(w_cross, member, place, slice(0, width)))
+            if member == 0:
+                d_normed_two[:, at] = part
+            else:
+                d_normed_two[:, at] += part
+    links.store(d_keyval, d_keyval_out)
+
+    def norm_two(rows):
+        gain = gains[1:2]
+        _, scaled, inverse = layer_norm(resid_one[rows], gain)
+        d_part, gain_grad = norm_backward(d_normed_two[rows], scaled, inverse, gain)
+        gain_out[1:2] += gain_grad[None]
+        value = d_resid[rows] + d_part
+        d_resid[rows] = value
+        seed[rows] = value.astype(low)
+
+    row_steps(BLOCK, norm_two)
+    links.store(d_resid, d_resid_out)
+    links.store(seed, seed_out)
+    sums_last.add()
+    for place in range(4):
+        rows_at = slice(place * 2 * share, (place + 1) * 2 * share)
+        for member in range(4):
+            at_member = slice(member * width, (member + 1) * width)
+            left = dot_rows(normed_two[:, rows_at], query[:, at_member]).astype(low)
+            w_cross[member, place, :, :, :width] = left.reshape(2, share, width)
+            right = dot_rows(cross_seed[:, rows_at], crossed[:, at_member]).astype(low)
+            w_cross[member, place, :, :, width:] = right.reshape(2, share, width)
+    links.store(w_cross, grads_out)
+    sums_last.arrive()
+
+    def add_last(rows):
+        total[rows] = resid_two[rows] + parts_last[0, rows].astype(jnp.float32) + sums_last.total(rows)
+
+    row_steps(BLOCK, add_last)
+    links.store(total, block_out)
+    links.finish()
+
+
+def cross_back_part(cotangent, gains, parts, last, kept):
+    normed_two, resid_two, resid_one, query, crossed, cross_logs, keyval, cross_all = kept
+    model = cotangent.shape[1]
+    low, high = jnp.bfloat16, jnp.float32
+    outs = [
+        ((BLOCK, model), high),
+        ((BLOCK, model), high),
+        ((BLOCK, model), low),
+        (cross_all.shape, low),
+        (keyval.shape, low),
+        ((8, model), high),
+    ]
+    work = [
+        ((4, BLOCK, model), low),
+        ((4, BLOCK, model), low),
+    ]
+    more = [
+        (cross_all.shape, low),
+        ((BLOCK, model), low),
+        ((BLOCK, model), low),
+        ((BLOCK, model), high),
+        (keyval.shape, low),
+        (keyval.shape, low),
+        ((PAIR, FULL), high),
+        ((PAIR, FULL), high),
+        ((BLOCK, model), high),
+        ((BLOCK, model), high),
+        ((BLOCK, model), low),
+        ((BLOCK, model), low),
+        ((BLOCK, model), high),
+    ]
+    scratch = [pltpu.VMEM(*buffer) for buffer in work] + [sum_buffers(model), sum_buffers(model)]
+    scratch += [pltpu.VMEM(*buffer) for buffer in more]
+    scratch += [pltpu.SemaphoreType.DMA((24,)), pltpu.SemaphoreType.DMA((24,)), pltpu.SemaphoreType.DMA((24,))]
+    return pl.pallas_call(
+        cross_back_kernel,
+        out_shape=[jax.ShapeDtypeStruct(*out) for out in outs],
+        in_specs=[whole_vmem()] * 5 + [anywhere()] * 7,
+        out_specs=[anywhere()] * 5 + [whole_vmem()],
+        scratch_shapes=scratch,
+        compiler_params=pltpu.CompilerParams(collective_id=3, has_side_effects=True, vmem_limit_bytes=VMEM_BYTES),
+        cost_estimate=pl.CostEstimate(flops=2**35, bytes_accessed=2**26, transcendentals=2**21),
+    )(
+        cotangent, gains, normed_two, resid_two, resid_one, parts, last, query, crossed, cross_logs, keyval, cross_all
     )
 
 
@@ -1291,7 +1470,7 @@
     hidden_wide = w_gate.shape[1]
     gains = jnp.stack([gain_attn, gain_cross, gain_mlp])
     (
-        rows_one, rows_two, rows_three, mlp_seed, qkv_all, attn_out_t, cross_all, cross_kv, mlp_all, down_all,
+        rows_one, normed_two, rows_three, mlp_seed, qkv_all, attn_out_t, cross_all, cross_kv, mlp_all, down_all,
         rotated, attended, logs, cross_query, keyval, crossed, cross_logs, resid_one, resid_two, tables,
     ) = forward_part(
         latents,
@@ -1315,14 +1494,26 @@
     block_shape = (4, latents.shape[0], -1)
     parts = dot_cols(d_both, mlp_all).astype(low).reshape(block_shape)
     last = dot_cols(hidden, down_all).astype(low).reshape(block_shape)
-    kept = (
-        resid_one, resid_two, qkv_all, attn_out_t, cross_all, cross_kv, rows_one, rows_two, rotated, attended, logs,
-        cross_query, keyval, crossed, cross_logs, tables,
-    )
-    (
-        block_out, grad_latents, grad_context, grad_gains, grad_qkv, grad_attn_out, grad_cross_q, grad_cross_kv,
-        grad_cross_out,
-    ) = backward_part(latents, gains, conditioning, cotangent, parts, last, kept)
+    block_out, d_resid, seed, grads_cross, d_keyval, gain_rows = cross_back_part(
+        cotangent,
+        gains,
+        parts,
+        last,
+        (normed_two, resid_two, resid_one, cross_query, crossed, cross_logs, keyval, cross_all),
+    )
+    grad_latents, grad_context, grad_gains, grad_qkv, grad_attn_out, grad_cross_q, grad_cross_kv, grad_cross_out = (
+        backward_part(
+            latents,
+            gains,
+            conditioning,
+            gain_rows,
+            d_resid,
+            seed,
+            grads_cross,
+            d_keyval,
+            (qkv_all, attn_out_t, cross_kv, rows_one, rotated, attended, logs, tables),
+        )
+    )
     return (
         block_out,
         grad_latents,

time: 542 us -> 528 us (0.974)
  Pallas kernels: 429 us -> 415 us
    pallas_call x1, Pallas kernels: 217 us -> 150 us  [backward_part(): pl.pallas_call(backward_kernel, out_shape=[jax.ShapeDtypeStruct(*out) for...]
    pallas_call x0 -> x1, Pallas kernels: none -> 62.1 us  [cross_back_part(): pl.pallas_call(cross_back_kernel, out_shape=[jax.ShapeDtypeStruct(*out) f...]
    pallas_call x1, Pallas kernels: 212 us -> 203 us  [forward_part(): pl.pallas_call(forward_kernel, out_shape=[jax.ShapeDtypeStruct(*out) for...]
where the time goes in v4:
time: 528 us; the launch traced here: 519 us
  Pallas kernels  415 us (79%)
  matrix products  69.6 us (13%)
  between operations  14.4 us (3%)
  local copies, waits for them, and re-layouts  13.9 us (3%)
  other arithmetic  5.89 us (1%)
    pallas_call x1, Pallas kernels, forward_part(): pl.pallas_call(forward_kernel, out_shape=[jax.ShapeDtypeStruct(*out) for...  203 us
    pallas_call x1, Pallas kernels, backward_part(): pl.pallas_call(backward_kernel, out_shape=[jax.ShapeDtypeStruct(*out) for...  150 us
    pallas_call x1, Pallas kernels, cross_back_part(): pl.pallas_call(cross_back_kernel, out_shape=[jax.ShapeDtypeStruct(*out) f...  62.1 us
    dot_general x2, matrix products, dot_rows(): lax.dot_general(left_op, right_op, (((0,), (0,)), ((), ())), preferred_el...  23.6 us
    dot_general x2, matrix products, dot_plain(): return jnp.dot(left_op, right_op, preferred_element_type=jnp.float32)  23.4 us
    dot_general x2, matrix products, dot_cols(): lax.dot_general(left_op, right_op, (((1,), (1,)), ((), ())), preferred_el...  22.6 us
  transfers between devices with their start and end apart: 2, of which 0 were waited for; matrix products, arithmetic and copies ran while one was open for 8% of the time, Pallas kernels for 41%

profile of v4, /device:TPU:0, one launch (start us, length us, event | category | flops | bytes accessed | tf_op | source)
XLA Modules:
  0.0 519.1 jit_solution(15733932553114264917)
XLA Ops:
  7.2 0.0 reduce-scatter.5.cloned.1.call-start
  7.2 0.7 stack.12
  7.9 0.7 stack.13
  8.6 0.7 stack.14
  9.3 0.6 pad_maximum_fusion.5.gains
  10.0 203.1 %shard_map.245 = (bf16[4,256,1536]{2,1,0:T(8,128)(2,1)}, bf16[256,1536]{1,0:T(8,128)(2,1)}, bf16[4,256,1536]{2,1,0:T(8,128)(2,1)}, bf16[4,256,1536]{2,1,0:T(8,12...) custom-call(bf16[256,1536]{1,0:T(8,128)(2,1)} %latents.3, ...), custom_call_target="tpu_custom_call" | custom-call | flops 137438953472 | bytes 67108864 | tf_op jit(solution)/shard_map/pallas_call | solution.py:899
  213.1 0.0 copy-start.8
  213.1 13.5 %fusion.5 = f32[1024,3072]{1,0:T(8,128)S(1)} fusion(bf16[1024,1536]{1,0:T(8,128)(2,1)} %bitcast.26, bf16[1536,3072]{1,0:T(8,128)(2,1)} %get-tuple-element.54), kind=kOutput, calls=%fused_computation.20 | convolution fusion | flops 9663676416 | bytes 25165824 | tf_op jit(solution)/shard_map/dot_general | solution.py:186
  226.7 9.8 %multiply_convert_fusion.2 = (bf16[1024,1536]{1,0:T(8,128)(2,1)}, bf16[1024,1536]{1,0:T(8,128)(2,1)}, bf16[1024,1536]{1,0:T(8,128)(2,1)}) fusion(f32[1024,3072]{1,0:T(8,128)S(1)} %fusion.5, bf16[1024,1536]{1,0:T(8,128)(2,1)S(1)} %bitcast.28, bf16[1536,1536]{1,0:T(8,128)(2,1)S(1)} %copy-done.10), kind=kOutput, calls=%fused_computation.5 | convolution fusion | flops 4855431168 | bytes 29884416 | tf_op jit(solution)/shard_map/dot_general | solution.py:186
  236.5 8.6 %convolution_convert_fusion.1 = bf16[1536,1536]{1,0:T(8,128)(2,1)} fusion(bf16[1024,1536]{1,0:T(8,128)(2,1)S(1)} %bitcast.29, bf16[1024,1536]{1,0:T(8,128)(2,1)} %get-tuple-element.101), kind=kOutput, calls=%fused_computation.1 | convolution fusion | flops 4834197504 | bytes 11010048 | tf_op jit(solution)/shard_map/dot_general | solution.py:190
  245.1 0.0 reduce-scatter.5.cloned.1.call-update
  245.1 0.0 reduce-scatter.3.cloned.1.call-start
  245.2 1.8 copy-done.7
  247.0 15.0 %convolution_convert_fusion = bf16[1536,3072]{1,0:T(8,128)(2,1)} fusion(bf16[1024,1536]{1,0:T(8,128)(2,1)S(1)} %bitcast.27, bf16[1024,1536]{1,0:T(8,128)(2,1)} %get-tuple-element.100, bf16[1024,1536]{1,0:T(8,128)(2,1)} %get-tuple-element.99), kind=kOutput, calls=%fused_computation | convolution fusion | flops 9680977920 | bytes 18874368 | tf_op jit(solution)/shard_map/dot_general | solution.py:190
  262.0 0.0 reduce-scatter.3.cloned.1.call-update
  262.0 0.0 slice-start.1
  262.0 0.0 slice-start.2
  262.1 9.5 %convolution_convert_fusion.2 = bf16[1024,1536]{1,0:T(8,128)(2,1)} fusion(bf16[1024,1536]{1,0:T(8,128)(2,1)} %get-tuple-element.101, bf16[1536,1536]{1,0:T(8,128)(2,1)} %get-tuple-element.52), kind=kOutput, calls=%fused_computation.9 | convolution fusion | flops 4833411072 | bytes 11010048 | tf_op jit(solution)/shard_map/dot_general | solution.py:196
  271.6 13.1 %fusion.2 = bf16[1024,1536]{1,0:T(8,128)(2,1)} fusion(bf16[1536,3072]{1,0:T(8,128)(2,1)S(1)} %bitcast.33, bf16[1024,1536]{1,0:T(8,128)(2,1)} %get-tuple-element.100, bf16[1024,1536]{1,0:T(8,128)(2,1)S(1)} %copy-done.9), kind=kOutput, calls=%fused_computation.10 | convolution fusion | flops 9677832192 | bytes 18874368 | tf_op jit(solution)/shard_map/dot_general | solution.py:196
  284.7 62.1 %shard_map.246 = (f32[256,1536]{1,0:T(8,128)}, f32[256,1536]{1,0:T(8,128)}, bf16[256,1536]{1,0:T(8,128)(2,1)}, bf16[4,4,2,192,768]{4,3,2,1,0:T(8,128)(2,1)}, bf1...) custom-call(bf16[256,1536]{1,0:T(8,128)(2,1)} %cotangent.3, f32[3,1536]{1,0:T(4,128)} %pad_maximum_fusion.5.gains, ...), custom_call_target="tpu_custom_call" | custom-call | flops 34359738368 | bytes 67108864 | tf_op jit(solution)/shard_map/pallas_call | solution.py:1440
  346.9 149.9 %shard_map.247 = (f32[256,1536]{1,0:T(8,128)}, f32[1,130,768]{2,1,0:T(8,128)}, f32[8,1536]{1,0:T(8,128)}, f32[192,1152]{1,0:T(8,128)}, f32[192,384]{1,0:T(8,128)...) custom-call(bf16[256,1536]{1,0:T(8,128)(2,1)} %latents.3, f32[3,1536]{1,0:T(4,128)} %pad_maximum_fusion.5.gains, ...), custom_call_target="tpu_custom_call" | custom-call | flops 137438953472 | bytes 67108864 | tf_op jit(solution)/shard_map/pallas_call | solution.py:1285
  496.8 2.3 copy.28
  499.1 1.6 slice_reduce_fusion
  500.7 2.2 convert_bitcast_fusion
  502.9 3.1 slice_convert_fusion
  505.9 1.1 copy.36
  507.1 1.1 copy.37
  508.2 0.9 copy.38
  509.2 0.7 copy.39
  509.9 0.7 copy.40
  510.6 0.7 copy.41
  511.3 0.7 copy.42
  (27 shorter events, 0.1 us)
Async XLA Ops:
  7.2 493.5 %reduce-scatter.5.cloned.1.call-start = ((), (), s32[]{:S(2)}) async-start(), calls=%async_computation.3 | async-start | bytes 5308416 | tf_op jit(solution)/shard_map/reduce_scatter | solution.py:305
  213.1 13.6 %copy-start.8 = (bf16[4,256,1536]{2,1,0:T(8,128)(2,1)S(1)}, bf16[4,256,1536]{2,1,0:T(8,128)(2,1)}, u32[]{:S(2)}) copy-start(bf16[4,256,1536]{2,1,0:T(8,128)(2,1)} %get-tuple-element.51) | copy-start | bytes 9437188
  213.1 13.6 %copy-start.10 = (bf16[1536,1536]{1,0:T(8,128)(2,1)S(1)}, bf16[1536,1536]{1,0:T(8,128)(2,1)}, u32[]{:S(2)}) copy-start(bf16[1536,1536]{1,0:T(8,128)(2,1)} %get-tuple-element.52) | copy-start | bytes 14155780
  245.1 1.9 copy-start.7
  245.1 257.8 %reduce-scatter.3.cloned.1.call-start = ((), (), s32[]{:S(2)}) async-start(), calls=%async_computation.2 | async-start | bytes 10616832 | tf_op jit(solution)/shard_map/reduce_scatter | solution.py:305
  262.0 9.5 %slice-start = ((s8[9437184]{0:T(1024)(128)(4,1)}), s8[1048576]{0:T(1024)(128)(4,1)S(1)}, s32[]{:S(2)}) async-start(s8[9437184]{0:T(1024)(128)(4,1)} %bitcast.32), calls=%async_computation.4 | async-start | bytes 2097152
  262.0 9.5 %slice-start.1 = ((s8[9437184]{0:T(1024)(128)(4,1)}), s8[4194304]{0:T(1024)(128)(4,1)S(1)}, s32[]{:S(2)}) async-start(s8[9437184]{0:T(1024)(128)(4,1)} %bitcast.32), calls=%async_computation.5 | async-start | bytes 8388608
  262.0 9.5 %slice-start.2 = ((s8[9437184]{0:T(1024)(128)(4,1)}), s8[4194304]{0:T(1024)(128)(4,1)S(1)}, s32[]{:S(2)}) async-start(s8[9437184]{0:T(1024)(128)(4,1)} %bitcast.32), calls=%async_computation.6 | async-start | bytes 8388608
  262.0 9.5 %copy-start.9 = (bf16[1024,1536]{1,0:T(8,128)(2,1)S(1)}, bf16[1024,1536]{1,0:T(8,128)(2,1)}, u32[]{:S(2)}) copy-start(bf16[1024,1536]{1,0:T(8,128)(2,1)} %get-tuple-element.99) | copy-start | bytes 9437188
  496.8 9.1 %copy-start = (f32[256,1536]{1,0:T(8,128)S(1)}, f32[256,1536]{1,0:T(8,128)}, u32[]{:S(2)}) copy-start(f32[256,1536]{1,0:T(8,128)} %get-tuple-element.118) | copy-start | bytes 4718596
  502.9 4.2 copy-start.1
  505.9 2.3 copy-start.2
  507.1 2.1 copy-start.6
  507.1 2.8 copy-start.5
  507.1 3.5 copy-start.4
  507.1 4.2 copy-start.3
Sparse Core Ops, SparseCore 0:
  245.2 54.0 reduce-scatter.4
  301.6 97.8 reduce-scatter.2

commit v5 on v4

--- a/solution.py
+++ b/solution.py
@@ -365,6 +365,8 @@
         pl.semaphore_wait(barrier, len(partners))
 
     def finish(self):
+        assert self.used <= self.send.shape[0]
+        assert self.used_local <= self.local.shape[0]
         for copy in self.pending:
             copy.wait_send()
         for copy in self.pending_local:
@@ -406,49 +408,49 @@
 
 
 class SpreadCross:
-    def __init__(self, links, weights):
-        self.links, self.weights = links, weights
+    def __init__(self, links, weights, place):
+        self.links, self.weights, self.place = links, weights, place
         self.which = links.dp % 2
-        self.near = links.go(self.half(0), self.half(1), 0, 1)
-        self.far = links.go(self.half(0), self.half(2), 0, 2)
+        half = weights.shape[3] // 2
+        self.low, self.high = pl.ds(0, half), pl.ds(half, half)
+        whole = slice(None)
+        self.near = links.go(self.piece(0, whole), self.piece(1, whole), 0, 1)
+        self.far = links.go(self.piece(0, whole), self.piece(2, whole), 0, 2)
         self.core = [self.cross(0)]
 
-    def half(self, member, places=slice(None)):
-        return self.weights.at[member, places, self.which]
+    def piece(self, member, rows):
+        return self.weights.at[member, self.place, self.which, rows]
 
     def cross(self, member):
-        return self.links.go(self.half(member), self.half(member), 1, 0)
-
-    def pump(self):
+        return self.links.go(self.piece(member, slice(None)), self.piece(member, slice(None)), 1, 0)
+
+    def forward(self):
         links = self.links
-        first, second = pl.ds(0, 2), pl.ds(2, 2)
         self.near.wait_recv()
-        self.last_low = links.go(self.half(1, first), self.half(3, first), 0, 2)
+        self.last_low = links.go(self.piece(1, self.low), self.piece(3, self.low), 0, 2)
         self.core.append(self.cross(1))
         self.far.wait_recv()
-        self.last_high = links.go(self.half(2, second), self.half(3, second), 0, 1)
+        self.last_high = links.go(self.piece(2, self.high), self.piece(3, self.high), 0, 1)
         self.core.append(self.cross(2))
 
-    def wait(self, member):
-        if member == 3:
-            self.last_low.wait_recv()
-            self.last_high.wait_recv()
-            self.core.append(self.cross(3))
-        self.core[member].wait_recv()
+    def last(self):
+        self.last_low.wait_recv()
+        self.last_high.wait_recv()
+        self.core.append(self.cross(3))
 
 
 class Gather:
     def __init__(self, links, shard, whole, both_cores=True):
         self.links, self.whole, self.both_cores = links, whole, both_cores
         self.size = shard.shape[0]
-        self.place = links.dp // 2
+        self.place, self.which = links.dp // 2, links.dp % 2
         self.middle = (self.place == 1) | (self.place == 2)
         own = self.rows(0)
         self.own = links.store(shard, own)
         self.core = []
         self.pass_on(shard, own)
+        self.skip = links.go(shard, own, 4, 0)
         self.beside = links.go(shard, own, 2, 0)
-        self.skip = links.go(shard, own, 4, 0)
         self.third_at = links.used
         self.third = links.remote(shard, own, 6, 0)
 
@@ -462,7 +464,7 @@
 
     def rows(self, step):
         if len(self.whole.shape) == 4:
-            return self.whole.at[self.place ^ step, self.links.dp % 2]
+            return self.whole.at[self.place ^ step, self.which]
         start = pl.multiple_of((self.links.dp ^ (2 * step)) * self.size, self.size)
         return self.whole.at[pl.ds(start, self.size)]
 
@@ -497,6 +499,10 @@
         links.settle(self.own)
         for copy in self.core:
             copy.wait_recv()
+
+    def sent(self):
+        self.links.settle_sends(self.core)
+        self.finish()
 
     def finish(self):
         @pl.when(self.middle)
@@ -625,8 +631,8 @@
 
 def forward_kernel(
     latents, gains, conditioning, f32_qkv,
-    f32_attn_out, f32_cross_q, f32_cross_kv, f32_cross_out, f32_gate, f32_up, f32_down, cotangent,
-    rows_one_out, normed_two_out, rows_three_out, seeds_out, qkv_out, attn_out_out, cross_out, keyval_w_out, mlp_out,
+    f32_attn_out, f32_cross_q, f32_cross_kv, f32_cross_out, f32_gate, f32_up, f32_down,
+    rows_one_out, normed_two_out, rows_three_out, qkv_out, attn_out_out, cross_out, keyval_w_out, mlp_out,
     down_out, rotated_out, attended_out, logs_out,
     query_out, keyval_out, crossed_out, cross_logs_out, resid_one_out, resid_two_out, tables_out,
     rows_one, normed_two, rows_three, w_qkv, w_attn_out, w_cross, w_keyval, rotated, attended, logs, query, keyval,
@@ -646,7 +652,6 @@
             (f32_cross_out, raw_cross_out), (f32_gate, raw_gate), (f32_up, raw_up), (f32_down, raw_down),
         )
     ]
-    seed_own = links.store(cotangent, seeds_out.at[0])
     for part in range(3):
         for pair in range(pairs):
             at = part * width + pair * PAIR
@@ -675,14 +680,16 @@
     own_mlp[:, :hidden] = raw_gate[...].astype(low)
     own_mlp[:, hidden:] = raw_up[...].astype(low)
     own_down[...] = raw_down[...].astype(low)
+    links.store(own_down, down_out)
     context[...] = jnp.zeros_like(context)
     context[:CTX] = conditioning[0]
     spread_one.wait(1)
     gather_qkv.forward()
     gather_attn_out = Gather(links, own_attn_out, w_attn_out)
     gather_cross = Gather(links, own_cross, w_cross.at[0], False)
-    gather_keyval = Gather(links, own_keyval, w_keyval)
     spread_one.wait(2)
+    links.settle(gather_cross.own)
+    spread_cross = [SpreadCross(links, w_cross, links.dp // 2)]
     gather_qkv.arrive()
     links.store(w_qkv, qkv_out)
 
@@ -731,14 +738,22 @@
             gather_attn_out.arrive()
             links.store(w_attn_out, attn_out_out)
         out_project(attended, block, lambda cols: w_attn_out[cols, :], sums_one)
+        if block == 3:
+            spread_cross[0].forward()
+            gather_keyval = Gather(links, own_keyval, w_keyval)
+            gather_cross.forward()
+            gather_mlp = Gather(links, own_mlp, mlp_out)
+            spread_cross.append(SpreadCross(links, w_cross, (links.dp // 2) ^ 2))
         if block == 1:
-            gather_cross.forward()
+            gather_cross.beside.wait_recv()
+            spread_cross.append(SpreadCross(links, w_cross, (links.dp // 2) ^ 1))
+        if block == 2:
             gather_keyval.forward()
-            gather_mlp = Gather(links, own_mlp, mlp_out)
-        if block == 2:
             sums_one.add()
-    gather_cross.arrive()
-    spread_cross = SpreadCross(links, w_cross)
+            spread_cross[1].forward()
+    gather_cross.third.wait_recv()
+    spread_cross.append(SpreadCross(links, w_cross, (links.dp // 2) ^ 3))
+    spread_cross[2].forward()
     links.store(attended, attended_out)
     links.store(logs, logs_out)
     sums_one.arrive()
@@ -755,10 +770,13 @@
     links.store(w_keyval, keyval_w_out)
     keyval[0] = dot_plain(context[...], w_keyval[...]).astype(low)
     spread_keyval = Spread(links, keyval)
-    spread_cross.pump()
+    spread_cross[3].forward()
+    for spread in spread_cross:
+        spread.last()
     resid_two[...] = resid_one[...]
     for member in range(4):
-        spread_cross.wait(member)
+        for spread in spread_cross:
+            spread.core[member].wait_recv()
         spread_keyval.wait(member)
         at_member = slice(member * width, (member + 1) * width)
         query[:, at_member] = dot_plain(normed_two[...], cross_columns(w_cross, member, slice(0, width))).astype(low)
@@ -776,7 +794,6 @@
             resid_two[:, at] += dot_cols(crossed[:, at_member], tile)
         if member == 1:
             gather_mlp.forward()
-            gather_down = Gather(links, own_down, down_out)
     links.store(w_cross, cross_out)
     links.store(keyval, keyval_out)
     links.store(query, query_out)
@@ -785,24 +802,13 @@
     links.store(resid_two, resid_two_out)
 
     def norm_three(rows):
-        rows_three[0, rows] = layer_norm(resid_two[rows], gains[2:3])[0].astype(low)
+        rows_three[rows] = layer_norm(resid_two[rows], gains[2:3])[0].astype(low)
 
     row_steps(BLOCK, norm_three)
-    spread_three = Spread(links, rows_three)
-    links.settle(seed_own)
-    spread_seed = Spread(links, seeds_out)
-    spread_three.wait(1)
-    spread_seed.wait(1)
-    spread_seed.wait(2)
-    spread_three.wait(2)
-    gather_down.forward()
     gather_mlp.arrive()
-    spread_seed.wait(3)
-    spread_three.wait(3)
     links.store(rows_three, rows_three_out)
-    gather_down.arrive()
     links.finish()
-    for gather in (gather_qkv, gather_attn_out, gather_cross, gather_keyval, gather_mlp, gather_down):
+    for gather in (gather_qkv, gather_attn_out, gather_cross, gather_keyval, gather_mlp):
         gather.finish()
 
 
@@ -823,7 +829,7 @@
     ]
 
 
-def forward_part(latents, gains, conditioning, weights, cotangent):
+def forward_part(latents, gains, conditioning, weights):
     w_qkv, w_attn_out, w_cross_q, w_cross_kv, w_cross_out, w_gate, w_up, w_down = weights
     model = latents.shape[1]
     depth = conditioning.shape[2]
@@ -836,14 +842,13 @@
     outs = [
         ((4, BLOCK, model), low),
         ((BLOCK, model), low),
-        ((4, BLOCK, model), low),
-        ((4, BLOCK, model), low),
+        ((BLOCK, model), low),
         ((model, wide), low),
         ((model, width), low),
         ((4, 4, 2, share, 2 * width), low),
         ((depth, 2 * width), low),
-        ((model, 2 * hidden), low),
-        ((model, hidden), low),
+        ((4, 2, share, 2 * hidden), low),
+        ((share, hidden), low),
         ((LENGTH, wide), low),
         ((LENGTH, width), low),
         ((LENGTH, width), high),
@@ -858,7 +863,7 @@
     work = [
         ((4, BLOCK, model), low),
         ((BLOCK, model), low),
-        ((4, BLOCK, model), low),
+        ((BLOCK, model), low),
         ((model, wide), low),
         ((model, width), low),
         ((4, 4, 2, share, 2 * width), low),
@@ -899,12 +904,12 @@
     return pl.pallas_call(
         forward_kernel,
         out_shape=[jax.ShapeDtypeStruct(*out) for out in outs],
-        in_specs=[whole_vmem()] * 4 + [anywhere()] * 8,
+        in_specs=[whole_vmem()] * 4 + [anywhere()] * 7,
         out_specs=[anywhere()] * len(outs),
         scratch_shapes=scratch,
         compiler_params=pltpu.CompilerParams(collective_id=1, has_side_effects=True, vmem_limit_bytes=VMEM_BYTES),
         cost_estimate=pl.CostEstimate(flops=2**37, bytes_accessed=2**26, transcendentals=2**23),
-    )(latents, gains, conditioning, *weights, cotangent)
+    )(latents, gains, conditioning, *weights)
 
 
 class Scatter:
@@ -1034,7 +1039,7 @@
     model = latents.shape[1]
     links = Links(send, recv, local)
     which = links.dp % 2
-    load_seed = links.store(in_seed, seeds.at[0])
+    load_seed = links.store(in_seed, seeds)
     load_self = [
         links.store(source, target)
         for source, target in (
@@ -1046,14 +1051,30 @@
     load_cross = [links.store(in_grads_cross.at[member, :, which], grads_cross.at[member]) for member in range(4)]
     load_late = [links.store(in_qkv, w_qkv), links.store(in_rows_one, rows_one), links.store(in_d_resid, d_resid)]
     links.greet([(1, 0), (2, 0), (4, 0), (6, 0), (0, 1), (0, 2)])
-    links.settle(load_seed)
-    spread = Spread(links, seeds)
     core_copies = [
         links.go(in_grads_cross.at[member, :, 1 - which], core_cross.at[member], 1, 0) for member in range(4)
     ]
     gain_rows[...] = in_gain[...]
     context[...] = jnp.zeros_like(context)
     context[:CTX] = conditioning[0]
+    sums_keyval = Sums(links, keyval_parts, *got_keyval)
+    sums_cross = Sums(links, grads_cross, *got_cross)
+    for load in load_keyval:
+        links.settle(load)
+    for part in (3, 1, 2):
+        sums_keyval.ready(part)
+    for member in (3, 1, 2, 0):
+        links.settle(load_cross[member])
+        core_copies[member].wait_recv()
+
+        def add(place, carry):
+            total = grads_cross[member, place].astype(jnp.float32) + core_cross[member, place].astype(jnp.float32)
+            grads_cross[member, place] = total.astype(low)
+            return carry
+
+        lax.fori_loop(0, 4, add, 0)
+        sums_cross.ready(member)
+    links.settle(load_seed)
     for load in load_self:
         links.settle(load)
     for pair in range(pairs):
@@ -1064,8 +1085,6 @@
     d_keys_t[...] = jnp.zeros_like(d_keys_t)
     d_values_t[...] = jnp.zeros_like(d_values_t)
     cosine, sine = (tables.at[part] for part in range(2))
-    sums_keyval = Sums(links, keyval_parts, *got_keyval)
-    sums_cross = Sums(links, grads_cross, *got_cross)
 
     def whole(rows, cols):
         return rows[:, :, cols].reshape(LENGTH, -1)
@@ -1077,9 +1096,13 @@
         columns(model, 384, product)
 
     for block in range(4):
-        spread.wait(block)
+        d_attended[block_rows(block)] = dot_plain(seeds[block], w_attn_out[...]).astype(low)
+    grads_into(w_attn_out, seeds, attended[...])
+    scatter_attn_out = Scatter(links, w_attn_out, core_attn_out, extra_attn_out, far_attn_out)
+    scatter_attn_out.pair_up()
+
+    for block in range(4):
         rows = block_rows(block)
-        d_attended[rows] = dot_plain(seeds[block], w_attn_out[...]).astype(low)
         turn = (cosine[rows], -sine[rows])
 
         def one_pair(pair, carry):
@@ -1094,29 +1117,27 @@
 
         lax.fori_loop(0, pairs, one_pair, 0)
         if block == 0:
-            for load in load_keyval + load_cross:
-                links.settle(load)
-            for copy in core_copies:
-                copy.wait_recv()
-            for member in range(4):
-
-                def add(place, carry):
-                    total = grads_cross[member, place].astype(jnp.float32) + core_cross[member, place].astype(jnp.float32)
-                    grads_cross[member, place] = total.astype(low)
-                    return carry
-
-                lax.fori_loop(0, 4, add, 0)
-        if block == 1:
-            for part in (3, 1, 2):
-                sums_keyval.ready(part)
-            for part in (3, 1, 2):
-                sums_cross.ready(part)
-        if block == 2:
             sums_keyval.add()
             sums_cross.add()
-    grads_into(w_attn_out, seeds, attended[...])
-    scatter_attn_out = Scatter(links, w_attn_out, core_attn_out, extra_attn_out, far_attn_out)
-    scatter_attn_out.pair_up()
+        if block == 1:
+            scatter_attn_out.combine()
+        if block == 2:
+            sums_keyval.arrive()
+            d_keyval = keyval_parts[0].astype(jnp.float32) + sums_keyval.total(slice(None))
+            d_keyval = d_keyval.astype(low)
+            context_sum[...] = dot_cols(d_keyval, w_keyval[...]).astype(low)
+            context_near = links.go(context_sum, context_got.at[0], 0, 1)
+            w_keyval[...] = dot_rows(context[...], d_keyval).astype(low)
+            scatter_keyval = Scatter(links, w_keyval, core_keyval, extra_keyval, far_keyval)
+            scatter_keyval.pair_up()
+    sums_cross.arrive()
+    for place in range(4):
+        total = grads_cross[0, place].astype(jnp.float32) + sums_cross.total(place)
+        grads_cross[0, place] = total.astype(low)
+    scatter_cross = Scatter(links, grads_cross.at[0], None, extra_cross, far_cross)
+    scatter_cross.start()
+    scatter_attn_out.relay()
+    scatter_keyval.combine()
     for pair in range(pairs):
         for block in range(4):
             rows = block_rows(block)
@@ -1135,32 +1156,17 @@
 
         columns(model, 512, project)
         sums.ready(block)
-    scatter_attn_out.combine()
     grads_into(w_qkv, rows_one, rotated[...])
     scatter_qkv = Scatter(links, w_qkv, core_qkv, extra_qkv, far_qkv)
     scatter_qkv.pair_up()
     sums.add()
     scatter_qkv.combine()
-    sums_keyval.arrive()
-    d_keyval = keyval_parts[0].astype(jnp.float32) + sums_keyval.total(slice(None))
-    d_keyval = d_keyval.astype(low)
-    context_sum[...] = dot_cols(d_keyval, w_keyval[...]).astype(low)
-    context_near = links.go(context_sum, context_got.at[0], 0, 1)
-    w_keyval[...] = dot_rows(context[...], d_keyval).astype(low)
-    scatter_keyval = Scatter(links, w_keyval, core_keyval, extra_keyval, far_keyval)
-    scatter_keyval.pair_up()
-    sums_cross.arrive()
-    for place in range(4):
-        total = grads_cross[0, place].astype(jnp.float32) + sums_cross.total(place)
-        grads_cross[0, place] = total.astype(low)
-    scatter_cross = Scatter(links, grads_cross.at[0], None, extra_cross, far_cross)
-    scatter_cross.start()
-    scatter_keyval.combine()
+    scatter_cross.relay()
+    scatter_keyval.relay()
     context_near.wait_recv()
     links.settle_sends((context_near,))
     context_sum[...] = (context_sum[...].astype(jnp.float32) + context_got[0].astype(jnp.float32)).astype(low)
     context_far = links.go(context_sum, context_got.at[1], 0, 2)
-    scatter_attn_out.relay()
     sums.arrive()
 
     def norm_one(rows):
@@ -1181,10 +1187,6 @@
         trade.start()
         if step == 1:
             scatter_qkv.relay()
-        if step == 2:
-            scatter_cross.relay()
-        if step == 3:
-            scatter_keyval.relay()
         trade.wait()
         gain_rows[...] += gain_got[step]
     grad_gains[...] = gain_rows[...]
@@ -1296,41 +1298,220 @@
     )
 
 
-def cross_back_kernel(
-    cotangent, gains, normed_two, resid_two, resid_one, in_parts, in_last, in_query, in_crossed, in_cross_logs,
-    in_keyval, in_cross,
-    block_out, d_resid_out, seed_out, grads_out, d_keyval_out, gain_out,
-    parts, parts_last, got, got_last, w_cross, query, crossed, cross_logs, keyval, d_keyval, d_keys_t, d_values_t,
-    d_resid, d_normed_two, cross_seed, seed, total, send, recv, local,
+class ScatterFar:
+    def __init__(self, links, grads, got_core, extra, got):
+        self.links, self.grads, self.got_core, self.extra, self.got = links, grads, got_core, extra, got
+        self.place, self.which = links.dp // 2, links.dp % 2
+        self.middle = (self.place == 1) | (self.place == 2)
+        self.core = [
+            links.go(grads.at[place, 1 - self.which], got_core.at[place], 1, 0) for place in range(4)
+        ]
+
+    def combine(self, stage, spots):
+        links, self.spots = self.links, spots
+        for copy in self.core:
+            copy.wait_recv()
+        size = spots[0].shape[0]
+        slots = [stage.at[slot, 0] for slot in range(2)]
+        mine = [links.store(self.grads.at[self.place ^ step, self.which], spots[step]) for step in range(4)]
+        order = (3, 2, 1, 0)
+        others = [links.store(self.got_core.at[self.place ^ step], slots[at]) for at, step in enumerate(order[:2])]
+        for at, step in enumerate(order):
+            links.settle(mine[step])
+            links.settle(others[at])
+
+            def add(rows):
+                total = spots[step][rows].astype(jnp.float32) + slots[at % 2][rows].astype(jnp.float32)
+                spots[step][rows] = total.astype(jnp.bfloat16)
+
+            row_steps(size, add)
+            if at < 2:
+                others.append(links.store(self.got_core.at[self.place ^ order[at + 2]], slots[at]))
+        self.to_extra = links.remote(spots[3], self.extra, 2, 0)
+        self.to_third = links.remote(spots[3], self.got.at[2], 6, 0)
+        self.to_skip = links.remote(spots[2], self.got.at[1], 4, 0)
+
+        @pl.when(self.middle)
+        def _():
+            self.to_third.start()
+
+        @pl.when(jnp.logical_not(self.middle))
+        def _():
+            self.to_extra.start()
+            self.to_skip.start()
+
+        self.beside = links.go(spots[1], self.got.at[0], 2, 0)
+
+    def relay(self):
+        @pl.when(self.middle)
+        def _():
+            self.to_extra.wait_recv()
+
+            def add(rows):
+                total = self.spots[2][rows].astype(jnp.float32) + self.extra[rows].astype(jnp.float32)
+                self.spots[2][rows] = total.astype(jnp.bfloat16)
+
+            row_steps(self.spots[0].shape[0], add)
+            self.to_skip.start()
+
+    def finish(self):
+        self.beside.wait_recv()
+        self.to_skip.wait()
+
+        @pl.when(self.middle)
+        def _():
+            self.to_third.wait()
+
+        @pl.when(jnp.logical_not(self.middle))
+        def _():
+            self.to_extra.wait_send()
+
+
+def middle_kernel(
+    cotangent, gains, normed_two, resid_two, resid_one, in_rows, in_mlp, own_down, in_query, in_crossed,
+    in_cross_logs, in_keyval, in_cross,
+    block_out, d_resid_out, seed_out, grads_out, d_keyval_out, gain_out, grads_down_out, grads_gate_out, grads_up_out,
+    core_down, core_gate, far_down, far_gate, own_down_out, own_gate_out,
+    rows_three, seeds, w_mlp, w_down, hidden, both, parts, parts_last, stage, extra_down, extra_gate, spots_down,
+    got, got_last,
+    cross_logs, keyval, d_keyval, d_keys_t, d_values_t, d_resid, d_normed_two,
+    send, recv, local, stage_sem,
 ):
     low = jnp.bfloat16
     model = cotangent.shape[1]
     width = model // 4
-    share = w_cross.shape[3]
+    share = own_down.shape[0]
+    units = w_down.shape[1]
     pairs = width // PAIR
     links = Links(send, recv, local)
-    load_parts = [links.store(in_parts.at[block], parts.at[block]) for block in (3, 1, 2, 0)]
-    load_last = [links.store(in_last.at[block], parts_last.at[block]) for block in (3, 1, 2, 0)]
+    load_rows = links.store(in_rows, rows_three.at[0])
+    load_mlp = links.store(in_mlp, w_mlp)
+    seeds[0] = cotangent[...]
+    links.greet([(1, 0), (2, 0), (4, 0), (6, 0), (0, 1), (0, 2)])
+    gather_down = Gather(links, own_down, w_down)
+    links.settle(load_rows)
+    spread_three = Spread(links, rows_three)
+    spread_seeds = Spread(links, seeds)
     loads = [
         links.store(source, target)
         for source, target in (
-            (in_query, query), (in_crossed, crossed), (in_cross_logs, cross_logs), (in_keyval, keyval),
-            (in_cross, w_cross),
+            (in_cross_logs, cross_logs), (in_keyval, keyval),
         )
     ]
     gain_out[...] = jnp.zeros_like(gain_out)
-    links.greet([(0, 1), (0, 2)])
+    links.settle(load_mlp)
+    for block in range(4):
+        spread_three.wait(block)
+        if block == 3:
+            spread_seeds.wait(1)
+        rows = block_rows(block)
+
+        def up(cols):
+            above_at = pl.ds(pl.multiple_of(units + cols.start, cols.size), cols.size)
+            gate = dot_plain(rows_three[block], w_mlp[:, :, :, cols].reshape(model, -1))
+            above = dot_plain(rows_three[block], w_mlp[:, :, :, above_at].reshape(model, -1))
+            sigma = 1.0 / (1.0 + jnp.exp(-gate))
+            swish = gate * sigma
+            hidden[rows, cols] = (swish * above).astype(low)
+            both[rows, cols] = (above * sigma * (1.0 + gate * (1.0 - sigma))).astype(low)
+            both[rows, above_at] = swish.astype(low)
+
+        columns(units, 256, up)
+    gather_down.forward()
+    spread_seeds.wait(3)
+
+    def tiles_out(count, product, place):
+        def copy(index, slot):
+            return pltpu.make_async_copy(stage.at[slot], place(index), stage_sem.at[slot])
+
+        def step(index, carry):
+            slot = index % 2
+
+            @pl.when(index >= 2)
+            def _():
+                copy(index - 2, slot).wait()
+
+            for start in (0, units // 2):
+                cols = pl.ds(start, units // 2)
+                stage[slot, :, :, cols] = product(index, cols).reshape(2, share, -1)
+            copy(index, slot).start()
+            return carry
+
+        lax.fori_loop(0, count, step, 0)
+        for index in (count - 2, count - 1):
+            copy(index, index % 2).wait()
+
+    def rows_of(index, size):
+        return pl.ds(pl.multiple_of(index * size, size), size)
+
+    tile = 2 * share
+
+    def whole(rows, index):
+        return rows[:, :, rows_of(index, tile)].reshape(LENGTH, -1)
+
+    tiles_out(
+        model // tile,
+        lambda index, cols: dot_rows(whole(seeds, index), hidden[:, cols]).astype(low),
+        lambda index: grads_down_out.at[index],
+    )
+    scatter_down = ScatterFar(links, grads_down_out, core_down, extra_down, far_down)
+    gather_down.arrive()
+    scatter_down.combine(stage, [spots_down.at[place] for place in range(4)])
     sums = Sums(links, parts, *got)
-    for load, block in zip(load_parts, (3, 1, 2, 0)):
+    for block in (3, 1, 2, 0):
+        rows = block_rows(block)
+
+        def back(cols):
+            above_at = pl.ds(pl.multiple_of(units + cols.start, cols.size), cols.size)
+            d_hidden = dot_plain(seeds[block], w_down[:, cols])
+            both[rows, cols] = (both[rows, cols].astype(jnp.float32) * d_hidden).astype(low)
+            both[rows, above_at] = (both[rows, above_at].astype(jnp.float32) * d_hidden).astype(low)
+
+        columns(units, 256, back)
+
+        def down(place, carry):
+            weights = w_mlp[place].reshape(2 * share, -1)
+            parts[block, :, rows_of(place, 2 * share)] = dot_cols(both[rows], weights).astype(low)
+            return carry
+
+        lax.fori_loop(0, 4, down, 0)
+        sums.ready(block)
+    sums.add()
+    scatter_down.relay()
+    w_cross = [w_mlp.at[:, :, :, pl.ds(member * 2 * width, 2 * width)] for member in range(4)]
+    load_cross = [links.store(in_cross.at[member], w_cross[member]) for member in range(4)]
+    for block in range(4):
+
+        def last(cols):
+            parts_last[block, :, cols] = dot_cols(hidden[block_rows(block)], w_down[cols, :]).astype(low)
+
+        columns(model, 512, last)
+
+    def grads_mlp(half, target):
+        start = half * units
+        tiles_out(
+            model // tile,
+            lambda index, cols: dot_rows(
+                whole(rows_three, index), both[:, pl.ds(start + cols.start, cols.size)]
+            ).astype(low),
+            lambda index: target.at[index],
+        )
+
+    grads_mlp(0, grads_gate_out)
+    scatter_gate = ScatterFar(links, grads_gate_out, core_gate, extra_gate, far_gate)
+    gather_down.sent()
+    query, crossed, cross_seed, seed = (w_down.at[block_rows(spot)] for spot in range(4))
+    loads += [links.store(in_query, query), links.store(in_crossed, crossed)]
+    for load in loads + load_cross:
         links.settle(load)
-        sums.ready(block)
-    for load in loads + load_last:
-        links.settle(load)
-    sums.add()
+    sums.arrive()
     sums_last = Sums(links, parts_last, *got_last)
     for block in (3, 1, 2):
         sums_last.ready(block)
-    sums.arrive()
+    scatter_gate.combine(stage, [hidden.at[pl.ds(place * BLOCK, share)] for place in range(4)])
+
+    def cross_columns(member, cols):
+        return w_cross[member][:, :, :, cols].reshape(model, -1)
 
     def norm_three(rows):
         gain = gains[2:3]
@@ -1345,7 +1526,7 @@
     row_steps(BLOCK, norm_three)
     for member in range(4):
         at_member = slice(member * width, (member + 1) * width)
-        d_crossed = dot_plain(cross_seed[...], cross_columns(w_cross, member, slice(width, 2 * width))).astype(low)
+        d_crossed = dot_plain(cross_seed[...], cross_columns(member, slice(width, 2 * width))).astype(low)
         for pair in range(pairs):
             at = slice(member * width + pair * PAIR, member * width + (pair + 1) * PAIR)
             keys_at = slice(pair * PAIR, (pair + 1) * PAIR)
@@ -1364,12 +1545,13 @@
             d_keyval[member, :, values_at] = d_values_t[...].T.astype(low)
         for place in range(4):
             at = slice(place * 2 * share, (place + 1) * 2 * share)
-            part = dot_cols(query[:, at_member], cross_tile(w_cross, member, place, slice(0, width)))
+            part = dot_cols(query[:, at_member], w_cross[member][place, :, :, :width].reshape(2 * share, width))
             if member == 0:
                 d_normed_two[:, at] = part
             else:
                 d_normed_two[:, at] += part
     links.store(d_keyval, d_keyval_out)
+    scatter_gate.relay()
 
     def norm_two(rows):
         gain = gains[1:2]
@@ -1381,48 +1563,74 @@
         seed[rows] = value.astype(low)
 
     row_steps(BLOCK, norm_two)
+    links.settle(links.store(seed, seed_out.at[0]))
+    spread_seed = Spread(links, seed_out)
     links.store(d_resid, d_resid_out)
-    links.store(seed, seed_out)
     sums_last.add()
+    grads_mlp(1, grads_up_out)
     for place in range(4):
         rows_at = slice(place * 2 * share, (place + 1) * 2 * share)
         for member in range(4):
             at_member = slice(member * width, (member + 1) * width)
             left = dot_rows(normed_two[:, rows_at], query[:, at_member]).astype(low)
-            w_cross[member, place, :, :, :width] = left.reshape(2, share, width)
+            w_cross[member][place, :, :, :width] = left.reshape(2, share, width)
             right = dot_rows(cross_seed[:, rows_at], crossed[:, at_member]).astype(low)
-            w_cross[member, place, :, :, width:] = right.reshape(2, share, width)
-    links.store(w_cross, grads_out)
+            w_cross[member][place, :, :, width:] = right.reshape(2, share, width)
+    for member in range(4):
+        links.store(w_cross[member], grads_out.at[member])
+    spread_seed.wait(1)
     sums_last.arrive()
 
     def add_last(rows):
-        total[rows] = resid_two[rows] + parts_last[0, rows].astype(jnp.float32) + sums_last.total(rows)
+        d_normed_two[rows] = resid_two[rows] + parts_last[0, rows].astype(jnp.float32) + sums_last.total(rows)
 
     row_steps(BLOCK, add_last)
-    links.store(total, block_out)
+    links.store(d_normed_two, block_out)
+    spread_seed.wait(3)
+    links.store(scatter_down.spots[0], own_down_out)
+    links.store(scatter_gate.spots[0], own_gate_out)
     links.finish()
-
-
-def cross_back_part(cotangent, gains, parts, last, kept):
+    scatter_down.finish()
+    scatter_gate.finish()
+
+
+def middle_part(cotangent, gains, rows_three, mlp_all, own_down, kept):
     normed_two, resid_two, resid_one, query, crossed, cross_logs, keyval, cross_all = kept
     model = cotangent.shape[1]
+    share, units = own_down.shape
     low, high = jnp.bfloat16, jnp.float32
     outs = [
         ((BLOCK, model), high),
         ((BLOCK, model), high),
-        ((BLOCK, model), low),
+        ((4, BLOCK, model), low),
         (cross_all.shape, low),
         (keyval.shape, low),
         ((8, model), high),
+        ((4, 2, share, units), low),
+        ((4, 2, share, units), low),
+        ((4, 2, share, units), low),
+        ((4, share, units), low),
+        ((4, share, units), low),
+        ((3, share, units), low),
+        ((3, share, units), low),
+        ((share, units), low),
+        ((share, units), low),
     ]
     work = [
         ((4, BLOCK, model), low),
         ((4, BLOCK, model), low),
+        (mlp_all.shape, low),
+        ((model, units), low),
+        ((LENGTH, units), low),
+        ((LENGTH, 2 * units), low),
+        ((4, BLOCK, model), low),
+        ((4, BLOCK, model), low),
+        ((2, 2, share, units), low),
+        ((share, units), low),
+        ((share, units), low),
+        ((4, share, units), low),
     ]
     more = [
-        (cross_all.shape, low),
-        ((BLOCK, model), low),
-        ((BLOCK, model), low),
         ((BLOCK, model), high),
         (keyval.shape, low),
         (keyval.shape, low),
@@ -1430,24 +1638,67 @@
         ((PAIR, FULL), high),
         ((BLOCK, model), high),
         ((BLOCK, model), high),
-        ((BLOCK, model), low),
-        ((BLOCK, model), low),
-        ((BLOCK, model), high),
     ]
     scratch = [pltpu.VMEM(*buffer) for buffer in work] + [sum_buffers(model), sum_buffers(model)]
     scratch += [pltpu.VMEM(*buffer) for buffer in more]
-    scratch += [pltpu.SemaphoreType.DMA((24,)), pltpu.SemaphoreType.DMA((24,)), pltpu.SemaphoreType.DMA((24,))]
+    scratch += [pltpu.SemaphoreType.DMA((96,)), pltpu.SemaphoreType.DMA((96,)), pltpu.SemaphoreType.DMA((64,))]
+    scratch += [pltpu.SemaphoreType.DMA((2,))]
     return pl.pallas_call(
-        cross_back_kernel,
+        middle_kernel,
         out_shape=[jax.ShapeDtypeStruct(*out) for out in outs],
-        in_specs=[whole_vmem()] * 5 + [anywhere()] * 7,
-        out_specs=[anywhere()] * 5 + [whole_vmem()],
+        in_specs=[whole_vmem()] * 5 + [anywhere()] * 8,
+        out_specs=[anywhere()] * 5 + [whole_vmem()] + [anywhere()] * 9,
         scratch_shapes=scratch,
         compiler_params=pltpu.CompilerParams(collective_id=3, has_side_effects=True, vmem_limit_bytes=VMEM_BYTES),
-        cost_estimate=pl.CostEstimate(flops=2**35, bytes_accessed=2**26, transcendentals=2**21),
+        cost_estimate=pl.CostEstimate(flops=2**36, bytes_accessed=2**26, transcendentals=2**21),
     )(
-        cotangent, gains, normed_two, resid_two, resid_one, parts, last, query, crossed, cross_logs, keyval, cross_all
-    )
+        cotangent, gains, normed_two, resid_two, resid_one, rows_three, mlp_all, own_down, query, crossed,
+        cross_logs, keyval, cross_all,
+    )
+
+
+def finish_kernel(
+    in_out, in_latents, in_qkv, in_attn_out, in_cross_q, in_keyval, in_cross_out, own_gate, far_gate, own_down, far_down,
+    in_up,
+    block_out, grad_latents, grad_qkv, grad_attn_out, grad_cross_q, grad_keyval, grad_cross_out, grad_gate, grad_up,
+    grad_down,
+):
+    for source, target in (
+        (in_out, block_out), (in_latents, grad_latents), (in_qkv, grad_qkv), (in_attn_out, grad_attn_out),
+        (in_cross_q, grad_cross_q), (in_keyval, grad_keyval), (in_cross_out, grad_cross_out),
+    ):
+
+        def move(rows):
+            target[rows] = source[rows].astype(jnp.float32)
+
+        row_steps(source.shape[0], move)
+    place = lax.axis_index("dp") // 2
+    middle = (place == 1) | (place == 2)
+    for own, far, target in ((own_gate, far_gate, grad_gate), (own_down, far_down, grad_down)):
+
+        def add(rows):
+            third = jnp.where(middle, far[2, rows].astype(jnp.float32), 0.0)
+            total = own[rows].astype(jnp.float32) + far[0, rows].astype(jnp.float32)
+            target[rows] = total + far[1, rows].astype(jnp.float32) + third
+
+        row_steps(own.shape[0], add)
+
+    def widen(rows):
+        grad_up[rows] = in_up[rows].astype(jnp.float32)
+
+    row_steps(in_up.shape[0], widen)
+
+
+def finish_part(raw, own_gate, far_gate, own_down, far_down, sum_up):
+    wide = jax.ShapeDtypeStruct(sum_up.shape, jnp.float32)
+    return pl.pallas_call(
+        finish_kernel,
+        out_shape=[jax.ShapeDtypeStruct(array.shape, jnp.float32) for array in raw] + [wide] * 3,
+        in_specs=[whole_vmem()] * 12,
+        out_specs=[whole_vmem()] * 10,
+        compiler_params=pltpu.CompilerParams(vmem_limit_bytes=VMEM_BYTES),
+        cost_estimate=pl.CostEstimate(flops=2**22, bytes_accessed=2**24, transcendentals=0),
+    )(*raw, own_gate, far_gate, own_down, far_down, sum_up)
 
 
 def per_device(
@@ -1467,40 +1718,28 @@
     cotangent,
 ):
     low = jnp.bfloat16
-    hidden_wide = w_gate.shape[1]
     gains = jnp.stack([gain_attn, gain_cross, gain_mlp])
     (
-        rows_one, normed_two, rows_three, mlp_seed, qkv_all, attn_out_t, cross_all, cross_kv, mlp_all, down_all,
+        rows_one, normed_two, rows_three, qkv_all, attn_out_t, cross_all, cross_kv, mlp_all, own_down,
         rotated, attended, logs, cross_query, keyval, crossed, cross_logs, resid_one, resid_two, tables,
     ) = forward_part(
         latents,
         gains,
         conditioning,
         (w_qkv, w_attn_out.T, w_cross_q, w_cross_kv, w_cross_out.T, w_gate, w_up, w_down.T),
-        cotangent,
-    )
-    rows_three, mlp_seed = (array.reshape(LENGTH, -1) for array in (rows_three, mlp_seed))
-    both = dot_plain(rows_three, mlp_all)
-    gate_pre, up_pre = both[:, :hidden_wide], both[:, hidden_wide:]
-    sigma_gate = jax.nn.sigmoid(gate_pre)
-    swish = gate_pre * sigma_gate
-    hidden = (swish * up_pre).astype(low)
-    sum_down = dp_sum(dot_rows(mlp_seed, hidden))
-    d_hidden = dot_plain(mlp_seed, down_all)
-    d_gate = (d_hidden * up_pre * sigma_gate * (1.0 + gate_pre * (1.0 - sigma_gate))).astype(low)
-    d_up = (d_hidden * swish).astype(low)
-    d_both = jnp.concatenate([d_gate, d_up], axis=1)
-    sum_mlp = dp_sum(dot_rows(rows_three, d_both))
-    block_shape = (4, latents.shape[0], -1)
-    parts = dot_cols(d_both, mlp_all).astype(low).reshape(block_shape)
-    last = dot_cols(hidden, down_all).astype(low).reshape(block_shape)
-    block_out, d_resid, seed, grads_cross, d_keyval, gain_rows = cross_back_part(
+    )
+    (
+        block_out, d_resid, seed, grads_cross, d_keyval, gain_rows, _, _, grads_up, _, _, far_down, far_gate, own_down,
+        own_gate,
+    ) = middle_part(
         cotangent,
         gains,
-        parts,
-        last,
+        rows_three,
+        mlp_all,
+        own_down,
         (normed_two, resid_two, resid_one, cross_query, crossed, cross_logs, keyval, cross_all),
     )
+    sum_up = dp_sum(grads_up.reshape(w_gate.shape[0] * 8, -1))
     grad_latents, grad_context, grad_gains, grad_qkv, grad_attn_out, grad_cross_q, grad_cross_kv, grad_cross_out = (
         backward_part(
             latents,
@@ -1514,6 +1753,11 @@
             (qkv_all, attn_out_t, cross_kv, rows_one, rotated, attended, logs, tables),
         )
     )
+    raw = (block_out, grad_latents, grad_qkv, grad_attn_out, grad_cross_q, grad_cross_kv, grad_cross_out)
+    (
+        block_out, grad_latents, grad_qkv, grad_attn_out, grad_cross_q, grad_cross_kv, grad_cross_out, grad_gate,
+        grad_up, grad_down,
+    ) = finish_part(raw, own_gate, far_gate, own_down, far_down, sum_up)
     return (
         block_out,
         grad_latents,
@@ -1526,9 +1770,9 @@
         grad_cross_kv,
         grad_cross_out.T,
         grad_gains[2],
-        sum_mlp[:, :hidden_wide].astype(jnp.float32),
-        sum_mlp[:, hidden_wide:].astype(jnp.float32),
-        sum_down.astype(jnp.float32).T,
+        grad_gate,
+        grad_up,
+        grad_down.T,
     )
 
 

time: 528 us -> 511 us (0.968)
  matrix products: 69.6 us -> 0 us
  Pallas kernels: 415 us -> 481 us
  local copies, waits for them, and re-layouts: 13.9 us -> 5.83 us
    pallas_call x1 -> x2, Pallas kernels: 62.1 us -> 192 us  [the longest x1 184 us: middle_part(): pl.pallas_call(middle_kernel, out_shape=[jax.ShapeDtypeStruct(*out) for o...]
    dot_general x6 -> x0, matrix products: 69.6 us -> none  [the longest x2 23.6 us: dot_rows(): lax.dot_general(left_op, right_op, (((0,), (0,)), ((), ())), preferred_el...]
    pallas_call x1, Pallas kernels: 203 us -> 162 us  [forward_part(): pl.pallas_call(forward_kernel, out_shape=[jax.ShapeDtypeStruct(*out) for...]
    pallas_call x1, Pallas kernels: 150 us -> 127 us  [backward_part(): pl.pallas_call(backward_kernel, out_shape=[jax.ShapeDtypeStruct(*out) for...]
    unnamed x36 -> x1, local copies, waits for them, and re-layouts: 10.2 us -> 2.16 us
  transfers between devices with their start and end apart: 2 -> 1, of which waited for: 0 -> 0; matrix products, arithmetic and copies ran while one was open for 8% -> 1% of each run, Pallas kernels for 41% -> 25%
where the time goes in v5:
time: 511 us; the launch traced here: 502 us
  Pallas kernels  481 us (94%)
  between operations  14.5 us (3%)
  local copies, waits for them, and re-layouts  5.83 us (1%)
    pallas_call x1, Pallas kernels, middle_part(): pl.pallas_call(middle_kernel, out_shape=[jax.ShapeDtypeStruct(*out) for o...  184 us
    pallas_call x1, Pallas kernels, forward_part(): pl.pallas_call(forward_kernel, out_shape=[jax.ShapeDtypeStruct(*out) for...  162 us
    pallas_call x1, Pallas kernels, backward_part(): pl.pallas_call(backward_kernel, out_shape=[jax.ShapeDtypeStruct(*out) for...  127 us
  transfers between devices with their start and end apart: 1, of which 0 were waited for; matrix products, arithmetic and copies ran while one was open for 1% of the time, Pallas kernels for 25%

profile of v5, /device:TPU:0, one launch (start us, length us, event | category | flops | bytes accessed | tf_op | source)
XLA Modules:
  0.0 502.2 jit_solution(6207196977446702962)
XLA Ops:
  7.2 0.0 reduce-scatter.2.cloned.1.call-start
  7.2 0.7 stack.12
  7.9 0.7 stack.13
  8.6 0.7 stack.14
  9.3 0.6 pad_maximum_fusion.gains
  10.0 161.8 %shard_map.245 = (bf16[4,256,1536]{2,1,0:T(8,128)(2,1)}, bf16[256,1536]{1,0:T(8,128)(2,1)}, bf16[256,1536]{1,0:T(8,128)(2,1)}, bf16[1536,1152]{1,0:T(8,128)(2,1)...) custom-call(bf16[256,1536]{1,0:T(8,128)(2,1)} %latents.3, ...), custom_call_target="tpu_custom_call" | custom-call | flops 137438953472 | bytes 67108864 | tf_op jit(solution)/shard_map/pallas_call | solution.py:904
  171.8 183.7 %shard_map.246 = (f32[256,1536]{1,0:T(8,128)}, f32[256,1536]{1,0:T(8,128)}, bf16[4,256,1536]{2,1,0:T(8,128)(2,1)}, bf16[4,4,2,192,768]{4,3,2,1,0:T(8,128)(2,1)},...) custom-call(bf16[256,1536]{1,0:T(8,128)(2,1)} %cotangent.1, ...), custom_call_target="tpu_custom_call" | custom-call | flops 68719476736 | bytes 67108864 | tf_op jit(solution)/shard_map/pallas_call | solution.py:1646
  355.5 0.0 reduce-scatter.2.cloned.1.call-update
  355.5 126.9 %shard_map.247 = (f32[256,1536]{1,0:T(8,128)}, f32[1,130,768]{2,1,0:T(8,128)}, f32[8,1536]{1,0:T(8,128)}, f32[192,1152]{1,0:T(8,128)}, f32[192,384]{1,0:T(8,128)...) custom-call(bf16[256,1536]{1,0:T(8,128)(2,1)} %latents.3, f32[3,1536]{1,0:T(4,128)} %pad_maximum_fusion.gains, ...), custom_call_target="tpu_custom_call" | custom-call | flops 137438953472 | bytes 67108864 | tf_op jit(solution)/shard_map/pallas_call | solution.py:1287
  482.5 2.2 copy.28
  484.6 1.6 slice_reduce_fusion
  486.2 0.0 reduce-scatter.2.cloned.1.call-done.in_up
  486.2 8.7 %shard_map.248 = (f32[256,1536]{1,0:T(8,128)}, f32[256,1536]{1,0:T(8,128)}, f32[192,1152]{1,0:T(8,128)}, f32[192,384]{1,0:T(8,128)}, f32[192,384]{1,0:T(8,128)},...) custom-call(f32[256,1536]{1,0:T(8,128)} %get-tuple-element.73.in_out, ...), custom_call_target="tpu_custom_call" | custom-call | flops 4194304 | bytes 16777216 | tf_op jit(solution)/shard_map/pallas_call | solution.py:1694
Async XLA Ops:
  7.2 479.0 %reduce-scatter.2.cloned.1.call-start = ((), (), s32[]{:S(2)}) async-start(), calls=%async_computation.1 | async-start | bytes 5308416 | tf_op jit(solution)/shard_map/reduce_scatter | solution.py:305
Sparse Core Ops, SparseCore 0:
  355.6 67.0 reduce-scatter.1

commit v6 on v5

--- a/solution.py
+++ b/solution.py
@@ -695,6 +695,11 @@
 
     for block in range(4):
         spread_one.wait(block)
+        if block == 2:
+            gather_attn_out.forward()
+        if block == 3:
+            gather_cross.forward()
+            gather_keyval = Gather(links, own_keyval, w_keyval)
         rows = block_rows(block)
         turn = (cosine[rows], sine[rows])
 
@@ -734,14 +739,11 @@
 
         lax.fori_loop(0, pairs, one_pair, 0)
         if block == 3:
-            gather_attn_out.forward()
             gather_attn_out.arrive()
             links.store(w_attn_out, attn_out_out)
         out_project(attended, block, lambda cols: w_attn_out[cols, :], sums_one)
         if block == 3:
             spread_cross[0].forward()
-            gather_keyval = Gather(links, own_keyval, w_keyval)
-            gather_cross.forward()
             gather_mlp = Gather(links, own_mlp, mlp_out)
             spread_cross.append(SpreadCross(links, w_cross, (links.dp // 2) ^ 2))
         if block == 1:
@@ -1391,7 +1393,6 @@
     gather_down = Gather(links, own_down, w_down)
     links.settle(load_rows)
     spread_three = Spread(links, rows_three)
-    spread_seeds = Spread(links, seeds)
     loads = [
         links.store(source, target)
         for source, target in (
@@ -1401,9 +1402,11 @@
     gain_out[...] = jnp.zeros_like(gain_out)
     links.settle(load_mlp)
     for block in range(4):
+        if block == 3:
+            gather_down.forward()
         spread_three.wait(block)
-        if block == 3:
-            spread_seeds.wait(1)
+        if block == 2:
+            spread_seeds = Spread(links, seeds)
         rows = block_rows(block)
 
         def up(cols):
@@ -1417,7 +1420,7 @@
             both[rows, above_at] = swish.astype(low)
 
         columns(units, 256, up)
-    gather_down.forward()
+    spread_seeds.wait(1)
     spread_seeds.wait(3)
 
     def tiles_out(count, product, place):
@@ -1456,7 +1459,6 @@
     )
     scatter_down = ScatterFar(links, grads_down_out, core_down, extra_down, far_down)
     gather_down.arrive()
-    scatter_down.combine(stage, [spots_down.at[place] for place in range(4)])
     sums = Sums(links, parts, *got)
     for block in (3, 1, 2, 0):
         rows = block_rows(block)
@@ -1476,6 +1478,8 @@
 
         lax.fori_loop(0, 4, down, 0)
         sums.ready(block)
+        if block == 3:
+            scatter_down.combine(stage, [spots_down.at[place] for place in range(4)])
     sums.add()
     scatter_down.relay()
     w_cross = [w_mlp.at[:, :, :, pl.ds(member * 2 * width, 2 * width)] for member in range(4)]

time: 511 us -> 507 us (level)
  transfers between devices with their start and end apart: 1 -> 1, of which waited for: 0 -> 0; matrix products, arithmetic and copies ran while one was open for 1% -> 1% of each run, Pallas kernels for 25% -> 26%
where the time goes in v6:
time: 507 us; the launch traced here: 498 us
  Pallas kernels  477 us (94%)
  between operations  14.5 us (3%)
  local copies, waits for them, and re-layouts  5.83 us (1%)
    pallas_call x1, Pallas kernels, middle_part(): pl.pallas_call(middle_kernel, out_shape=[jax.ShapeDtypeStruct(*out) for o...  180 us
    pallas_call x1, Pallas kernels, forward_part(): pl.pallas_call(forward_kernel, out_shape=[jax.ShapeDtypeStruct(*out) for...  161 us
    pallas_call x1, Pallas kernels, backward_part(): pl.pallas_call(backward_kernel, out_shape=[jax.ShapeDtypeStruct(*out) for...  127 us
  transfers between devices with their start and end apart: 1, of which 0 were waited for; matrix products, arithmetic and copies ran while one was open for 1% of the time, Pallas kernels for 26%

profile of v6, /device:TPU:0, one launch (start us, length us, event | category | flops | bytes accessed | tf_op | source)
XLA Modules:
  0.0 498.3 jit_solution(11386649276886195100)
XLA Ops:
  7.2 0.0 reduce-scatter.2.cloned.1.call-start
  7.2 0.7 stack.12
  7.9 0.7 stack.13
  8.6 0.7 stack.14
  9.3 0.6 pad_maximum_fusion.gains
  10.0 161.2 %shard_map.245 = (bf16[4,256,1536]{2,1,0:T(8,128)(2,1)}, bf16[256,1536]{1,0:T(8,128)(2,1)}, bf16[256,1536]{1,0:T(8,128)(2,1)}, bf16[1536,1152]{1,0:T(8,128)(2,1)...) custom-call(bf16[256,1536]{1,0:T(8,128)(2,1)} %latents.3, ...), custom_call_target="tpu_custom_call" | custom-call | flops 137438953472 | bytes 67108864 | tf_op jit(solution)/shard_map/pallas_call | solution.py:906
  171.2 180.2 %shard_map.246 = (f32[256,1536]{1,0:T(8,128)}, f32[256,1536]{1,0:T(8,128)}, bf16[4,256,1536]{2,1,0:T(8,128)(2,1)}, bf16[4,4,2,192,768]{4,3,2,1,0:T(8,128)(2,1)},...) custom-call(bf16[256,1536]{1,0:T(8,128)(2,1)} %cotangent.1, ...), custom_call_target="tpu_custom_call" | custom-call | flops 68719476736 | bytes 67108864 | tf_op jit(solution)/shard_map/pallas_call | solution.py:1650
  351.4 0.0 reduce-scatter.2.cloned.1.call-update
  351.5 127.1 %shard_map.247 = (f32[256,1536]{1,0:T(8,128)}, f32[1,130,768]{2,1,0:T(8,128)}, f32[8,1536]{1,0:T(8,128)}, f32[192,1152]{1,0:T(8,128)}, f32[192,384]{1,0:T(8,128)...) custom-call(bf16[256,1536]{1,0:T(8,128)(2,1)} %latents.3, f32[3,1536]{1,0:T(4,128)} %pad_maximum_fusion.gains, ...), custom_call_target="tpu_custom_call" | custom-call | flops 137438953472 | bytes 67108864 | tf_op jit(solution)/shard_map/pallas_call | solution.py:1289
  478.6 2.2 copy.28
  480.8 1.6 slice_reduce_fusion
  482.3 0.0 reduce-scatter.2.cloned.1.call-done.in_up
  482.3 8.7 %shard_map.248 = (f32[256,1536]{1,0:T(8,128)}, f32[256,1536]{1,0:T(8,128)}, f32[192,1152]{1,0:T(8,128)}, f32[192,384]{1,0:T(8,128)}, f32[192,384]{1,0:T(8,128)},...) custom-call(f32[256,1536]{1,0:T(8,128)} %get-tuple-element.73.in_out, ...), custom_call_target="tpu_custom_call" | custom-call | flops 4194304 | bytes 16777216 | tf_op jit(solution)/shard_map/pallas_call | solution.py:1698
Async XLA Ops:
  7.2 475.2 %reduce-scatter.2.cloned.1.call-start = ((), (), s32[]{:S(2)}) async-start(), calls=%async_computation.1 | async-start | bytes 5308416 | tf_op jit(solution)/shard_map/reduce_scatter | solution.py:305
Sparse Core Ops, SparseCore 0:
  351.6 66.3 reduce-scatter.1

commit v7 on v6

--- a/solution.py
+++ b/solution.py
@@ -1722,7 +1722,7 @@
     cotangent,
 ):
     low = jnp.bfloat16
-    gains = jnp.stack([gain_attn, gain_cross, gain_mlp])
+    gains = jnp.concatenate([gain_attn, gain_cross, gain_mlp]).reshape(3, -1)
     (
         rows_one, normed_two, rows_three, qkv_all, attn_out_t, cross_all, cross_kv, mlp_all, own_down,
         rotated, attended, logs, cross_query, keyval, crossed, cross_logs, resid_one, resid_two, tables,

time: 507 us -> 506 us (level)
  no operation moved by 1% of the time
where the time goes in v7:
time: 506 us; the launch traced here: 497 us
  Pallas kernels  477 us (94%)
  between operations  14.5 us (3%)
    pallas_call x1, Pallas kernels, middle_part(): pl.pallas_call(middle_kernel, out_shape=[jax.ShapeDtypeStruct(*out) for o...  180 us
    pallas_call x1, Pallas kernels, forward_part(): pl.pallas_call(forward_kernel, out_shape=[jax.ShapeDtypeStruct(*out) for...  161 us
    pallas_call x1, Pallas kernels, backward_part(): pl.pallas_call(backward_kernel, out_shape=[jax.ShapeDtypeStruct(*out) for...  127 us
  transfers between devices with their start and end apart: 1, of which 0 were waited for; matrix products, arithmetic and copies ran while one was open for 1% of the time, Pallas kernels for 26%

profile of v7, /device:TPU:0, one launch (start us, length us, event | category | flops | bytes accessed | tf_op | source)
XLA Modules:
  0.0 496.9 jit_solution(3129988009154084755)
XLA Ops:
  7.2 0.0 reduce-scatter.2.cloned.1.call-start
  7.2 0.7 pad_maximum_fusion
  8.0 0.6 reshape.34.gains
  8.6 161.2 %shard_map.245 = (bf16[4,256,1536]{2,1,0:T(8,128)(2,1)}, bf16[256,1536]{1,0:T(8,128)(2,1)}, bf16[256,1536]{1,0:T(8,128)(2,1)}, bf16[1536,1152]{1,0:T(8,128)(2,1)...) custom-call(bf16[256,1536]{1,0:T(8,128)(2,1)} %latents.3, ...), custom_call_target="tpu_custom_call" | custom-call | flops 137438953472 | bytes 67108864 | tf_op jit(solution)/shard_map/pallas_call | solution.py:906
  169.8 180.2 %shard_map.246 = (f32[256,1536]{1,0:T(8,128)}, f32[256,1536]{1,0:T(8,128)}, bf16[4,256,1536]{2,1,0:T(8,128)(2,1)}, bf16[4,4,2,192,768]{4,3,2,1,0:T(8,128)(2,1)},...) custom-call(bf16[256,1536]{1,0:T(8,128)(2,1)} %cotangent.1, ...), custom_call_target="tpu_custom_call" | custom-call | flops 68719476736 | bytes 67108864 | tf_op jit(solution)/shard_map/pallas_call | solution.py:1650
  350.1 0.0 reduce-scatter.2.cloned.1.call-update
  350.1 127.1 %shard_map.247 = (f32[256,1536]{1,0:T(8,128)}, f32[1,130,768]{2,1,0:T(8,128)}, f32[8,1536]{1,0:T(8,128)}, f32[192,1152]{1,0:T(8,128)}, f32[192,384]{1,0:T(8,128)...) custom-call(bf16[256,1536]{1,0:T(8,128)(2,1)} %latents.3, f32[3,1536]{1,0:T(4,128)} %reshape.34.gains, ...), custom_call_target="tpu_custom_call" | custom-call | flops 137438953472 | bytes 67108864 | tf_op jit(solution)/shard_map/pallas_call | solution.py:1289
  477.2 2.2 copy.28
  479.3 1.6 slice_reduce_fusion
  480.9 0.0 reduce-scatter.2.cloned.1.call-done.in_up
  480.9 8.7 %shard_map.248 = (f32[256,1536]{1,0:T(8,128)}, f32[256,1536]{1,0:T(8,128)}, f32[192,1152]{1,0:T(8,128)}, f32[192,384]{1,0:T(8,128)}, f32[192,384]{1,0:T(8,128)},...) custom-call(f32[256,1536]{1,0:T(8,128)} %get-tuple-element.73.in_out, ...), custom_call_target="tpu_custom_call" | custom-call | flops 4194304 | bytes 16777216 | tf_op jit(solution)/shard_map/pallas_call | solution.py:1698
Async XLA Ops:
  7.2 473.7 %reduce-scatter.2.cloned.1.call-start = ((), (), s32[]{:S(2)}) async-start(), calls=%async_computation.1 | async-start | bytes 5308416 | tf_op jit(solution)/shard_map/reduce_scatter | solution.py:305
Sparse Core Ops, SparseCore 0:
  350.2 66.3 reduce-scatter.1
